TPU v7x, 128 devices: a whole 4x4x4 slice. The times are simulated.
128 devices in a mesh: dp: 8 (over z, x_lo), section: 4 (over y), mp: 4 (over x_hi, core).
Axes of the slice: x: 4 (x_hi: 2, x_lo: 2; x = x_hi * 2 + x_lo), y: 4, z: 4, core: 2. Of those that a mesh axis runs over, the one named last changes fastest.
Arguments:
- block_input: bfloat16 [32, 256, 1280], P(('dp', 'section')), may hold values from -6 to 6
- windows: int32 [32, 64], P(('dp', 'section')), may hold values from 0 to 3, never falling along the last dimension, each value on 1 to 32 neighbouring positions
- cell_rows: int32 [4, 2048], P('section', 'dp'), may hold values from -1 to 511, as said below
- text_vectors: bfloat16 [4, 2048, 8192], P('section', 'dp', 'mp'), may hold values from -6 to 6
- sequence_cotangent: bfloat16 [4, 2048, 8192], P('section', 'dp', 'mp'), may hold values from -2.5 to 2.5
- norm_gains: float32 [2, 1280], replicated, may hold values from 0.1 to 1.9
- merge_gain: float32 [1280], replicated, may hold values from 0.1 to 1.9
- triple_weight: bfloat16 [1280, 3, 1280], P('section', None, 'mp'), may hold values from -0.15625 to 0.15625
- output_weight: bfloat16 [1280, 1280], P('section', 'mp'), may hold values from -0.15625 to 0.15625
- gate_up_weight: bfloat16 [1280, 2, 3420], P('section', None, 'mp'), may hold values from -0.15625 to 0.15625
- down_weight: bfloat16 [1280, 3420], P('section', 'mp'), may hold values from -0.109375 to 0.109375
- merge_up: bfloat16 [5120, 5120], P(None, ('section', 'mp')), may hold values from -0.078125 to 0.078125
- merge_down: bfloat16 [5120, 8192], P(('section', 'mp')), may hold values from -0.078125 to 0.078125
Outputs:
- sequence: bfloat16 [4, 2048, 8192], P('section', 'dp', 'mp')
- input_gradient: float32 [32, 256, 1280], P(('dp', 'section'))
- triple_gradient: float32 [1280, 3, 1280], P('section', None, 'mp')
- output_gradient: float32 [1280, 1280], P('section', 'mp')
- gate_up_gradient: float32 [1280, 2, 3420], P('section', None, 'mp')
- down_gradient: float32 [1280, 3420], P('section', 'mp')
- gain_gradient: float32 [2, 1280], replicated
Inputs may be any that keep to these rules, and one draw needn't show every extreme that they name: `cell_rows`: in sequence s the rows that are not -1 hold each index d * 64 + c (cell c of pack d * 4 + s) exactly once, rising along the rows; the rows d * 256 to (d + 1) * 256 - 1 hold only indices from d * 64 to (d + 2) * 64 - 1.
All inputs are finite; a program needn't handle non-finite values.
Results may differ from a plain program's by a relative error of at most 0.034.
Values may be sent and summed in bfloat16 or wider, within the bound.
A program may use at most 128 MiB of HBM per device.

v0:
```python
import math

import jax
import jax.numpy as jnp
from jax import lax
from jax.sharding import PartitionSpec as P

HEAD_DIM = 80


epsilon = 1e-06
root_half = 0.7071067811865476
density_scale = 0.3989422804014327


def passed_along(value, axis, steps):
    count = lax.axis_size(axis)
    initial, last = (max(0, -steps), min(count, count - steps))
    return lax.ppermute(value, axis, [(source, source + steps) for source in range(initial, last)])


def root_scale(values):
    return lax.rsqrt(jnp.mean(values * values, axis=-1, keepdims=True) + epsilon)


def norm_backward(cotangent, values, scale, gain):
    weighted = cotangent * gain
    return scale * weighted - values * scale**3 * jnp.mean(
        weighted * values, axis=-1, keepdims=True
    )


def gelu_value(values):
    return 0.5 * values * (1.0 + jax.scipy.special.erf(values * root_half))


def gelu_slope(values):
    return (
        0.5 * (1.0 + jax.scipy.special.erf(values * root_half))
        + values * jnp.exp(-0.5 * values * values) * density_scale
    )


def product(left, right):
    return jnp.dot(left, right, preferred_element_type=jnp.float32)


def contract_last(left, right):
    return lax.dot_general(
        left, right, (((1,), (1,)), ((), ())), preferred_element_type=jnp.float32
    )


def contract_first(left, right):
    return lax.dot_general(
        left, right, (((0,), (0,)), ((), ())), preferred_element_type=jnp.float32
    )


def local_attention(queries, keys, values, allowed):
    scale = 1.0 / math.sqrt(queries.shape[-1])
    scores = jnp.einsum("qhd,khd->hqk", queries, keys, preferred_element_type=jnp.float32) * scale
    scores = jnp.where(allowed[None], scores, -1e30)
    highest = jnp.max(scores, axis=-1, keepdims=True)
    raised = jnp.exp(scores - highest)
    shares = raised / jnp.sum(raised, axis=-1, keepdims=True)
    shares_low = shares.astype(jnp.bfloat16)
    mixed = jnp.einsum(
        "hqk,khd->qhd", shares_low, values, preferred_element_type=jnp.float32
    ).astype(jnp.bfloat16)
    return (shares, shares_low, mixed)


def local_attention_backward(mixed_back, queries, keys, values, shares, shares_low):
    scale = 1.0 / math.sqrt(queries.shape[-1])
    share_back = jnp.einsum("qhd,khd->hqk", mixed_back, values, preferred_element_type=jnp.float32)
    value_back = jnp.einsum(
        "hqk,qhd->khd", shares_low, mixed_back, preferred_element_type=jnp.float32
    )
    centre = jnp.sum(shares * share_back, axis=-1, keepdims=True)
    score_back = (shares * (share_back - centre) * scale).astype(jnp.bfloat16)
    query_back = jnp.einsum("hqk,khd->qhd", score_back, keys, preferred_element_type=jnp.float32)
    key_back = jnp.einsum("hqk,qhd->khd", score_back, queries, preferred_element_type=jnp.float32)
    return jnp.stack([query_back, key_back, value_back], axis=1).astype(jnp.bfloat16)


def pack_terms(
    attend_rows, middle_rows, feed_rows, out_rows, triple_back, heads_out, gate_up_back, activated
):
    width = attend_rows.shape[1]
    return (
        contract_first(attend_rows, triple_back).reshape(width, 3, -1).astype(jnp.bfloat16),
        contract_first(middle_rows, heads_out).astype(jnp.bfloat16),
        contract_first(feed_rows, gate_up_back).reshape(width, 2, -1).astype(jnp.bfloat16),
        contract_first(out_rows, activated).astype(jnp.bfloat16),
    )


def local(
    block_input,
    windows,
    cell_rows,
    text_vectors,
    sequence_cotangent,
    norm_gains,
    merge_gain,
    triple_weight,
    output_weight,
    gate_up_weight,
    down_weight,
    merge_up,
    merge_down,
):
    sections = lax.axis_size("section")
    columns = lax.axis_size("mp")
    whole_triple, whole_output, whole_gate_up, whole_down = (
        lax.all_gather(triple_weight, "section", axis=0, tiled=True),
        lax.all_gather(output_weight, "section", axis=0, tiled=True),
        lax.all_gather(gate_up_weight, "section", axis=0, tiled=True),
        lax.all_gather(down_weight, "section", axis=0, tiled=True),
    )
    patches = block_input[0]
    rows, width = patches.shape
    cells = rows // 4
    start = patches.astype(jnp.float32)
    scale_one = root_scale(start)
    attend_input = (start * scale_one * norm_gains[0]).astype(jnp.bfloat16)
    projected = (
        product(attend_input, whole_triple.reshape(width, -1))
        .astype(jnp.bfloat16)
        .reshape(rows, 3, -1, HEAD_DIM)
    )
    patch_windows = jnp.repeat(windows[0], 4)
    allowed = patch_windows[:, None] == patch_windows[None, :]
    shares, shares_low, mixed = local_attention(
        projected[:, 0], projected[:, 1], projected[:, 2], allowed
    )
    heads_out = mixed.reshape(rows, -1)
    middle = start + lax.psum(
        contract_last(heads_out, whole_output).astype(jnp.bfloat16), "mp"
    ).astype(jnp.float32)
    scale_two = root_scale(middle)
    feed_input = (middle * scale_two * norm_gains[1]).astype(jnp.bfloat16)
    gate_up = product(feed_input, whole_gate_up.reshape(width, -1)).reshape(rows, 2, -1)
    activated = (jax.nn.silu(gate_up[:, 0]) * gate_up[:, 1]).astype(jnp.bfloat16)
    block_out = middle + lax.psum(
        contract_last(activated, whole_down).astype(jnp.bfloat16), "mp"
    ).astype(jnp.float32)
    scale_three = root_scale(block_out)
    merged = (block_out * scale_three * merge_gain).astype(jnp.bfloat16).reshape(cells, 4 * width)
    pre = product(lax.all_gather(merged, "section", axis=0, tiled=True), merge_up)
    hidden_cells = gelu_value(pre).astype(jnp.bfloat16)
    local_units = merge_up.shape[1]
    llm_width = merge_down.shape[1]
    terms = jnp.einsum(
        "sck,kme->smce",
        hidden_cells.reshape(sections, cells, local_units),
        merge_down.reshape(local_units, columns, llm_width // columns),
        preferred_element_type=jnp.float32,
    )
    visual = (
        lax.psum_scatter(
            terms.reshape(sections * columns, cells, -1).astype(jnp.bfloat16),
            ("section", "mp"),
            scatter_dimension=0,
            tiled=True,
        )
        .astype(jnp.float32)[0]
        .astype(jnp.bfloat16)
    )
    following = passed_along(visual, "dp", -1)
    candidates = jnp.concatenate([visual, following], axis=0)
    offset = lax.axis_index("dp") * cells
    row_cells = cell_rows[0]
    is_visual = row_cells >= 0
    local_cells = jnp.where(is_visual, row_cells - offset, 0)
    picked = jnp.take(candidates, local_cells, axis=0)
    sequence = jnp.where(is_visual[:, None], picked, text_vectors[0])[None]
    slots = jnp.where(is_visual, row_cells - offset, 2 * cells)
    arrived = (
        jnp.zeros((2 * cells + 1, visual.shape[1]), jnp.bfloat16)
        .at[slots]
        .set(sequence_cotangent[0])
    )
    returned = passed_along(arrived[cells : 2 * cells], "dp", 1)
    visual_back = arrived[:cells] + returned
    gathered_back = lax.all_gather(visual_back[None], ("section", "mp"), axis=0, tiled=True)
    hidden_back = jnp.einsum(
        "smce,kme->sck",
        gathered_back.reshape(sections, columns, cells, -1),
        merge_down.reshape(local_units, columns, -1),
        preferred_element_type=jnp.float32,
    )
    pre_back = (hidden_back.reshape(sections * cells, local_units) * gelu_slope(pre)).astype(
        jnp.bfloat16
    )
    pieces = contract_last(pre_back, merge_up).reshape(sections, cells, -1)
    owned = lax.psum_scatter(
        pieces.astype(jnp.bfloat16), "section", scatter_dimension=0, tiled=True
    )
    cells_back = lax.psum(owned, "mp").astype(jnp.float32)[0]
    cells_back = cells_back.reshape(rows, width)
    out_back = norm_backward(cells_back, block_out, scale_three, merge_gain)
    out_low = out_back.astype(jnp.bfloat16)
    activated_back = product(out_low, whole_down)
    gate = gate_up[:, 0]
    upper = gate_up[:, 1]
    sigmoid_gate = jax.nn.sigmoid(gate)
    gate_part = activated_back * upper * sigmoid_gate * (1.0 + gate * (1.0 - sigmoid_gate))
    up_part = activated_back * gate * sigmoid_gate
    gate_up_back = jnp.stack([gate_part, up_part], axis=1).astype(jnp.bfloat16).reshape(rows, -1)
    feed_back = lax.psum(
        contract_last(gate_up_back, whole_gate_up.reshape(width, -1)).astype(jnp.bfloat16), "mp"
    ).astype(jnp.float32)
    middle_back = out_back + norm_backward(feed_back, middle, scale_two, norm_gains[1])
    middle_low = middle_back.astype(jnp.bfloat16)
    heads_back = product(middle_low, whole_output).astype(jnp.bfloat16).reshape(rows, -1, HEAD_DIM)
    triple_back = local_attention_backward(
        heads_back, projected[:, 0], projected[:, 1], projected[:, 2], shares, shares_low
    ).reshape(rows, -1)
    attend_back = lax.psum(
        contract_last(triple_back, whole_triple.reshape(width, -1)).astype(jnp.bfloat16), "mp"
    ).astype(jnp.float32)
    input_gradient = (middle_back + norm_backward(attend_back, start, scale_one, norm_gains[0]))[
        None
    ]
    gain_terms = jnp.stack(
        [
            jnp.sum(attend_back * start * scale_one, axis=0),
            jnp.sum(feed_back * middle * scale_two, axis=0),
        ]
    )
    gain_gradient = lax.psum(gain_terms, ("dp", "section"))
    local_terms = pack_terms(
        attend_input,
        middle_low,
        feed_input,
        out_low,
        triple_back,
        heads_out,
        gate_up_back,
        activated,
    )
    owned_terms = (
        lax.psum_scatter(local_terms[0], "section", scatter_dimension=0, tiled=True).astype(
            jnp.float32
        ),
        lax.psum_scatter(local_terms[1], "section", scatter_dimension=0, tiled=True).astype(
            jnp.float32
        ),
        lax.psum_scatter(local_terms[2], "section", scatter_dimension=0, tiled=True).astype(
            jnp.float32
        ),
        lax.psum_scatter(local_terms[3], "section", scatter_dimension=0, tiled=True).astype(
            jnp.float32
        ),
    )
    gradients = (
        lax.psum(owned_terms[0].astype(jnp.bfloat16), "dp").astype(jnp.float32),
        lax.psum(owned_terms[1].astype(jnp.bfloat16), "dp").astype(jnp.float32),
        lax.psum(owned_terms[2].astype(jnp.bfloat16), "dp").astype(jnp.float32),
        lax.psum(owned_terms[3].astype(jnp.bfloat16), "dp").astype(jnp.float32),
    )
    return (
        sequence,
        input_gradient,
        gradients[0],
        gradients[1],
        gradients[2],
        gradients[3],
        gain_gradient,
    )


def solution(mesh):
    placed = (
        P(("dp", "section"), None, None),
        P(("dp", "section"), None),
        P("section", "dp"),
        P("section", "dp", "mp"),
        P("section", "dp", "mp"),
        P(),
        P(),
        P("section", None, "mp"),
        P("section", "mp"),
        P("section", None, "mp"),
        P("section", "mp"),
        P(None, ("section", "mp")),
        P(("section", "mp"), None),
    )
    return jax.shard_map(
        local,
        mesh=mesh,
        in_specs=placed,
        out_specs=(
            P("section", "dp", "mp"),
            P(("dp", "section"), None, None),
            P("section", None, "mp"),
            P("section", "mp"),
            P("section", None, "mp"),
            P("section", "mp"),
            P(),
        ),
        check_vma=False,
    )
```

profile of v0, /device:TPU:0, one launch (start us, length us, event | category | flops | bytes accessed | tf_op | source)
XLA Modules:
  0.0 919.6 jit_solution(9612748075527445025)
XLA Ops:
  16.6 19.7 %all_gather.19 = bf16[1280,320]{1,0:T(8,128)(2,1)} all-gather(bf16[320,320]{1,0:T(8,128)(2,1)S(1)} %copy-done.15), channel_id=1, replica_groups=mesh['dp'=8,'section'=4,'mp'=4] {'section'}, dimensions={0}, use_global_device_ids=true | all-gather | bytes 1024000 | tf_op jit(solution)/shard_map/all_gather | solution.py:118
  36.3 27.1 %all-gather.7.cloned.1.call-done = bf16[1280,3,320]{2,1,0:T(4,128)(2,1)} async-done(((bf16[320,3,320]{2,1,0:T(4,128)(2,1)}), bf16[1280,3,320]{2,1,0:T(4,128)(2,1)}) %all-gather.7.cloned.1.call-update) | async-done | bytes 2457616 | tf_op jit(solution)/shard_map/all_gather | solution.py:117
  63.4 7.5 copy.57
  70.9 3.6 convolution_convert_fusion.8
  89.7 4.1 collective-permute-start.1
  93.9 32.7 %all-reduce.8.cloned.1.call-done = bf16[256,1280]{1,0:T(8,128)(2,1)} async-done(((bf16[256,1280]{1,0:T(8,128)(2,1)}), bf16[256,1280]{1,0:T(8,128)(2,1)}) %all-reduce.8.cloned.1.call-update) | async-done | bytes 655376 | tf_op jit(solution)/shard_map/psum | solution.py:139
  128.7 51.1 %all-gather.9.cloned.1.call-done = bf16[1280,2,855]{2,0,1:T(8,128)(2,1)} async-done(((bf16[320,2,855]{2,0,1:T(8,128)(2,1)}), bf16[1280,2,855]{2,0,1:T(8,128)(2,1)}) %all-gather.9.cloned.1.call-update) | async-done | bytes 4377616 | tf_op jit(solution)/shard_map/all_gather | solution.py:119
  179.9 7.2 copy.60
  187.1 5.2 reshape.295
  192.3 5.3 dot_general.87
  197.6 4.2 fusion.95
  204.0 10.3 %all-gather.11.cloned.1.call-done = bf16[1280,855]{1,0:T(8,128)(2,1)} async-done(((bf16[320,855]{1,0:T(8,128)(2,1)}), bf16[1280,855]{1,0:T(8,128)(2,1)}) %all-gather.11.cloned.1.call-update) | async-done | bytes 2188816 | tf_op jit(solution)/shard_map/all_gather | solution.py:120
  220.2 52.1 %all-reduce.10.cloned.1.call-done = bf16[256,1280]{1,0:T(8,128)(2,1)} async-done(((bf16[256,1280]{1,0:T(8,128)(2,1)}), bf16[256,1280]{1,0:T(8,128)(2,1)}) %all-reduce.10.cloned.1.call-update) | async-done | bytes 655376 | tf_op jit(solution)/shard_map/psum | solution.py:146
  277.9 4.8 copy.63
  282.7 31.3 %all-gather.13.cloned.1.call-done = bf16[256,5120]{1,0:T(8,128)(2,1)} async-done(((bf16[64,5120]{1,0:T(8,128)(2,1)}), bf16[256,5120]{1,0:T(8,128)(2,1)}) %all-gather.13.cloned.1.call-update) | async-done | bytes 2621456 | tf_op jit(solution)/shard_map/all_gather | solution.py:151
  314.0 3.6 multiply_convert_fusion.3
  317.6 11.0 %convolution_convert_fusion = bf16[256,5120]{1,0:T(8,128)(2,1)} fusion(bf16[5120,320]{0,1:T(8,128)(2,1)S(1)} %copy-done, bf16[256,2048,4]{1,0,2:T(8,128)(2,1)} %bitcast.246, bf16[40,4,8,2048]{3,2,1,0:T(8,128)(2,1)} %bitcast.243, f32[256,320]{0,1:T(8,128)} %get-tuple-element.58), kind=kOutput, calls=%fused_computation.4 | convolution fusion | flops 2183168000 | bytes 15663104 | tf_op jit(solution)/shard_map/dot_general | solution.py:49
  328.7 34.0 %reduce-scatter.9.cloned.1.call-done = bf16[1,64,5120]{2,1,0:T(8,128)(2,1)} async-done(((bf16[4,64,5120]{2,1,0:T(8,128)(2,1)}), bf16[1,64,5120]{2,1,0:T(8,128)(2,1)}) %reduce-scatter.9.cloned.1.call-update) | async-done | bytes 655376 | tf_op jit(solution)/shard_map/reduce_scatter | solution.py:198
  365.1 42.6 %all-reduce.12.cloned.1.call-done = bf16[256,1280]{1,0:T(8,128)(2,1)} async-done(((bf16[256,1280]{1,0:T(8,128)(2,1)}), bf16[256,1280]{1,0:T(8,128)(2,1)}) %all-reduce.12.cloned.1.call-update) | async-done | bytes 655376 | tf_op jit(solution)/shard_map/psum | solution.py:201
  409.4 3.8 multiply_bitcast_fusion.1
  415.9 42.2 %all-reduce.14.cloned.1.call-done = bf16[256,1280]{1,0:T(8,128)(2,1)} async-done(((bf16[256,1280]{1,0:T(8,128)(2,1)}), bf16[256,1280]{1,0:T(8,128)(2,1)}) %all-reduce.14.cloned.1.call-update) | async-done | bytes 655376 | tf_op jit(solution)/shard_map/psum | solution.py:212
  463.2 3.7 convolution_convert_fusion.3
  489.5 4.7 convolution_convert_fusion.1
  495.3 6.9 fusion.7
  505.9 14.4 %reduce-scatter.17.cloned.1.call-done = bf16[320,855]{1,0:T(8,128)(2,1)} async-done(((bf16[1280,855]{1,0:T(8,128)(2,1)}), bf16[320,855]{1,0:T(8,128)(2,1)}) %reduce-scatter.17.cloned.1.call-update) | async-done | bytes 547216 | tf_op jit(solution)/shard_map/reduce_scatter | solution.py:254
  520.3 38.7 %reduce-scatter.11.cloned.1.call-done = bf16[320,3,320]{2,0,1:T(8,128)(2,1)} async-done(((bf16[1280,3,320]{2,0,1:T(8,128)(2,1)}), bf16[320,3,320]{2,0,1:T(8,128)(2,1)}) %reduce-scatter.11.cloned.1.call-update) | async-done | bytes 614416 | tf_op jit(solution)/shard_map/reduce_scatter | solution.py:245
  558.9 52.4 %reduce-scatter.15.cloned.1.call-done = bf16[320,2,855]{2,0,1:T(8,128)(2,1)} async-done(((bf16[1280,2,855]{2,0,1:T(8,128)(2,1)}), bf16[320,2,855]{2,0,1:T(8,128)(2,1)}) %reduce-scatter.15.cloned.1.call-update) | async-done | bytes 1094416 | tf_op jit(solution)/shard_map/reduce_scatter | solution.py:251
  611.3 84.6 %reduce-scatter.7.cloned.1.call-done = bf16[1,64,2048]{2,1,0:T(8,128)(2,1)} async-done(((bf16[16,64,2048]{2,1,0:T(8,128)(2,1)}), bf16[1,64,2048]{2,1,0:T(8,128)(2,1)}) %reduce-scatter.7.cloned.1.call-update) | async-done | bytes 262160 | tf_op jit(solution)/shard_map/reduce_scatter | solution.py:162
  697.4 7.2 collective-permute-done
  710.7 30.0 %all-reduce.16.cloned.1.call-done = bf16[256,1280]{1,0:T(8,128)(2,1)} async-done(((bf16[256,1280]{1,0:T(8,128)(2,1)}), bf16[256,1280]{1,0:T(8,128)(2,1)}) %all-reduce.16.cloned.1.call-update) | async-done | bytes 655376 | tf_op jit(solution)/shard_map/psum | solution.py:221
  742.3 160.5 %psum.79 = f32[2,1280]{1,0:T(2,128)} all-reduce(f32[2,1280]{1,0:T(2,128)S(1)} %pad_maximum_fusion.1), channel_id=1, replica_groups=mesh['dp'=8,'section'=4,'mp'=4] {'dp','section'}, use_global_device_ids=true, to_apply=%region_27.28 | all-reduce | flops 2560 | bytes 20480 | tf_op jit(solution)/shard_map/psum | solution.py:233
  904.2 3.9 copy.70
  (157 shorter events, 93.0 us)
Async XLA Ops:
  8.0 306.0 %copy-start = (bf16[5120,320]{0,1:T(8,128)(2,1)S(1)}, bf16[5120,320]{0,1:T(8,128)(2,1)}, u32[]{:S(2)}) copy-start(bf16[5120,320]{0,1:T(8,128)(2,1)} %param.24) | copy-start | bytes 9830404
  8.0 55.4 %all-gather.7.cloned.1.call-start = ((), (), s32[]{:S(2)}) async-start(), calls=%async_computation.6 | async-start | bytes 4915200 | tf_op jit(solution)/shard_map/all_gather | solution.py:117
  10.9 5.7 copy-start.15
  10.9 115.6 %all-reduce.8.cloned.1.call-start = ((), (), s32[]{:S(2)}) async-start(), calls=%async_computation.7 | async-start | bytes 1310720 | tf_op jit(solution)/shard_map/psum | solution.py:139
  81.4 98.4 %all-gather.9.cloned.1.call-start = ((), (), s32[]{:S(2)}) async-start(), calls=%async_computation.8 | async-start | bytes 5734400 | tf_op jit(solution)/shard_map/all_gather | solution.py:119
  83.9 130.4 %all-gather.11.cloned.1.call-start = ((), (), s32[]{:S(2)}) async-start(), calls=%async_computation.9 | async-start | bytes 2867200 | tf_op jit(solution)/shard_map/all_gather | solution.py:120
  84.5 187.8 %all-reduce.10.cloned.1.call-start = ((), (), s32[]{:S(2)}) async-start(), calls=%async_computation.10 | async-start | bytes 1310720 | tf_op jit(solution)/shard_map/psum | solution.py:146
  89.7 128.1 %collective-permute-start.1 = (bf16[64,2048]{1,0:T(8,128)(2,1)}, bf16[64,2048]{1,0:T(8,128)(2,1)}, u32[]{:S(2)}, u32[]{:S(2)}) collective-permute-start(bf16[64,2048]{1,0:T(8,128)(2,1)} %slice.51), channel_id=1, source_target_pairs={{0,16},{16,32},{32,48},{48,64},{64,80},{80,96},{96,112},{1,17},{17... | collective-permute-start | bytes 786440 | tf_op jit(solution)/shard_map/ppermute | solution.py:19
  217.8 60.1 %all-gather.15.cloned.1.call-start = ((), (), s32[]{:S(2)}) async-start(), calls=%async_computation.21 | async-start | bytes 4456448 | tf_op jit(solution)/shard_map/all_gather | solution.py:187
  219.7 54.6 %copy-start.18 = (f32[1280]{0:T(1024)S(1)}, f32[1280]{0:T(1024)}, u32[]{:S(2)}) copy-start(f32[1280]{0:T(1024)} %param.19) | copy-start | bytes 15364
  219.7 94.3 %all-gather.13.cloned.1.call-start = ((), (), s32[]{:S(2)}) async-start(), calls=%async_computation.11 | async-start | bytes 3276800 | tf_op jit(solution)/shard_map/all_gather | solution.py:151
  274.3 135.1 %copy-start.20 = (f32[256]{0:T(256)}, f32[256]{0:T(256)S(1)}, u32[]{:S(2)}) copy-start(f32[256]{0:T(256)S(1)} %get-tuple-element.53) | copy-start | bytes 3076
  277.9 84.9 %reduce-scatter.9.cloned.1.call-start = ((), (), s32[]{:S(2)}) async-start(), calls=%async_computation.13 | async-start | bytes 3276800 | tf_op jit(solution)/shard_map/reduce_scatter | solution.py:198
  328.7 79.0 %copy-start.3 = (bf16[1,256,1280]{2,1,0:T(8,128)(2,1)S(1)}, bf16[1,256,1280]{2,1,0:T(8,128)(2,1)}, u32[]{:S(2)}) copy-start(bf16[1,256,1280]{2,1,0:T(8,128)(2,1)} %param.13) | copy-start | bytes 1966084
  328.7 79.0 %copy-start.5 = (bf16[256,1280]{1,0:T(8,128)(2,1)S(1)}, bf16[256,1280]{1,0:T(8,128)(2,1)}, u32[]{:S(2)}) copy-start(bf16[256,1280]{1,0:T(8,128)(2,1)} %all-reduce.8.cloned.1.call-done) | copy-start | bytes 1966084
  328.7 79.0 %copy-start.7 = (bf16[256,1280]{1,0:T(8,128)(2,1)S(1)}, bf16[256,1280]{1,0:T(8,128)(2,1)}, u32[]{:S(2)}) copy-start(bf16[256,1280]{1,0:T(8,128)(2,1)} %all-reduce.10.cloned.1.call-done) | copy-start | bytes 1966084
  328.7 79.0 %all-reduce.12.cloned.1.call-start = ((), (), s32[]{:S(2)}) async-start(), calls=%async_computation.14 | async-start | bytes 1310720 | tf_op jit(solution)/shard_map/psum | solution.py:201
  365.0 93.1 %all-reduce.14.cloned.1.call-start = ((), (), s32[]{:S(2)}) async-start(), calls=%async_computation.15 | async-start | bytes 1310720 | tf_op jit(solution)/shard_map/psum | solution.py:212
  407.7 5.6 slice-start
  409.4 3.9 slice-start.1
  415.7 90.2 %reduce-scatter.13.cloned.1.call-start = ((), (), s32[]{:S(2)}) async-start(), calls=%async_computation.18 | async-start | bytes 1228800 | tf_op jit(solution)/shard_map/reduce_scatter | solution.py:248
  463.2 57.1 %reduce-scatter.17.cloned.1.call-start = ((), (), s32[]{:S(2)}) async-start(), calls=%async_computation.20 | async-start | bytes 2867200 | tf_op jit(solution)/shard_map/reduce_scatter | solution.py:254
  467.0 92.0 %reduce-scatter.11.cloned.1.call-start = ((), (), s32[]{:S(2)}) async-start(), calls=%async_computation.17 | async-start | bytes 3686400 | tf_op jit(solution)/shard_map/reduce_scatter | solution.py:245
  482.8 128.5 %reduce-scatter.15.cloned.1.call-start = ((), (), s32[]{:S(2)}) async-start(), calls=%async_computation.19 | async-start | bytes 5734400 | tf_op jit(solution)/shard_map/reduce_scatter | solution.py:251
  494.2 201.7 %reduce-scatter.7.cloned.1.call-start = ((), (), s32[]{:S(2)}) async-start(), calls=%async_computation.12 | async-start | bytes 4456448 | tf_op jit(solution)/shard_map/reduce_scatter | solution.py:162
  502.3 238.4 %all-reduce.16.cloned.1.call-start = ((), (), s32[]{:S(2)}) async-start(), calls=%async_computation.16 | async-start | bytes 1310720 | tf_op jit(solution)/shard_map/psum | solution.py:221
  505.8 398.5 %all-reduce.18.cloned.1.call-start = ((), (), s32[]{:S(2)}) async-start(), calls=%async_computation.22 | async-start | bytes 5406720 | tf_op jit(solution)/shard_map/psum | solution.py:261
  695.9 8.7 collective-permute-start
  710.7 192.1 %copy-start.24 = (f32[256]{0:T(256)S(1)}, f32[256]{0:T(256)}, u32[]{:S(2)}) copy-start(f32[256]{0:T(256)} %get-tuple-element.49) | copy-start | bytes 3076
  740.7 162.1 %copy-start.9 = (bf16[256,1280]{1,0:T(8,128)(2,1)S(1)}, bf16[256,1280]{1,0:T(8,128)(2,1)}, u32[]{:S(2)}) copy-start(bf16[256,1280]{1,0:T(8,128)(2,1)} %all-reduce.16.cloned.1.call-done) | copy-start | bytes 1966084
  904.2 3.9 copy-start.11
  908.1 3.9 copy-start.1
  (16 other events, 33.0 us)
Sparse Core Ops, SparseCore 0:
  11.1 52.2 all-gather.6
  81.5 44.9 all-reduce.7
  128.8 51.0 all-gather.8
  181.4 32.8 all-gather.10
  218.0 54.3 all-reduce.9
  365.1 42.5 all-reduce.11
  415.8 42.2 all-reduce.13
  463.3 22.7 reduce-scatter.12
  489.2 30.9 reduce-scatter.16
  522.5 36.3 reduce-scatter.10
  561.5 49.7 reduce-scatter.14
  615.7 80.1 reduce-scatter.6
  699.0 41.6 all-reduce.15
  743.3 131.4 all-reduce.17
Sparse Core Ops, SparseCore 1:
  220.8 56.7 all-gather.14
  279.7 34.3 all-gather.12
  328.7 33.9 reduce-scatter.8
where the time goes:
time: 929 us; the launch traced here: 920 us
  waiting for transfers between devices  551 us (59%)
  blocking collectives  180 us (19%)
  matrix products  74 us (8%)
  local copies, waits for them, and re-layouts  61 us (7%)
  other arithmetic  29.8 us (3%)
  between operations  16.2 us (2%)
    psum x1, blocking collectives, local(): gain_gradient = lax.psum(gain_terms, ('dp', 'section'))  160 us
    reduce_scatter x1, waiting for transfers between devices, local(): lax.psum_scatter(terms.reshape(sections * columns, cells, -1).astype(jnp....  84.6 us
    reduce_scatter x1, waiting for transfers between devices, local(): lax.psum_scatter(local_terms[2], 'section', scatter_dimension=0, tiled=True)  52.4 us
    psum x1, waiting for transfers between devices, local(): lax.psum(contract_last(activated, whole_down).astype(jnp.bfloat16), 'mp')  52.1 us
    all_gather x1, waiting for transfers between devices, local(): lax.all_gather(gate_up_weight, 'section', axis=0, tiled=True)  51.1 us
    psum x1, waiting for transfers between devices, local(): cells_back = lax.psum(owned, 'mp').astype(jnp.float32)[0]  42.6 us
    psum x1, waiting for transfers between devices, local(): lax.psum(contract_last(gate_up_back, whole_gate_up.reshape(width, -1)).as...  42.2 us
    reduce_scatter x1, waiting for transfers between devices, local(): lax.psum_scatter(local_terms[0], 'section', scatter_dimension=0, tiled=True)  38.7 us
  transfers between devices with their start and end apart: 19, of which 15 were waited for; matrix products, arithmetic and copies ran while one was open for 11% of the time, Pallas kernels for 0%

commit v1 on v0

--- a/solution.py
+++ b/solution.py
@@ -1,8 +1,11 @@
+import functools
 import math
 
 import jax
 import jax.numpy as jnp
 from jax import lax
+from jax.experimental import pallas as pl
+from jax.experimental.pallas import tpu as pltpu
 from jax.sharding import PartitionSpec as P
 
 HEAD_DIM = 80
@@ -11,6 +14,423 @@
 epsilon = 1e-06
 root_half = 0.7071067811865476
 density_scale = 0.3989422804014327
+
+MESH = pl.DeviceIdType.MESH
+VMEM_LIMIT = 60 * 1024 * 1024
+VMEM = pl.BlockSpec(memory_space=pltpu.VMEM)
+ANY = pl.BlockSpec(memory_space=pl.ANY)
+
+
+class Place:
+    def __init__(self):
+        dp, self.y, mp = lax.axis_index("dp"), lax.axis_index("section"), lax.axis_index("mp")
+        self.z, self.low = dp // 2, dp % 2
+        self.high, self.core = mp // 2, mp % 2
+
+    def at(self, z=None, low=None, y=None, high=None, core=None):
+        z = self.z if z is None else z
+        low = self.low if low is None else low
+        y = self.y if y is None else y
+        high = self.high if high is None else high
+        core = self.core if core is None else core
+        return (z * 2 + low, y, high * 2 + core)
+
+    def along_y(self, k):
+        return (self.y + k) % 4
+
+    def along_z(self, k):
+        return (self.z + k) % 4
+
+
+def greet(devices):
+    barrier = pltpu.get_barrier_semaphore()
+    for device in devices:
+        pl.semaphore_signal(barrier, inc=1, device_id=device, device_id_type=MESH)
+    pl.semaphore_wait(barrier, len(devices))
+
+
+def send(source, target, sems, index, device):
+    copy = pltpu.make_async_remote_copy(
+        src_ref=source,
+        dst_ref=target,
+        send_sem=sems[0].at[index],
+        recv_sem=sems[1].at[index],
+        device_id=device,
+        device_id_type=MESH,
+    )
+    copy.start()
+    return copy
+
+
+def sem_pair(*shape):
+    return [pltpu.SemaphoreType.DMA(shape), pltpu.SemaphoreType.DMA(shape)]
+
+
+def wide(values):
+    return values.astype(jnp.float32)
+
+
+def low(values):
+    return values.astype(jnp.bfloat16)
+
+
+def sum_kernel(chunks, part, out, got, half, other, s1, r1, s2, r2, s3, r3):
+    me = Place()
+    sibling, partner = me.at(core=1 - me.core), me.at(high=1 - me.high)
+    rows = part.shape[0] // 2
+    step = rows // chunks
+    greet((sibling, partner))
+    mine, theirs = me.core * rows, (1 - me.core) * rows
+    first = [
+        send(
+            part.at[pl.ds(pl.multiple_of(theirs + k * step, step), step)],
+            got.at[pl.ds(k * step, step)],
+            (s1, r1),
+            k,
+            sibling,
+        )
+        for k in range(chunks)
+    ]
+    second, third = [], []
+    for k in range(chunks):
+        here = pl.ds(k * step, step)
+        first[k].wait_recv()
+        half[here] = low(
+            wide(part[pl.ds(pl.multiple_of(mine + k * step, step), step)]) + wide(got[here])
+        )
+        second.append(send(half.at[here], other.at[here], (s2, r2), k, partner))
+    for k in range(chunks):
+        here = pl.ds(k * step, step)
+        there = pl.ds(pl.multiple_of(mine + k * step, step), step)
+        second[k].wait_recv()
+        out[there] = low(wide(half[here]) + wide(other[here]))
+        third.append(send(out.at[there], out.at[there], (s3, r3), k, sibling))
+    for k in range(chunks):
+        third[k].wait()
+        first[k].wait_send()
+        second[k].wait_send()
+
+
+def sum_mp(part):
+    rows, width = part.shape
+    chunks = 4
+    half = pltpu.VMEM((rows // 2, width), jnp.bfloat16)
+    return pl.pallas_call(
+        functools.partial(sum_kernel, chunks),
+        out_shape=jax.ShapeDtypeStruct((rows, width), jnp.bfloat16),
+        in_specs=[VMEM],
+        out_specs=VMEM,
+        scratch_shapes=[half, half, half]
+        + sem_pair(chunks)
+        + sem_pair(chunks)
+        + sem_pair(chunks),
+        compiler_params=pltpu.CompilerParams(
+            collective_id=1, has_side_effects=True, vmem_limit_bytes=VMEM_LIMIT
+        ),
+        name="sum_mp",
+    )(part)
+
+
+Z_ROWS = (48, 32, 32, 48)
+
+
+def gather_kernel(count, *refs):
+    shards, wholes = refs[:count], refs[count : 2 * count]
+    own, s1, r1, s2, r2, s3, r3 = refs[2 * count :]
+    me = Place()
+    others = (1, 2, 3)
+    greet(
+        [me.at(y=me.along_y(k)) for k in others]
+        + [me.at(z=me.along_z(k)) for k in others]
+        + [me.at(low=1 - me.low)]
+    )
+    locals_, first, second = [], [], []
+    spans = []
+    for t in range(count):
+        rows = shards[t].shape[1]
+        quarter = Z_ROWS[t]
+        side = (rows - 4 * quarter) // 2
+        by_z = pl.ds(pl.multiple_of(me.z * quarter, 16), quarter)
+        by_low = pl.ds(pl.multiple_of(4 * quarter + me.low * side, 16), side)
+        spans.append((by_z, by_low))
+    for t in range(count):
+        for k in (1, 3, 2):
+            for part in range(2):
+                span = spans[t][part]
+                first.append(
+                    send(
+                        shards[t].at[:, span],
+                        wholes[t].at[:, me.y, span],
+                        (s1, r1),
+                        (t * 3 + k - 1) * 2 + part,
+                        me.at(y=me.along_y(k)),
+                    )
+                )
+        copy = pltpu.make_async_copy(shards[t], wholes[t].at[:, me.y], own.at[t])
+        copy.start()
+        locals_.append(copy)
+    at = 0
+    for t in range(count):
+        for k in (1, 3, 2):
+            source = me.along_y(4 - k)
+            for part in range(2):
+                first[at].wait_recv()
+                at += 1
+                block = wholes[t].at[:, source, spans[t][part]]
+                if part == 0:
+                    for j in (1, 3, 2):
+                        second.append(
+                            send(
+                                block,
+                                block,
+                                (s2, r2),
+                                (t * 3 + k - 1) * 3 + j - 1,
+                                me.at(z=me.along_z(j)),
+                            )
+                        )
+                else:
+                    second.append(
+                        send(block, block, (s3, r3), t * 3 + k - 1, me.at(low=1 - me.low))
+                    )
+    for copy in second:
+        copy.wait_recv()
+    for copy in first + second:
+        copy.wait_send()
+    for copy in locals_:
+        copy.wait()
+
+
+def gather_weights(*shards):
+    count = len(shards)
+    return pl.pallas_call(
+        functools.partial(gather_kernel, count),
+        out_shape=[
+            jax.ShapeDtypeStruct((s.shape[0], 4) + s.shape[1:], jnp.bfloat16) for s in shards
+        ],
+        in_specs=[ANY] * count,
+        out_specs=[ANY] * count,
+        scratch_shapes=[pltpu.SemaphoreType.DMA((count,))]
+        + sem_pair(count * 6)
+        + sem_pair(count * 9)
+        + sem_pair(count * 3),
+        compiler_params=pltpu.CompilerParams(
+            collective_id=2, has_side_effects=True, vmem_limit_bytes=VMEM_LIMIT
+        ),
+        name="gather_weights",
+    )(*shards)
+
+
+A_ROWS = 192
+A_PART = A_ROWS // 4
+B_ROWS = 128
+B_PART = B_ROWS // 4
+E_ROWS = A_PART + B_PART
+TILE = 16
+
+
+def over_rows(planes, rows, body):
+    tiles = rows // TILE
+
+    @pl.loop(0, planes * tiles)
+    def _(i):
+        body(i // tiles, pl.multiple_of((i % tiles) * TILE, TILE))
+
+
+def reduce_kernel(count, *refs):
+    terms, gain = refs[:count], refs[count]
+    outs, gain_out = refs[count + 1 : 2 * count + 1], refs[2 * count + 1]
+    scratch = refs[2 * count + 2 :]
+    per = 9
+    work = [scratch[t * per : (t + 1) * per] for t in range(count)]
+    gain_got, gain_sum, *sems = scratch[count * per :]
+    ya_s, za_s, zb_s, yb_s, ex_s, fa_s, g_s = [
+        (sems[2 * i], sems[2 * i + 1]) for i in range(7)
+    ]
+    me = Place()
+    others = (1, 2, 3)
+    y_at = [None] + [me.at(y=me.along_y(k)) for k in others]
+    z_at = [None] + [me.at(z=me.along_z(k)) for k in others]
+    side = me.at(low=1 - me.low)
+    greet(y_at[1:] + z_at[1:] + [side])
+    pending = []
+
+    def go(*arguments):
+        copy = send(*arguments)
+        pending.append(copy)
+        return copy
+
+    order = (1, 3, 2)
+    first_a, first_b = [], []
+    gain_copies = [go(gain, gain_got.at[k - 1], g_s, k - 1, y_at[k]) for k in order]
+    for t in range(count):
+        ya, sa, za, zb, sb, yb, ee, ex, fa = work[t]
+        first_a.append(
+            [
+                go(terms[t].at[:, me.along_y(k), pl.ds(0, A_ROWS)], ya.at[k - 1], ya_s, t * 3 + k - 1, y_at[k])
+                for k in order
+            ]
+        )
+        first_b.append(
+            [
+                go(
+                    terms[t].at[:, :, pl.ds(pl.multiple_of(A_ROWS + me.along_z(k) * B_PART, TILE), B_PART)],
+                    zb.at[k - 1],
+                    zb_s,
+                    t * 3 + k - 1,
+                    z_at[k],
+                )
+                for k in order
+            ]
+        )
+    second_a, second_b, third, fourth = [], [], [], []
+    for copy in gain_copies:
+        copy.wait_recv()
+    gain_sum[0] = gain[...] + gain_got[0] + gain_got[1] + gain_got[2]
+    gain_copies = [go(gain_sum.at[0], gain_got.at[2 + k], g_s, 2 + k, z_at[k]) for k in order]
+    for t in range(count):
+        ya, sa, za, zb, sb, yb, ee, ex, fa = work[t]
+        planes = terms[t].shape[0]
+        for copy in first_b[t]:
+            copy.wait_recv()
+
+        def add_b(i, r):
+            p, q = i // 4, i % 4
+            here = pl.ds(r, TILE)
+            own = terms[t][p, q, pl.ds(pl.multiple_of(A_ROWS + me.z * B_PART + r, TILE), TILE)]
+            sb[p, q, here] = low(
+                wide(own) + wide(zb[0, p, q, here]) + wide(zb[1, p, q, here]) + wide(zb[2, p, q, here])
+            )
+
+        over_rows(planes * 4, B_PART, add_b)
+        second_b.append(
+            [go(sb.at[:, me.along_y(k)], yb.at[k - 1], yb_s, t * 3 + k - 1, y_at[k]) for k in order]
+        )
+        for copy in first_a[t]:
+            copy.wait_recv()
+
+        def add_a(p, r):
+            here = pl.ds(r, TILE)
+            sa[p, here] = low(
+                wide(terms[t][p, me.y, here]) + wide(ya[0, p, here]) + wide(ya[1, p, here]) + wide(ya[2, p, here])
+            )
+
+        over_rows(planes, A_ROWS, add_a)
+        second_a.append(
+            [
+                go(
+                    sa.at[:, pl.ds(pl.multiple_of(me.along_z(k) * A_PART, TILE), A_PART)],
+                    za.at[k - 1],
+                    za_s,
+                    t * 3 + k - 1,
+                    z_at[k],
+                )
+                for k in order
+            ]
+        )
+    for copy in gain_copies:
+        copy.wait_recv()
+    gain_sum[1] = gain_sum[0] + gain_got[3] + gain_got[4] + gain_got[5]
+    gain_copies = [go(gain_sum.at[1], gain_got.at[6], g_s, 6, side)]
+    for t in range(count):
+        ya, sa, za, zb, sb, yb, ee, ex, fa = work[t]
+        planes = terms[t].shape[0]
+        for copy in second_b[t] + second_a[t]:
+            copy.wait_recv()
+
+        def add_a(p, r):
+            here = pl.ds(r, TILE)
+            own = sa[p, pl.ds(pl.multiple_of(me.z * A_PART + r, TILE), TILE)]
+            ee[p, here] = low(wide(own) + wide(za[0, p, here]) + wide(za[1, p, here]) + wide(za[2, p, here]))
+
+        def add_b(p, r):
+            here = pl.ds(r, TILE)
+            ee[p, pl.ds(pl.multiple_of(A_PART + r, TILE), TILE)] = low(
+                wide(sb[p, me.y, here]) + wide(yb[0, p, here]) + wide(yb[1, p, here]) + wide(yb[2, p, here])
+            )
+
+        over_rows(planes, A_PART, add_a)
+        over_rows(planes, B_PART, add_b)
+        third.append(go(ee, ex, ex_s, t, side))
+    for copy in gain_copies:
+        copy.wait_recv()
+    gain_out[...] = gain_sum[1] + gain_got[6]
+    for t in range(count):
+        ya, sa, za, zb, sb, yb, ee, ex, fa = work[t]
+        planes = terms[t].shape[0]
+        third[t].wait_recv()
+
+        def add(p, r):
+            here = pl.ds(r, TILE)
+            fa[0, p, here] = low(wide(ee[p, here]) + wide(ex[p, here]))
+
+        over_rows(planes, E_ROWS, add)
+        fourth.append([go(fa.at[0], fa.at[k], fa_s, t * 3 + k - 1, z_at[k]) for k in order])
+    for t in range(count):
+        ya, sa, za, zb, sb, yb, ee, ex, fa = work[t]
+        planes = terms[t].shape[0]
+        for k in (0,) + order:
+            if k:
+                fourth[t][order.index(k)].wait_recv()
+            source = (me.z + 4 - k) % 4
+
+            def put_a(p, r):
+                outs[t][p, pl.ds(pl.multiple_of(source * A_PART + r, TILE), TILE)] = wide(
+                    fa[k, p, pl.ds(r, TILE)]
+                )
+
+            def put_b(p, r):
+                outs[t][p, pl.ds(pl.multiple_of(A_ROWS + source * B_PART + r, TILE), TILE)] = wide(
+                    fa[k, p, pl.ds(pl.multiple_of(A_PART + r, TILE), TILE)]
+                )
+
+            over_rows(planes, A_PART, put_a)
+            over_rows(planes, B_PART, put_b)
+    for copy in pending:
+        copy.wait_send()
+
+
+def reduce_gradients(gain_terms, *terms):
+    count = len(terms)
+    scratch = []
+    for term in terms:
+        planes, _, _, width = term.shape
+
+        def buffer(*shape):
+            return pltpu.VMEM(shape + (width,), jnp.bfloat16)
+
+        scratch += [
+            buffer(3, planes, A_ROWS),
+            buffer(planes, A_ROWS),
+            buffer(3, planes, A_PART),
+            buffer(3, planes, 4, B_PART),
+            buffer(planes, 4, B_PART),
+            buffer(3, planes, B_PART),
+            buffer(planes, E_ROWS),
+            buffer(planes, E_ROWS),
+            buffer(4, planes, E_ROWS),
+        ]
+    gain_rows = (8, gain_terms.shape[1])
+    scratch += [pltpu.VMEM((7,) + gain_rows, jnp.float32), pltpu.VMEM((2,) + gain_rows, jnp.float32)]
+    for size in (3 * count, 3 * count, 3 * count, 3 * count, count, 3 * count, 7):
+        scratch += sem_pair(size)
+    padded = jnp.concatenate(
+        [gain_terms, jnp.zeros((6, gain_terms.shape[1]), jnp.float32)], axis=0
+    )
+    results = pl.pallas_call(
+        functools.partial(reduce_kernel, count),
+        out_shape=[
+            jax.ShapeDtypeStruct((t.shape[0],) + t.shape[2:], jnp.float32) for t in terms
+        ]
+        + [jax.ShapeDtypeStruct(gain_rows, jnp.float32)],
+        in_specs=[VMEM] * (count + 1),
+        out_specs=[VMEM] * (count + 1),
+        scratch_shapes=scratch,
+        compiler_params=pltpu.CompilerParams(
+            collective_id=3, has_side_effects=True, vmem_limit_bytes=VMEM_LIMIT
+        ),
+        name="reduce_gradients",
+    )(*terms, padded)
+    return results[:count], results[count][:2]
 
 
 def passed_along(value, axis, steps):
@@ -84,16 +504,15 @@
     return jnp.stack([query_back, key_back, value_back], axis=1).astype(jnp.bfloat16)
 
 
-def pack_terms(
-    attend_rows, middle_rows, feed_rows, out_rows, triple_back, heads_out, gate_up_back, activated
-):
-    width = attend_rows.shape[1]
-    return (
-        contract_first(attend_rows, triple_back).reshape(width, 3, -1).astype(jnp.bfloat16),
-        contract_first(middle_rows, heads_out).astype(jnp.bfloat16),
-        contract_first(feed_rows, gate_up_back).reshape(width, 2, -1).astype(jnp.bfloat16),
-        contract_first(out_rows, activated).astype(jnp.bfloat16),
-    )
+def planes_of(weight):
+    return jnp.transpose(weight, (1, 0, 2))
+
+
+def stacked(left, back, planes):
+    width = left.shape[1]
+    pieces = back.reshape(back.shape[0], planes, -1)
+    terms = jnp.einsum("ri,rpj->pij", left, pieces, preferred_element_type=jnp.float32)
+    return low(terms).reshape(planes, 4, width // 4, -1)
 
 
 def local(
@@ -113,12 +532,17 @@
 ):
     sections = lax.axis_size("section")
     columns = lax.axis_size("mp")
-    whole_triple, whole_output, whole_gate_up, whole_down = (
-        lax.all_gather(triple_weight, "section", axis=0, tiled=True),
-        lax.all_gather(output_weight, "section", axis=0, tiled=True),
-        lax.all_gather(gate_up_weight, "section", axis=0, tiled=True),
-        lax.all_gather(down_weight, "section", axis=0, tiled=True),
-    )
+    whole_triple, whole_output, whole_gate_up, whole_down = gather_weights(
+        planes_of(triple_weight),
+        output_weight[None],
+        planes_of(gate_up_weight),
+        down_weight[None],
+    )
+    width = block_input.shape[2]
+    whole_triple = planes_of(whole_triple.reshape(3, width, -1))
+    whole_gate_up = planes_of(whole_gate_up.reshape(2, width, -1))
+    whole_output = whole_output.reshape(width, -1)
+    whole_down = whole_down.reshape(width, -1)
     patches = block_input[0]
     rows, width = patches.shape
     cells = rows // 4
@@ -136,16 +560,12 @@
         projected[:, 0], projected[:, 1], projected[:, 2], allowed
     )
     heads_out = mixed.reshape(rows, -1)
-    middle = start + lax.psum(
-        contract_last(heads_out, whole_output).astype(jnp.bfloat16), "mp"
-    ).astype(jnp.float32)
+    middle = start + sum_mp(contract_last(heads_out, whole_output).astype(jnp.bfloat16)).astype(jnp.float32)
     scale_two = root_scale(middle)
     feed_input = (middle * scale_two * norm_gains[1]).astype(jnp.bfloat16)
     gate_up = product(feed_input, whole_gate_up.reshape(width, -1)).reshape(rows, 2, -1)
     activated = (jax.nn.silu(gate_up[:, 0]) * gate_up[:, 1]).astype(jnp.bfloat16)
-    block_out = middle + lax.psum(
-        contract_last(activated, whole_down).astype(jnp.bfloat16), "mp"
-    ).astype(jnp.float32)
+    block_out = middle + sum_mp(contract_last(activated, whole_down).astype(jnp.bfloat16)).astype(jnp.float32)
     scale_three = root_scale(block_out)
     merged = (block_out * scale_three * merge_gain).astype(jnp.bfloat16).reshape(cells, 4 * width)
     pre = product(lax.all_gather(merged, "section", axis=0, tiled=True), merge_up)
@@ -198,8 +618,7 @@
     owned = lax.psum_scatter(
         pieces.astype(jnp.bfloat16), "section", scatter_dimension=0, tiled=True
     )
-    cells_back = lax.psum(owned, "mp").astype(jnp.float32)[0]
-    cells_back = cells_back.reshape(rows, width)
+    cells_back = sum_mp(owned.reshape(rows, width)).astype(jnp.float32)
     out_back = norm_backward(cells_back, block_out, scale_three, merge_gain)
     out_low = out_back.astype(jnp.bfloat16)
     activated_back = product(out_low, whole_down)
@@ -209,8 +628,8 @@
     gate_part = activated_back * upper * sigmoid_gate * (1.0 + gate * (1.0 - sigmoid_gate))
     up_part = activated_back * gate * sigmoid_gate
     gate_up_back = jnp.stack([gate_part, up_part], axis=1).astype(jnp.bfloat16).reshape(rows, -1)
-    feed_back = lax.psum(
-        contract_last(gate_up_back, whole_gate_up.reshape(width, -1)).astype(jnp.bfloat16), "mp"
+    feed_back = sum_mp(
+        contract_last(gate_up_back, whole_gate_up.reshape(width, -1)).astype(jnp.bfloat16)
     ).astype(jnp.float32)
     middle_back = out_back + norm_backward(feed_back, middle, scale_two, norm_gains[1])
     middle_low = middle_back.astype(jnp.bfloat16)
@@ -218,8 +637,8 @@
     triple_back = local_attention_backward(
         heads_back, projected[:, 0], projected[:, 1], projected[:, 2], shares, shares_low
     ).reshape(rows, -1)
-    attend_back = lax.psum(
-        contract_last(triple_back, whole_triple.reshape(width, -1)).astype(jnp.bfloat16), "mp"
+    attend_back = sum_mp(
+        contract_last(triple_back, whole_triple.reshape(width, -1)).astype(jnp.bfloat16)
     ).astype(jnp.float32)
     input_gradient = (middle_back + norm_backward(attend_back, start, scale_one, norm_gains[0]))[
         None
@@ -230,36 +649,18 @@
             jnp.sum(feed_back * middle * scale_two, axis=0),
         ]
     )
-    gain_gradient = lax.psum(gain_terms, ("dp", "section"))
-    local_terms = pack_terms(
-        attend_input,
-        middle_low,
-        feed_input,
-        out_low,
-        triple_back,
-        heads_out,
-        gate_up_back,
-        activated,
-    )
-    owned_terms = (
-        lax.psum_scatter(local_terms[0], "section", scatter_dimension=0, tiled=True).astype(
-            jnp.float32
-        ),
-        lax.psum_scatter(local_terms[1], "section", scatter_dimension=0, tiled=True).astype(
-            jnp.float32
-        ),
-        lax.psum_scatter(local_terms[2], "section", scatter_dimension=0, tiled=True).astype(
-            jnp.float32
-        ),
-        lax.psum_scatter(local_terms[3], "section", scatter_dimension=0, tiled=True).astype(
-            jnp.float32
-        ),
+    gradients, gain_gradient = reduce_gradients(
+        gain_terms,
+        stacked(attend_input, triple_back, 3),
+        stacked(middle_low, heads_out, 1),
+        stacked(feed_input, gate_up_back, 2),
+        stacked(out_low, activated, 1),
     )
     gradients = (
-        lax.psum(owned_terms[0].astype(jnp.bfloat16), "dp").astype(jnp.float32),
-        lax.psum(owned_terms[1].astype(jnp.bfloat16), "dp").astype(jnp.float32),
-        lax.psum(owned_terms[2].astype(jnp.bfloat16), "dp").astype(jnp.float32),
-        lax.psum(owned_terms[3].astype(jnp.bfloat16), "dp").astype(jnp.float32),
+        planes_of(gradients[0]),
+        gradients[1][0],
+        planes_of(gradients[2]),
+        gradients[3][0],
     )
     return (
         sequence,

time: 929 us -> 656 us (0.71)
  waiting for transfers between devices: 551 us -> 168 us
  Pallas kernels: 0 us -> 296 us
  blocking collectives: 180 us -> 0 us
  local copies, waits for them, and re-layouts: 61 us -> 74.8 us
  other arithmetic: 29.8 us -> 19.5 us
    pallas_call x0 -> x7, Pallas kernels: none -> 296 us  [the longest x1 129 us: reduce_gradients(): pl.pallas_call(functools.partial(reduce_kernel, count), out_shape=[jax.Sh...]
    psum x6 -> x0, waiting for transfers between devices: 200 us -> none  [the longest x1 52.1 us: local(): lax.psum(contract_last(activated, whole_down).astype(jnp.bfloat16), 'mp')]
    psum x1 -> x0, blocking collectives: 160 us -> none  [local(): gain_gradient = lax.psum(gain_terms, ('dp', 'section'))]
    reduce_scatter x4 -> x0, waiting for transfers between devices: 105 us -> none  [the longest x1 52.4 us: local(): lax.psum_scatter(local_terms[2], 'section', scatter_dimension=0, tiled=True)]
    all_gather x3 -> x0, waiting for transfers between devices: 88.5 us -> none  [the longest x1 51.1 us: local(): lax.all_gather(gate_up_weight, 'section', axis=0, tiled=True)]
    all_gather x1, waiting for transfers between devices: 0.02 us -> 46 us  [local(): lax.all_gather(visual_back[None], ('section', 'mp'), axis=0, tiled=True)]
    all_gather x1 -> x0, blocking collectives: 19.7 us -> none  [local(): lax.all_gather(output_weight, 'section', axis=0, tiled=True)]
    reduce_scatter x1, waiting for transfers between devices: 84.6 us -> 66.6 us  [local(): lax.psum_scatter(terms.reshape(sections * columns, cells, -1).astype(jnp....]
  transfers between devices with their start and end apart: 19 -> 6, of which waited for: 15 -> 6; matrix products, arithmetic and copies ran while one was open for 11% -> 6% of each run, Pallas kernels for 0% -> 0%
where the time goes in v1:
time: 656 us; the launch traced here: 646 us
  Pallas kernels  296 us (45%)
  waiting for transfers between devices  168 us (26%)
  local copies, waits for them, and re-layouts  74.8 us (11%)
  matrix products  68.6 us (10%)
  other arithmetic  19.5 us (3%)
  between operations  14.6 us (2%)
    pallas_call x1, Pallas kernels, reduce_gradients(): pl.pallas_call(functools.partial(reduce_kernel, count), out_shape=[jax.Sh...  129 us
    pallas_call x1, Pallas kernels, gather_weights(): pl.pallas_call(functools.partial(gather_kernel, count), out_shape=[jax.Sh...  88.4 us
    pallas_call x5, Pallas kernels, sum_mp(): pl.pallas_call(functools.partial(sum_kernel, chunks), out_shape=jax.Shape...  79.1 us
    reduce_scatter x1, waiting for transfers between devices, local(): lax.psum_scatter(terms.reshape(sections * columns, cells, -1).astype(jnp....  66.6 us
    all_gather x1, waiting for transfers between devices, local(): lax.all_gather(visual_back[None], ('section', 'mp'), axis=0, tiled=True)  46 us
    reduce_scatter x1, waiting for transfers between devices, local(): lax.psum_scatter(pieces.astype(jnp.bfloat16), 'section', scatter_dimensio...  23 us
    dot_general x5, matrix products, contract_last(): lax.dot_general(left, right, (((1,), (1,)), ((), ())), preferred_element_...  19.4 us
    convert_element_type x4, local copies, waits for them, and re-layouts, low(): return values.astype(jnp.bfloat16)  19.1 us
  transfers between devices with their start and end apart: 6, of which 6 were waited for; matrix products, arithmetic and copies ran while one was open for 6% of the time, Pallas kernels for 0%

profile of v1, /device:TPU:0, one launch (start us, length us, event | category | flops | bytes accessed | tf_op | source)
XLA Modules:
  0.0 646.0 jit_solution(7337085378517514334)
XLA Ops:
  9.8 88.4 %gather_weights.1 = (bf16[3,4,320,320]{3,2,1,0:T(8,128)(2,1)}, bf16[1,4,320,320]{3,2,1,0:T(8,128)(2,1)}, bf16[2,4,320,855]{3,2,1,0:T(8,128)(2,1)}, bf16[1,4,320,855]{3,2,1,0:T(8,128)(2,1)}) custom-call(bf16[3,320,320]{2,1,0:T(8,128)(2,1)} %bitcast.328, bf16[1,320,320]{2,1,0:T(8,128)(2,1)} %bitcast.337, bf16[2,320,855]{2,1,0:T(8,128)(2,1)} %bitcast.317, ...), custom_call_target="tpu_custom_call" | custom-call | tf_op jit(solution)/shard_map/gather_weights/pallas_call | solution.py:205
  98.2 5.3 copy.48
  105.7 3.6 convolution_convert_fusion.8
  116.3 15.8 %sum_mp.5 = bf16[256,1280]{1,0:T(8,128)(2,1)} custom-call(bf16[256,1280]{1,0:T(8,128)(2,1)} %convolution_convert_fusion.6.part), custom_call_target="tpu_custom_call" | custom-call | tf_op jit(solution)/shard_map/sum_mp/pallas_call | solution.py:118
  134.1 7.2 %copy.50 = bf16[2,1280,855]{1,2,0:T(8,128)(2,1)} copy(bf16[2,1280,855]{2,1,0:T(8,128)(2,1)} %bitcast.316) | data formatting | bytes 8755200 | tf_op jit(solution)/shard_map/reshape | solution.py:543
  141.3 5.2 reshape.322
  146.5 5.1 dot_general.79
  151.6 4.2 fusion.127
  158.9 15.9 %sum_mp.6 = bf16[256,1280]{1,0:T(8,128)(2,1)} custom-call(bf16[256,1280]{1,0:T(8,128)(2,1)} %convolution_convert_fusion.7.part), custom_call_target="tpu_custom_call" | custom-call | tf_op jit(solution)/shard_map/sum_mp/pallas_call | solution.py:118
  181.1 3.5 scatter_custom_fusion
  188.2 6.0 collective-permute-done.1
  196.0 18.9 %all-gather.4.cloned.1.call-done = bf16[256,5120]{1,0:T(8,128)(2,1)} async-done(((bf16[64,5120]{1,0:T(8,128)(2,1)}), bf16[256,5120]{1,0:T(8,128)(2,1)}) %all-gather.4.cloned.1.call-update) | async-done | bytes 2621456 | tf_op jit(solution)/shard_map/all_gather | solution.py:571
  214.9 3.6 multiply_convert_fusion.3
  220.2 6.9 %fusion.8 = bf16[4,64,4,2048]{3,1,2,0:T(8,128)(2,1)} fusion(bf16[4,64,320,1]{2,1,3,0:T(8,128)(2,1)} %bitcast.338, bf16[40,4,8,2048]{3,2,1,0:T(8,128)(2,1)} %bitcast.306), kind=kOutput, calls=%fused_computation.13 | convolution fusion | flops 1344274432 | bytes 9601024 | tf_op jit(solution)/shard_map/sck,kme->smce/dot_general | solution.py:575
  227.2 46.0 %all-gather.6.cloned.1.call-done = bf16[1024,2048]{1,0:T(8,128)(2,1)} async-done(((bf16[64,2048]{1,0:T(8,128)(2,1)}), bf16[1024,2048]{1,0:T(8,128)(2,1)}) %all-gather.6.cloned.1.call-update) | async-done | bytes 4194320 | tf_op jit(solution)/shard_map/all_gather | solution.py:607
  273.2 4.7 copy.53
  278.0 11.0 %convolution_convert_fusion = bf16[256,5120]{1,0:T(8,128)(2,1)} fusion(bf16[5120,320]{0,1:T(8,128)(2,1)S(1)} %copy-done, bf16[256,2048,4]{1,0,2:T(8,128)(2,1)} %bitcast.310, bf16[40,4,8,2048]{3,2,1,0:T(8,128)(2,1)} %bitcast.307, f32[256,320]{0,1:T(8,128)} %get-tuple-element.65), kind=kOutput, calls=%fused_computation.4 | convolution fusion | flops 2183168000 | bytes 15663104 | tf_op jit(solution)/shard_map/dot_general | solution.py:469
  289.0 66.6 %reduce-scatter.3.cloned.1.call-done = bf16[1,64,2048]{2,1,0:T(8,128)(2,1)} async-done(((bf16[16,64,2048]{2,1,0:T(8,128)(2,1)}), bf16[1,64,2048]{2,1,0:T(8,128)(2,1)}) %reduce-scatter.3.cloned.1.call-update) | async-done | bytes 262160 | tf_op jit(solution)/shard_map/reduce_scatter | solution.py:582
  357.0 7.3 %collective-permute-done = bf16[64,2048]{1,0:T(8,128)(2,1)S(1)} collective-permute-done((bf16[64,2048]{1,0:T(8,128)(2,1)}, bf16[64,2048]{1,0:T(8,128)(2,1)S(1)}, u32[]{:S(2)}, u32[]{:S(2)}) %collective-permute-start) | collective-permute-done | bytes 262176 | tf_op jit(solution)/shard_map/ppermute | solution.py:439
  367.9 23.0 %reduce-scatter.5.cloned.1.call-done = bf16[1,64,5120]{2,1,0:T(8,128)(2,1)} async-done(((bf16[4,64,5120]{2,1,0:T(8,128)(2,1)}), bf16[1,64,5120]{2,1,0:T(8,128)(2,1)}) %reduce-scatter.5.cloned.1.call-update) | async-done | bytes 655376 | tf_op jit(solution)/shard_map/reduce_scatter | solution.py:618
  393.3 15.9 %sum_mp.7 = bf16[256,1280]{1,0:T(8,128)(2,1)} custom-call(bf16[256,1280]{1,0:T(8,128)(2,1)} %reshape.328.part), custom_call_target="tpu_custom_call" | custom-call | tf_op jit(solution)/shard_map/sum_mp/pallas_call | solution.py:118
  410.9 3.8 fusion.92
  417.1 15.8 %sum_mp.8 = bf16[256,1280]{1,0:T(8,128)(2,1)} custom-call(bf16[256,1280]{1,0:T(8,128)(2,1)} %fusion.11.part), custom_call_target="tpu_custom_call" | custom-call | tf_op jit(solution)/shard_map/sum_mp/pallas_call | solution.py:118
  442.5 3.4 convolution_convert_fusion.10
  448.4 3.7 fusion.10
  452.1 3.5 fusion.7
  459.3 15.8 %sum_mp.9 = bf16[256,1280]{1,0:T(8,128)(2,1)} custom-call(bf16[256,1280]{1,0:T(8,128)(2,1)} %convolution_convert_fusion.5.part), custom_call_target="tpu_custom_call" | custom-call | tf_op jit(solution)/shard_map/sum_mp/pallas_call | solution.py:118
  476.7 4.5 copy.61
  481.1 7.2 %copy.60 = bf16[2,1280,855]{2,1,0:T(8,128)(2,1)} copy(bf16[2,1280,855]{1,2,0:T(8,128)(2,1)} %fusion.7) | data formatting | bytes 8755200 | tf_op jit(solution)/shard_map/convert_element_type | solution.py:74
  492.9 5.2 copy.58
  498.9 128.7 %reduce_gradients.1 = (f32[3,320,320]{2,1,0:T(8,128)}, f32[1,320,320]{2,1,0:T(8,128)}, f32[2,320,855]{2,1,0:T(8,128)}, f32[1,320,855]{2,1,0:T(8,128)}, f32[8,1280]{1,0:T(8,128)}) custom-call(bf16[3,4,320,320]{3,2,1,0:T(8,128)(2,1)} %bitcast.311, bf16[1,4,320,320]{3,2,1,0:T(8,128)(2,1)} %bitcast.322, bf16[2,4,320,855]{3,2,1,0:T(8,128)(2,1)} %bitcast.308, ...), custom_call_target="tpu_custom_call" | custom-call | tf_op jit(solution)/shard_map/reduce_gradients/pallas_call | solution.py:419
  627.6 4.9 copy.62
  (154 shorter events, 70.8 us)
Async XLA Ops:
  7.2 207.7 %copy-start = (bf16[5120,320]{0,1:T(8,128)(2,1)S(1)}, bf16[5120,320]{0,1:T(8,128)(2,1)}, u32[]{:S(2)}) copy-start(bf16[5120,320]{0,1:T(8,128)(2,1)} %param.24) | copy-start | bytes 9830404
  7.2 207.7 %all-gather.4.cloned.1.call-start = ((), (), s32[]{:S(2)}) async-start(), calls=%async_computation.2 | async-start | bytes 3276800 | tf_op jit(solution)/shard_map/all_gather | solution.py:571
  98.2 5.3 copy-start.30
  98.2 7.2 %copy-start.37 = (s32[1,64]{1,0:T(1,128)S(1)}, s32[1,64]{1,0:T(1,128)}, u32[]{:S(2)}) copy-start(s32[1,64]{1,0:T(1,128)} %param.14) | copy-start | bytes 772
  105.4 3.9 copy-start.31
  105.7 6.1 copy-start.29
  113.7 18.5 %copy-start.2 = (bf16[1,256,1280]{2,1,0:T(8,128)(2,1)S(1)}, bf16[1,256,1280]{2,1,0:T(8,128)(2,1)}, u32[]{:S(2)}) copy-start(bf16[1,256,1280]{2,1,0:T(8,128)(2,1)} %param.13) | copy-start | bytes 1966084
  151.6 5.6 copy-start.38
  158.9 15.9 %copy-start.3 = (bf16[1,256,1280]{2,1,0:T(8,128)(2,1)S(1)}, bf16[1,256,1280]{2,1,0:T(8,128)(2,1)}, u32[]{:S(2)}) copy-start(bf16[1,256,1280]{2,1,0:T(8,128)(2,1)} %param.13) | copy-start | bytes 1966084
  174.8 2.3 copy-start.5
  178.3 2.8 copy-start.35
  180.6 92.6 %all-gather.6.cloned.1.call-start = ((), (), s32[]{:S(2)}) async-start(), calls=%async_computation.5 | async-start | bytes 4456448 | tf_op jit(solution)/shard_map/all_gather | solution.py:607
  185.6 8.6 %collective-permute-start.1 = (bf16[64,2048]{1,0:T(8,128)(2,1)S(1)}, bf16[64,2048]{1,0:T(8,128)(2,1)S(1)}, u32[]{:S(2)}, u32[]{:S(2)}) collective-permute-start(bf16[64,2048]{1,0:T(8,128)(2,1)S(1)} %slice.55), channel_id=1, source_target_pairs={{0,16},{16,32},{32,48},{48,64},{64,80},{80,96},{96,112},{1,17},{17... | collective-permute-start | bytes 786440 | tf_op jit(solution)/shard_map/ppermute | solution.py:439
  195.9 159.7 %reduce-scatter.3.cloned.1.call-start = ((), (), s32[]{:S(2)}) async-start(), calls=%async_computation.3 | async-start | bytes 4456448 | tf_op jit(solution)/shard_map/reduce_scatter | solution.py:582
  227.1 163.8 %reduce-scatter.5.cloned.1.call-start = ((), (), s32[]{:S(2)}) async-start(), calls=%async_computation.4 | async-start | bytes 3276800 | tf_op jit(solution)/shard_map/reduce_scatter | solution.py:618
  355.6 8.7 %collective-permute-start = (bf16[64,2048]{1,0:T(8,128)(2,1)}, bf16[64,2048]{1,0:T(8,128)(2,1)S(1)}, u32[]{:S(2)}, u32[]{:S(2)}) collective-permute-start(bf16[64,2048]{1,0:T(8,128)(2,1)} %bitcast.335), channel_id=1, source_target_pairs={{16,0},{32,16},{48,32},{64,48},{80,64},{96,80},{112,96},{17,1},{33... | collective-permute-start | bytes 786440 | tf_op jit(solution)/shard_map/ppermute | solution.py:439
  367.9 41.2 %copy-start.4 = (bf16[1,256,1280]{2,1,0:T(8,128)(2,1)S(1)}, bf16[1,256,1280]{2,1,0:T(8,128)(2,1)}, u32[]{:S(2)}) copy-start(bf16[1,256,1280]{2,1,0:T(8,128)(2,1)} %param.13) | copy-start | bytes 1966084
  367.9 41.2 %copy-start.6 = (bf16[256,1280]{1,0:T(8,128)(2,1)S(1)}, bf16[256,1280]{1,0:T(8,128)(2,1)}, u32[]{:S(2)}) copy-start(bf16[256,1280]{1,0:T(8,128)(2,1)} %sum_mp.5) | copy-start | bytes 1966084
  367.9 41.3 %copy-start.8 = (bf16[256,1280]{1,0:T(8,128)(2,1)S(1)}, bf16[256,1280]{1,0:T(8,128)(2,1)}, u32[]{:S(2)}) copy-start(bf16[256,1280]{1,0:T(8,128)(2,1)} %sum_mp.6) | copy-start | bytes 1966084
  393.3 17.6 %copy-start.33 = (f32[256]{0:T(256)S(1)}, f32[256]{0:T(256)}, u32[]{:S(2)}) copy-start(f32[256]{0:T(256)} %get-tuple-element.60) | copy-start | bytes 3076
  409.2 5.6 slice-start
  410.9 3.9 slice-start.1
  435.8 3.4 copy-start.40
  448.4 3.7 copy-start.16
  448.4 3.7 copy-start.18
  452.1 4.8 copy-start.25
  452.1 4.8 copy-start.26
  452.1 4.8 copy-start.27
  459.3 15.8 %copy-start.32 = (f32[256]{0:T(256)S(1)}, f32[256]{0:T(256)}, u32[]{:S(2)}) copy-start(f32[256]{0:T(256)} %copy-done.31) | copy-start | bytes 3076
  627.5 6.3 copy-start.12
  627.6 6.3 copy-start.36
  636.6 2.6 copy-start.1
  (17 other events, 28.6 us)
Sparse Core Ops, SparseCore 0:
  180.7 34.1 all-gather.3
  217.9 55.2 all-gather.5
  277.2 78.3 reduce-scatter.2
  358.0 32.8 reduce-scatter.4

commit v2 on v1

--- a/solution.py
+++ b/solution.py
@@ -433,12 +433,6 @@
     return results[:count], results[count][:2]
 
 
-def passed_along(value, axis, steps):
-    count = lax.axis_size(axis)
-    initial, last = (max(0, -steps), min(count, count - steps))
-    return lax.ppermute(value, axis, [(source, source + steps) for source in range(initial, last)])
-
-
 def root_scale(values):
     return lax.rsqrt(jnp.mean(values * values, axis=-1, keepdims=True) + epsilon)
 
@@ -502,6 +496,259 @@
     query_back = jnp.einsum("hqk,khd->qhd", score_back, keys, preferred_element_type=jnp.float32)
     key_back = jnp.einsum("hqk,qhd->khd", score_back, queries, preferred_element_type=jnp.float32)
     return jnp.stack([query_back, key_back, value_back], axis=1).astype(jnp.bfloat16)
+
+
+STEP = 512
+
+
+def last_with_last(left, right):
+    return lax.dot_general(
+        left, right, (((1,), (1,)), ((), ())), preferred_element_type=jnp.float32
+    )
+
+
+def merger_kernel(
+    rows_across,
+    rows_down,
+    cotangent,
+    text,
+    merged,
+    up,
+    down,
+    sequence,
+    cells_back,
+    spill,
+    spill_in,
+    backs,
+    cells,
+    pre,
+    hidden,
+    hidden_back,
+    terms,
+    terms_in,
+    visual_in,
+    visual,
+    following,
+    pieces,
+    pieces_in,
+    parts,
+    parts_in,
+    *sems,
+):
+    me = Place()
+    merged_s, share_s, dp_s, back_s, fore_s, terms_s, visual_s, pieces_s, parts_s, mp_s = [
+        (sems[2 * i], sems[2 * i + 1]) for i in range(10)
+    ]
+    sibling, partner = me.at(core=1 - me.core), me.at(high=1 - me.high)
+    turn = 1 - me.low
+    after = me.at(z=(me.z + me.low) % 4, low=turn)
+    before = me.at(z=(me.z + 3 + me.low) % 4, low=turn)
+    pairs = [(j, k) for k in (1, 3, 2) for j in (0, 1)] + [(1, 0)]
+
+    def peer(j, k):
+        return me.at(y=me.along_y(k), high=(me.high + j) % 2)
+
+    greet([peer(j, k) for j, k in pairs] + [sibling, after, before])
+    pending = []
+
+    def go(*arguments):
+        copy = send(*arguments)
+        pending.append(copy)
+        return copy
+
+    half = pl.ds(pl.multiple_of(me.core * 32, 32), 32)
+    merged_copies = {
+        k: go(merged.at[half], cells.at[me.y, half], merged_s, k, peer(0, k)) for k in (1, 3, 2)
+    }
+    cells[me.y] = merged[...]
+
+    slot = lax.broadcasted_iota(jnp.int32, (128, 256), 0)
+    offset = (me.z * 2 + me.low) * 64
+    taken = jnp.where(rows_across[...] - offset == slot, 1.0, 0.0).astype(jnp.bfloat16)
+    for i in range(4):
+        span = pl.ds(i * STEP, STEP)
+        arrived = low(product(taken, cotangent[:, span]))
+        spill[:, span] = arrived[64:]
+        backs[me.y, me.high * 2 + me.core, :, span] = arrived[:64]
+    spill_copy = go(spill, spill_in, dp_s, 0, after)
+    spill_copy.wait_recv()
+    own = me.high * 2 + me.core
+    for i in range(4):
+        span = pl.ds(i * STEP, STEP)
+        backs[me.y, own, :, span] = backs[me.y, own, :, span] + spill_in[:, span]
+    block = backs.at[me.y, own]
+    back_copies = [go(block, block, back_s, j * 4 + k, peer(j, k)) for j, k in pairs]
+    fore_copies = [go(block, block, fore_s, 0, sibling)]
+
+    share_copies = []
+    for k in (1, 3, 2):
+        merged_copies[k].wait_recv()
+        region = cells.at[me.along_y(4 - k), half]
+        share_copies.append(go(region, region, share_s, k, sibling))
+    for copy in share_copies:
+        copy.wait_recv()
+
+    pre[...] = jnp.zeros_like(pre)
+
+    @pl.loop(0, 10)
+    def _(i):
+        span = pl.ds(pl.multiple_of(i * STEP, STEP), STEP)
+        pre[...] += last_with_last(cells[:, :, span].reshape(256, STEP), up[:, span])
+
+    hidden[...] = low(gelu_value(pre[...]))
+
+    def term_block(column):
+        @pl.loop(0, 4)
+        def _(i):
+            span = pl.ds(pl.multiple_of(i * STEP, STEP), STEP)
+            whole = pl.ds(pl.multiple_of(column * 2048 + i * STEP, STEP), STEP)
+            terms[column, :, span] = low(product(hidden[...], down[:, whole]))
+
+    term_copies = []
+    for j in (0, 1):
+        column = j * 2 + 1 - me.core
+        term_block(column)
+        term_copies.append(go(terms.at[column], terms_in.at[j], terms_s, j, sibling))
+    for j in (0, 1):
+        term_block(j * 2 + me.core)
+
+    for (j, k), copy in zip(pairs, back_copies):
+        copy.wait_recv()
+        region = backs.at[me.along_y((4 - k) % 4), ((me.high + j) % 2) * 2 + me.core]
+        fore_copies.append(go(region, region, fore_s, j * 4 + k, sibling))
+    for j in (0, 1):
+        term_copies[j].wait_recv()
+        column = j * 2 + me.core
+
+        @pl.loop(0, 16)
+        def _(i):
+            here = pl.ds(pl.multiple_of(i * 16, 16), 16)
+            terms[column, here] = low(wide(terms[column, here]) + wide(terms_in[j, here]))
+
+    def visual_region(j, k):
+        rows = pl.ds(pl.multiple_of(me.along_y(k) * 64, 64), 64)
+        return terms.at[((me.high + j) % 2) * 2 + me.core, rows]
+
+    for copy in fore_copies:
+        copy.wait_recv()
+    hidden_back[...] = jnp.zeros_like(hidden_back)
+
+    @pl.loop(0, 16)
+    def _(i):
+        inner = pl.ds(pl.multiple_of((i % 4) * STEP, STEP), STEP)
+        outer = pl.ds(pl.multiple_of(i * STEP, STEP), STEP)
+        left = backs[:, i // 4, :, inner].reshape(256, STEP)
+        hidden_back[...] += last_with_last(left, down[:, outer])
+
+    hidden[...] = low(hidden_back[...] * gelu_slope(pre[...]))
+
+    @pl.loop(0, 10)
+    def _(i):
+        span = pl.ds(pl.multiple_of(i * STEP, STEP), STEP)
+        pieces[:, :, :, :, span] = low(product(hidden[...], up[:, span])).reshape(4, 2, 2, 16, STEP)
+
+    pieces_copy = go(pieces.at[:, :, 1 - me.core], pieces_in, pieces_s, 0, sibling)
+    pieces_copy.wait_recv()
+
+    @pl.loop(0, 8)
+    def _(i):
+        a, b = i // 2, i % 2
+        for n in range(4):
+            span = pl.ds(n * 1280, 1280)
+            parts[a, b, :, span] = low(
+                wide(pieces[a, b, me.core, :, span]) + wide(pieces_in[a, b, :, span])
+            )
+
+    part_copies = [
+        go(parts.at[me.along_y(k), (me.high + j) % 2], parts_in.at[j * 4 + k], parts_s, j * 4 + k, peer(j, k))
+        for j, k in pairs
+    ]
+    visual_copies = [
+        go(visual_region(j, k), visual_in.at[j * 4 + k], visual_s, j * 4 + k, peer(j, k))
+        for j, k in pairs
+    ]
+    for copy in part_copies:
+        copy.wait_recv()
+    mine = pl.ds(pl.multiple_of(own * 16, 16), 16)
+    for n in range(4):
+        span = pl.ds(n * 1280, 1280)
+        total = wide(parts[me.y, me.high, :, span])
+        for j, k in pairs:
+            total = total + wide(parts_in[j * 4 + k, :, span])
+        cells_back[mine, span] = low(total)
+    mp_copies = [
+        go(cells_back.at[mine], cells_back.at[mine], mp_s, 0, partner),
+        go(cells_back.at[mine], cells_back.at[mine], mp_s, 1, sibling),
+    ]
+    mp_copies[0].wait_recv()
+    theirs = pl.ds(pl.multiple_of(((1 - me.high) * 2 + me.core) * 16, 16), 16)
+    mp_copies.append(go(cells_back.at[theirs], cells_back.at[theirs], mp_s, 2, sibling))
+
+    for copy in visual_copies:
+        copy.wait_recv()
+    mine_rows = pl.multiple_of(me.y * 64, 64)
+
+    @pl.loop(0, 4)
+    def _(i):
+        here = pl.ds(pl.multiple_of(i * 16, 16), 16)
+        total = wide(terms[own, pl.ds(pl.multiple_of(mine_rows + i * 16, 16), 16)])
+        for j, k in pairs:
+            total = total + wide(visual_in[j * 4 + k, here])
+        visual[here] = low(total)
+
+    visual_copy = go(visual, following, dp_s, 1, before)
+    slot = lax.broadcasted_iota(jnp.int32, (256, 64), 1)
+    here_cells = jnp.where(rows_down[...] - offset == slot, 1.0, 0.0).astype(jnp.bfloat16)
+    next_cells = jnp.where(rows_down[...] - offset - 64 == slot, 1.0, 0.0).astype(jnp.bfloat16)
+    visual_copy.wait_recv()
+    for i in range(4):
+        span = pl.ds(i * STEP, STEP)
+        picked = product(here_cells, visual[:, span]) + product(next_cells, following[:, span])
+        sequence[:, span] = jnp.where(rows_down[...] >= 0, low(picked), text[:, span])
+    mp_copies[1].wait_recv()
+    mp_copies[2].wait_recv()
+    for copy in pending:
+        copy.wait_send()
+
+
+def merger(cell_rows, cotangent, text, merged, up, down):
+    def buffer(*shape):
+        return pltpu.VMEM(shape, jnp.bfloat16)
+
+    scratch = [
+        buffer(64, 2048),
+        buffer(64, 2048),
+        buffer(4, 4, 64, 2048),
+        buffer(4, 64, 5120),
+        pltpu.VMEM((256, 320), jnp.float32),
+        buffer(256, 320),
+        pltpu.VMEM((256, 320), jnp.float32),
+        buffer(4, 256, 2048),
+        buffer(2, 256, 2048),
+        buffer(8, 64, 2048),
+        buffer(64, 2048),
+        buffer(64, 2048),
+        buffer(4, 2, 2, 16, 5120),
+        buffer(4, 2, 16, 5120),
+        buffer(4, 2, 16, 5120),
+        buffer(8, 16, 5120),
+    ]
+    for size in (4, 4, 2, 8, 8, 2, 8, 1, 8, 3):
+        scratch += sem_pair(size)
+    return pl.pallas_call(
+        merger_kernel,
+        out_shape=[
+            jax.ShapeDtypeStruct(text.shape, jnp.bfloat16),
+            jax.ShapeDtypeStruct(merged.shape, jnp.bfloat16),
+        ],
+        in_specs=[VMEM] * 7,
+        out_specs=[VMEM] * 2,
+        scratch_shapes=scratch,
+        compiler_params=pltpu.CompilerParams(
+            collective_id=4, has_side_effects=True, vmem_limit_bytes=VMEM_LIMIT
+        ),
+        name="merger",
+    )(cell_rows[None], cell_rows[:, None], cotangent, text, merged, up, down)
 
 
 def planes_of(weight):
@@ -530,8 +777,6 @@
     merge_up,
     merge_down,
 ):
-    sections = lax.axis_size("section")
-    columns = lax.axis_size("mp")
     whole_triple, whole_output, whole_gate_up, whole_down = gather_weights(
         planes_of(triple_weight),
         output_weight[None],
@@ -568,57 +813,11 @@
     block_out = middle + sum_mp(contract_last(activated, whole_down).astype(jnp.bfloat16)).astype(jnp.float32)
     scale_three = root_scale(block_out)
     merged = (block_out * scale_three * merge_gain).astype(jnp.bfloat16).reshape(cells, 4 * width)
-    pre = product(lax.all_gather(merged, "section", axis=0, tiled=True), merge_up)
-    hidden_cells = gelu_value(pre).astype(jnp.bfloat16)
-    local_units = merge_up.shape[1]
-    llm_width = merge_down.shape[1]
-    terms = jnp.einsum(
-        "sck,kme->smce",
-        hidden_cells.reshape(sections, cells, local_units),
-        merge_down.reshape(local_units, columns, llm_width // columns),
-        preferred_element_type=jnp.float32,
-    )
-    visual = (
-        lax.psum_scatter(
-            terms.reshape(sections * columns, cells, -1).astype(jnp.bfloat16),
-            ("section", "mp"),
-            scatter_dimension=0,
-            tiled=True,
-        )
-        .astype(jnp.float32)[0]
-        .astype(jnp.bfloat16)
-    )
-    following = passed_along(visual, "dp", -1)
-    candidates = jnp.concatenate([visual, following], axis=0)
-    offset = lax.axis_index("dp") * cells
-    row_cells = cell_rows[0]
-    is_visual = row_cells >= 0
-    local_cells = jnp.where(is_visual, row_cells - offset, 0)
-    picked = jnp.take(candidates, local_cells, axis=0)
-    sequence = jnp.where(is_visual[:, None], picked, text_vectors[0])[None]
-    slots = jnp.where(is_visual, row_cells - offset, 2 * cells)
-    arrived = (
-        jnp.zeros((2 * cells + 1, visual.shape[1]), jnp.bfloat16)
-        .at[slots]
-        .set(sequence_cotangent[0])
-    )
-    returned = passed_along(arrived[cells : 2 * cells], "dp", 1)
-    visual_back = arrived[:cells] + returned
-    gathered_back = lax.all_gather(visual_back[None], ("section", "mp"), axis=0, tiled=True)
-    hidden_back = jnp.einsum(
-        "smce,kme->sck",
-        gathered_back.reshape(sections, columns, cells, -1),
-        merge_down.reshape(local_units, columns, -1),
-        preferred_element_type=jnp.float32,
-    )
-    pre_back = (hidden_back.reshape(sections * cells, local_units) * gelu_slope(pre)).astype(
-        jnp.bfloat16
-    )
-    pieces = contract_last(pre_back, merge_up).reshape(sections, cells, -1)
-    owned = lax.psum_scatter(
-        pieces.astype(jnp.bfloat16), "section", scatter_dimension=0, tiled=True
-    )
-    cells_back = sum_mp(owned.reshape(rows, width)).astype(jnp.float32)
+    sequence, cells_back = merger(
+        cell_rows[0], sequence_cotangent[0], text_vectors[0], merged, merge_up.T, merge_down
+    )
+    sequence = sequence[None]
+    cells_back = cells_back.reshape(rows, width).astype(jnp.float32)
     out_back = norm_backward(cells_back, block_out, scale_three, merge_gain)
     out_low = out_back.astype(jnp.bfloat16)
     activated_back = product(out_low, whole_down)

time: 656 us -> 505 us (0.77); the launches traced: 646 us -> 503 us
  waiting for transfers between devices: 168 us -> 0 us
  Pallas kernels: 296 us -> 392 us
  matrix products: 68.6 us -> 38 us
  between operations: 14.6 us -> 1.08 us
  local copies, waits for them, and re-layouts: 74.8 us -> 61.3 us
  other arithmetic: 19.5 us -> 10.7 us
    pallas_call x0 -> x1, Pallas kernels: none -> 113 us  [merger(): pl.pallas_call(merger_kernel, out_shape=[jax.ShapeDtypeStruct(text.shape,...]
    reduce_scatter x2 -> x0, waiting for transfers between devices: 89.5 us -> none  [the longest x1 66.6 us: local(): lax.psum_scatter(terms.reshape(sections * columns, cells, -1).astype(jnp....]
    all_gather x2 -> x0, waiting for transfers between devices: 65 us -> none  [the longest x1 46 us: local(): lax.all_gather(visual_back[None], ('section', 'mp'), axis=0, tiled=True)]
    pallas_call x5 -> x4, Pallas kernels: 79.1 us -> 63.1 us  [sum_mp(): pl.pallas_call(functools.partial(sum_kernel, chunks), out_shape=jax.Shape...]
    ppermute x2 -> x0, waiting for transfers between devices: 13.4 us -> none  [passed_along(): lax.ppermute(value, axis, [(source, source + steps) for source in range(i...]
    dot_general x5 -> x4, matrix products: 19.4 us -> 8.77 us  [contract_last(): lax.dot_general(left, right, (((1,), (1,)), ((), ())), preferred_element_...]
    dot_general x5 -> x4, matrix products: 15.8 us -> 7.31 us  [product(): return jnp.dot(left, right, preferred_element_type=jnp.float32)]
    dot_general x1 -> x0, matrix products: 6.9 us -> none  [local(): jnp.einsum('sck,kme->smce', hidden_cells.reshape(sections, cells, local_u...]
  transfers between devices with their start and end apart: 6 -> 0, of which waited for: 6 -> 0; matrix products, arithmetic and copies ran while one was open for 6% -> 0% of each run, Pallas kernels for 0% -> 0%
where the time goes in v2:
time: 505 us; the launch traced here: 503 us
  Pallas kernels  392 us (78%)
  local copies, waits for them, and re-layouts  61.3 us (12%)
  matrix products  38 us (8%)
  other arithmetic  10.7 us (2%)
    pallas_call x1, Pallas kernels, reduce_gradients(): pl.pallas_call(functools.partial(reduce_kernel, count), out_shape=[jax.Sh...  128 us
    pallas_call x1, Pallas kernels, merger(): pl.pallas_call(merger_kernel, out_shape=[jax.ShapeDtypeStruct(text.shape,...  113 us
    pallas_call x1, Pallas kernels, gather_weights(): pl.pallas_call(functools.partial(gather_kernel, count), out_shape=[jax.Sh...  88.4 us
    pallas_call x4, Pallas kernels, sum_mp(): pl.pallas_call(functools.partial(sum_kernel, chunks), out_shape=jax.Shape...  63.1 us
    convert_element_type x4, local copies, waits for them, and re-layouts, low(): return values.astype(jnp.bfloat16)  17 us
    unnamed x68, local copies, waits for them, and re-layouts  16.7 us

profile of v2, /device:TPU:0, one launch (start us, length us, event | category | flops | bytes accessed | tf_op | source)
XLA Modules:
  0.0 503.2 jit_solution(16232550653716179087)
XLA Ops:
  2.1 2.4 copy.49
  4.5 88.4 %gather_weights.1 = (bf16[3,4,320,320]{3,2,1,0:T(8,128)(2,1)}, bf16[1,4,320,320]{3,2,1,0:T(8,128)(2,1)}, bf16[2,4,320,855]{3,2,1,0:T(8,128)(2,1)}, bf16[1,4,320,855]{3,2,1,0:T(8,128)(2,1)}) custom-call(bf16[3,320,320]{2,1,0:T(8,128)(2,1)} %bitcast.259, bf16[1,320,320]{2,1,0:T(8,128)(2,1)} %bitcast.266, bf16[2,320,855]{2,1,0:T(8,128)(2,1)} %bitcast.246, ...), custom_call_target="tpu_custom_call" | custom-call | tf_op jit(solution)/shard_map/gather_weights/pallas_call | solution.py:205
  92.9 7.2 %copy.34 = bf16[2,1280,855]{1,2,0:T(8,128)(2,1)} copy(bf16[2,1280,855]{2,1,0:T(8,128)(2,1)} %bitcast.245) | data formatting | bytes 8755200 | tf_op jit(solution)/shard_map/reshape | solution.py:788
  100.2 5.2 %reshape.204 = bf16[1280,1710]{0,1:T(8,128)(2,1)} reshape(bf16[1280,2,855]{0,2,1:T(8,128)(2,1)} %bitcast.236) | data formatting | bytes 8755200 | tf_op jit(solution)/shard_map/reshape | solution.py:811
  105.4 5.1 %dot_general.63 = bf16[2,855,1280]{2,1,0:T(8,128)(2,1)} reshape(bf16[1710,1280]{1,0:T(8,128)(2,1)} %bitcast.240) | data formatting | bytes 8755200 | tf_op jit(solution)/shard_map/dot_general | solution.py:459
  110.5 4.0 copy.32
  114.8 1.7 convolution_convert_fusion.7
  116.8 2.5 fusion.95
  121.8 15.8 %sum_mp.4 = bf16[256,1280]{1,0:T(8,128)(2,1)} custom-call(bf16[256,1280]{1,0:T(8,128)(2,1)} %convolution_convert_fusion.5.part), custom_call_target="tpu_custom_call" | custom-call | tf_op jit(solution)/shard_map/sum_mp/pallas_call | solution.py:118
  139.1 3.9 fusion.93
  145.2 1.7 convolution_convert_fusion.6.part
  147.0 15.8 %sum_mp.5 = bf16[256,1280]{1,0:T(8,128)(2,1)} custom-call(bf16[256,1280]{1,0:T(8,128)(2,1)} %convolution_convert_fusion.6.part), custom_call_target="tpu_custom_call" | custom-call | tf_op jit(solution)/shard_map/sum_mp/pallas_call | solution.py:118
  162.8 1.5 multiply_reduce_fusion.1
  165.9 112.9 %merger.1 = (bf16[256,2048]{1,0:T(8,128)(2,1)}, bf16[64,5120]{1,0:T(8,128)(2,1)}) custom-call(s32[1,256]{1,0:T(1,128)} %rows_across.1, s32[256,1]{1,0:T(8,128)} %copy.35.rows_down, bf16[256,2048]{1,0:T(8,128)(2,1)} %bitcast.256, bf16[256,2048]{1,0:T(8,128)(2,1)} %bitcast.257, bf16[64,5120]{1,0:T(8,128)(2,1)} %reshape.206.merged, ...), custom_call_target="tpu_custom_call" | custom-call | tf_op jit(solution)/shard_map/merger/pallas_call | solution.py:738
  284.6 2.3 fusion.5.part
  286.9 15.8 %sum_mp.6 = bf16[256,1280]{1,0:T(8,128)(2,1)} custom-call(bf16[256,1280]{1,0:T(8,128)(2,1)} %fusion.5.part), custom_call_target="tpu_custom_call" | custom-call | tf_op jit(solution)/shard_map/sum_mp/pallas_call | solution.py:118
  302.7 1.7 fusion.29
  306.1 1.8 convolution_convert_fusion.8
  307.9 2.2 fusion.80
  310.1 2.9 convolution_convert_fusion.9
  313.0 2.9 convolution_convert_fusion.10
  316.0 3.4 convolution_convert_fusion.4.part
  319.4 15.8 %sum_mp.7 = bf16[256,1280]{1,0:T(8,128)(2,1)} custom-call(bf16[256,1280]{1,0:T(8,128)(2,1)} %convolution_convert_fusion.4.part), custom_call_target="tpu_custom_call" | custom-call | tf_op jit(solution)/shard_map/sum_mp/pallas_call | solution.py:118
  335.2 1.6 fusion.36
  338.2 2.4 fusion.3
  340.6 5.2 %copy.39 = bf16[3,1280,320]{2,1,0:T(8,128)(2,1)} copy(bf16[3,1280,320]{1,2,0:T(8,128)(2,1)} %fusion.3) | data formatting | bytes 4915200 | tf_op jit(solution)/shard_map/convert_element_type | solution.py:74
  348.5 3.5 fusion.2
  352.0 7.4 %copy.41 = bf16[2,1280,855]{2,1,0:T(8,128)(2,1)} copy(bf16[2,1280,855]{1,2,0:T(8,128)(2,1)} %fusion.2) | data formatting | bytes 8755200 | tf_op jit(solution)/shard_map/convert_element_type | solution.py:74
  359.4 1.8 fusion.4
  361.1 3.1 copy.42
  365.0 127.7 %reduce_gradients.1 = (f32[3,320,320]{2,1,0:T(8,128)}, f32[1,320,320]{2,1,0:T(8,128)}, f32[2,320,855]{2,1,0:T(8,128)}, f32[1,320,855]{2,1,0:T(8,128)}, f32[8,1280]{1,0:T(8,128)}) custom-call(bf16[3,4,320,320]{3,2,1,0:T(8,128)(2,1)} %bitcast.241, bf16[1,4,320,320]{3,2,1,0:T(8,128)(2,1)} %bitcast.249, bf16[2,4,320,855]{3,2,1,0:T(8,128)(2,1)} %bitcast.239, ...), custom_call_target="tpu_custom_call" | custom-call | tf_op jit(solution)/shard_map/reduce_gradients/pallas_call | solution.py:419
  492.8 4.9 copy.43
  (101 shorter events, 27.9 us)
Async XLA Ops:
  110.5 4.0 copy-start.25
  110.5 4.0 copy-start
  114.5 2.0 copy-start.6
  114.8 1.7 copy-start.26
  116.5 2.8 copy-start.24
  119.3 1.2 copy-start.9
  120.0 17.6 %copy-start.21 = (bf16[4,80,256]{2,1,0:T(8,128)(2,1)}, bf16[4,80,256]{2,1,0:T(8,128)(2,1)S(1)}, u32[]{:S(2)}) copy-start(bf16[4,80,256]{2,1,0:T(8,128)(2,1)S(1)} %convolution_convert_fusion.11) | copy-start | bytes 491524
  137.6 1.5 copy-start.1
  139.1 6.1 %copy-start.27 = (bf16[1,4,320,855]{3,2,1,0:T(8,128)(2,1)S(1)}, bf16[1,4,320,855]{3,2,1,0:T(8,128)(2,1)}, u32[]{:S(2)}) copy-start(bf16[1,4,320,855]{3,2,1,0:T(8,128)(2,1)} %get-tuple-element.21) | copy-start | bytes 6566404
  143.0 1.2 copy-start.11
  144.5 0.8 copy-start.13
  162.8 1.6 copy-start.2
  162.8 1.6 copy-start.23
  280.3 1.5 copy-start.12
  280.3 2.2 copy-start.28
  280.7 3.9 slice-start
  282.5 1.2 copy-start.3
  282.5 2.2 slice-start.1
  283.7 0.8 copy-start.14
  283.7 0.9 copy-start.16
  302.7 1.7 copy-start.4
  302.7 1.7 copy-start.7
  304.4 1.2 copy-start.10
  335.2 1.6 copy-start.8
  347.2 1.3 copy-start.15
  347.2 1.3 copy-start.17
  352.0 7.4 %copy-start.5 = (f32[256,1280]{1,0:T(8,128)S(1)}, f32[256,1280]{1,0:T(8,128)}, u32[]{:S(2)}) copy-start(f32[256,1280]{1,0:T(8,128)} %copy-done.3) | copy-start | bytes 3932164
  492.7 6.4 %copy-start.20 = (bf16[256,2048]{1,0:T(8,128)(2,1)S(1)}, bf16[256,2048]{1,0:T(8,128)(2,1)}, u32[]{:S(2)}) copy-start(bf16[256,2048]{1,0:T(8,128)(2,1)} %get-tuple-element.22) | copy-start | bytes 3145732
  497.6 2.5 copy-start.18
  500.1 1.3 copy-start.22
  500.1 2.1 copy-start.19

commit v3 on v0

v3 whole, which is shorter than its diff:
```python
import functools
import math

import jax
import jax.numpy as jnp
from jax import lax
from jax.experimental import pallas as pl
from jax.experimental.pallas import tpu as pltpu
from jax.sharding import PartitionSpec as P

HEAD_DIM = 80


epsilon = 1e-06
root_half = 0.7071067811865476
density_scale = 0.3989422804014327

MESH = pl.DeviceIdType.MESH
VMEM_LIMIT = 60 * 1024 * 1024
VMEM = pl.BlockSpec(memory_space=pltpu.VMEM)
ANY = pl.BlockSpec(memory_space=pl.ANY)


class Place:
    def __init__(self):
        dp, self.y, mp = lax.axis_index("dp"), lax.axis_index("section"), lax.axis_index("mp")
        self.z, self.low = dp // 2, dp % 2
        self.high, self.core = mp // 2, mp % 2

    def at(self, z=None, low=None, y=None, high=None, core=None):
        z = self.z if z is None else z
        low = self.low if low is None else low
        y = self.y if y is None else y
        high = self.high if high is None else high
        core = self.core if core is None else core
        return (z * 2 + low, y, high * 2 + core)

    def along_y(self, k):
        return (self.y + k) % 4

    def along_z(self, k):
        return (self.z + k) % 4


def greet(devices):
    barrier = pltpu.get_barrier_semaphore()
    for device in devices:
        pl.semaphore_signal(barrier, inc=1, device_id=device, device_id_type=MESH)
    pl.semaphore_wait(barrier, len(devices))


def send(source, target, sems, index, device):
    copy = pltpu.make_async_remote_copy(
        src_ref=source,
        dst_ref=target,
        send_sem=sems[0].at[index],
        recv_sem=sems[1].at[index],
        device_id=device,
        device_id_type=MESH,
    )
    copy.start()
    return copy


def sem_pair(*shape):
    return [pltpu.SemaphoreType.DMA(shape), pltpu.SemaphoreType.DMA(shape)]


def wide(values):
    return values.astype(jnp.float32)


def low(values):
    return values.astype(jnp.bfloat16)


def root_scale(values):
    return lax.rsqrt(jnp.mean(values * values, axis=-1, keepdims=True) + epsilon)


def norm_backward(cotangent, values, scale, gain):
    weighted = cotangent * gain
    return scale * weighted - values * scale**3 * jnp.mean(
        weighted * values, axis=-1, keepdims=True
    )


def gelu_value(values):
    return 0.5 * values * (1.0 + jax.scipy.special.erf(values * root_half))


def gelu_slope(values):
    return (
        0.5 * (1.0 + jax.scipy.special.erf(values * root_half))
        + values * jnp.exp(-0.5 * values * values) * density_scale
    )


def product(left, right):
    return jnp.dot(left, right, preferred_element_type=jnp.float32)


QUARTER, HALF = 48, 48
ALONE = 320 - 4 * QUARTER - 2 * HALF
UNITS = ((0, 0, 3), (1, 0, 1), (2, 0, 1), (2, 1, 1), (3, 0, 1))
PAIRS = [(j, k) for k in (1, 3, 2) for j in (0, 1)] + [(1, 0)]


STEP = 512


def last_with_last(left, right):
    return lax.dot_general(
        left, right, (((1,), (1,)), ((), ())), preferred_element_type=jnp.float32
    )


def merger_kernel(
    rows_down,
    text,
    merged,
    backs,
    up,
    down,
    sequence,
    cells_back,
    cells,
    pre,
    hidden,
    pre_back,
    hidden_back,
    terms,
    terms_in,
    visual_in,
    visual,
    following,
    pieces,
    pieces_in,
    parts,
    parts_in,
    *sems,
):
    me = Place()
    merged_s, share_s, dp_s, terms_s, visual_s, pieces_s, parts_s, mp_s = [
        (sems[2 * i], sems[2 * i + 1]) for i in range(8)
    ]
    sibling, partner = me.at(core=1 - me.core), me.at(high=1 - me.high)
    turn = 1 - me.low
    after = me.at(z=(me.z + me.low) % 4, low=turn)
    before = me.at(z=(me.z + 3 + me.low) % 4, low=turn)

    def peer(j, k):
        return me.at(y=me.along_y(k), high=(me.high + j) % 2)

    greet([peer(j, k) for j, k in PAIRS] + [sibling, after, before])
    pending = []

    def go(*arguments):
        copy = send(*arguments)
        pending.append(copy)
        return copy

    half = pl.ds(pl.multiple_of(me.core * 32, 32), 32)
    merged_copies = {
        k: go(merged.at[half], cells.at[me.y, half], merged_s, k, peer(0, k)) for k in (1, 3, 2)
    }
    cells[me.y] = merged[...]
    own = me.high * 2 + me.core
    hidden_back[...] = jnp.zeros_like(hidden_back)

    @pl.loop(0, 16)
    def _(i):
        inner = pl.ds(pl.multiple_of((i % 4) * STEP, STEP), STEP)
        outer = pl.ds(pl.multiple_of(i * STEP, STEP), STEP)
        left = backs[:, i // 4, :, inner].reshape(256, STEP)
        hidden_back[...] += last_with_last(left, down[:, outer])

    share_copies = []
    for k in (1, 3, 2):
        merged_copies[k].wait_recv()
        region = cells.at[me.along_y(4 - k), half]
        share_copies.append(go(region, region, share_s, k, sibling))
    for copy in share_copies:
        copy.wait_recv()

    pre[...] = jnp.zeros_like(pre)

    @pl.loop(0, 10)
    def _(i):
        span = pl.ds(pl.multiple_of(i * STEP, STEP), STEP)
        pre[...] += last_with_last(cells[:, :, span].reshape(256, STEP), up[:, span])

    pre_back[...] = low(hidden_back[...] * gelu_slope(pre[...]))

    @pl.loop(0, 10)
    def _(i):
        span = pl.ds(pl.multiple_of(i * STEP, STEP), STEP)
        pieces[:, :, :, :, span] = low(product(pre_back[...], up[:, span])).reshape(4, 2, 2, 16, STEP)

    pieces_copy = go(pieces.at[:, :, 1 - me.core], pieces_in, pieces_s, 0, sibling)
    hidden[...] = low(gelu_value(pre[...]))
    pieces_copy.wait_recv()

    @pl.loop(0, 8)
    def _(i):
        a, b = i // 2, i % 2
        for n in range(4):
            span = pl.ds(n * 1280, 1280)
            parts[a, b, :, span] = low(
                wide(pieces[a, b, me.core, :, span]) + wide(pieces_in[a, b, :, span])
            )

    part_copies = [
        go(parts.at[me.along_y(k), (me.high + j) % 2], parts_in.at[j * 4 + k], parts_s, j * 4 + k, peer(j, k))
        for j, k in PAIRS
    ]

    def term_block(column):
        @pl.loop(0, 4)
        def _(i):
            span = pl.ds(pl.multiple_of(i * STEP, STEP), STEP)
            whole = pl.ds(pl.multiple_of(column * 2048 + i * STEP, STEP), STEP)
            terms[column, :, span] = low(product(hidden[...], down[:, whole]))

    term_copies = []
    for j in (0, 1):
        column = j * 2 + 1 - me.core
        term_block(column)
        term_copies.append(go(terms.at[column], terms_in.at[j], terms_s, j, sibling))
    for j in (0, 1):
        column = j * 2 + me.core
        term_block(column)
        term_copies[j].wait_recv()

        @pl.loop(0, 16)
        def _(i):
            here = pl.ds(pl.multiple_of(i * 16, 16), 16)
            terms[column, here] = low(wide(terms[column, here]) + wide(terms_in[j, here]))

    def visual_region(j, k):
        rows = pl.ds(pl.multiple_of(me.along_y(k) * 64, 64), 64)
        return terms.at[((me.high + j) % 2) * 2 + me.core, rows]

    visual_copies = [
        go(visual_region(j, k), visual_in.at[j * 4 + k], visual_s, j * 4 + k, peer(j, k))
        for j, k in PAIRS
    ]
    for copy in part_copies:
        copy.wait_recv()
    mine = pl.ds(pl.multiple_of(own * 16, 16), 16)
    for n in range(4):
        span = pl.ds(n * 1280, 1280)
        total = wide(parts[me.y, me.high, :, span])
        for j, k in PAIRS:
            total = total + wide(parts_in[j * 4 + k, :, span])
        cells_back[mine, span] = low(total)
    mp_copies = [
        go(cells_back.at[mine], cells_back.at[mine], mp_s, 0, partner),
        go(cells_back.at[mine], cells_back.at[mine], mp_s, 1, sibling),
    ]
    mp_copies[0].wait_recv()
    theirs = pl.ds(pl.multiple_of(((1 - me.high) * 2 + me.core) * 16, 16), 16)
    mp_copies.append(go(cells_back.at[theirs], cells_back.at[theirs], mp_s, 2, sibling))

    for copy in visual_copies:
        copy.wait_recv()
    mine_rows = pl.multiple_of(me.y * 64, 64)

    @pl.loop(0, 4)
    def _(i):
        here = pl.ds(pl.multiple_of(i * 16, 16), 16)
        total = wide(terms[own, pl.ds(pl.multiple_of(mine_rows + i * 16, 16), 16)])
        for j, k in PAIRS:
            total = total + wide(visual_in[j * 4 + k, here])
        visual[here] = low(total)

    visual_copy = go(visual, following, dp_s, 0, before)
    slot = lax.broadcasted_iota(jnp.int32, (256, 64), 1)
    offset = (me.z * 2 + me.low) * 64
    here_cells = jnp.where(rows_down[...] - offset == slot, 1.0, 0.0).astype(jnp.bfloat16)
    next_cells = jnp.where(rows_down[...] - offset - 64 == slot, 1.0, 0.0).astype(jnp.bfloat16)
    visual_copy.wait_recv()
    for i in range(4):
        span = pl.ds(i * STEP, STEP)
        picked = product(here_cells, visual[:, span]) + product(next_cells, following[:, span])
        sequence[:, span] = jnp.where(rows_down[...] >= 0, low(picked), text[:, span])
    mp_copies[1].wait_recv()
    mp_copies[2].wait_recv()
    for copy in pending:
        copy.wait_send()


def merger(cell_rows, text, merged, backs, up, down):
    def buffer(*shape):
        return pltpu.VMEM(shape, jnp.bfloat16)

    scratch = [
        buffer(4, 64, 5120),
        pltpu.VMEM((256, 320), jnp.float32),
        buffer(256, 320),
        buffer(256, 320),
        pltpu.VMEM((256, 320), jnp.float32),
        buffer(4, 256, 2048),
        buffer(2, 256, 2048),
        buffer(8, 64, 2048),
        buffer(64, 2048),
        buffer(64, 2048),
        buffer(4, 2, 2, 16, 5120),
        buffer(4, 2, 16, 5120),
        buffer(4, 2, 16, 5120),
        buffer(8, 16, 5120),
    ]
    for size in (4, 4, 1, 2, 8, 1, 8, 3):
        scratch += sem_pair(size)
    return pl.pallas_call(
        merger_kernel,
        out_shape=[
            jax.ShapeDtypeStruct(text.shape, jnp.bfloat16),
            jax.ShapeDtypeStruct(merged.shape, jnp.bfloat16),
        ],
        in_specs=[VMEM] * 6,
        out_specs=[VMEM] * 2,
        scratch_shapes=scratch,
        compiler_params=pltpu.CompilerParams(
            collective_id=4, has_side_effects=True, vmem_limit_bytes=VMEM_LIMIT
        ),
        name="merger",
    )(cell_rows[:, None], text, merged, backs, up, down)


CHUNKS = 4


class SumOverMp:
    def __init__(self, me, go, buffers, sems):
        self.me, self.go = me, go
        self.outgoing, self.got, self.half, self.other, self.total = buffers
        self.sems = sems
        self.sibling, self.partner = me.at(core=1 - me.core), me.at(high=1 - me.high)
        self.mine = pl.multiple_of(me.core * 128, 128)
        self.theirs = pl.multiple_of((1 - me.core) * 128, 128)

    def begin(self, compute):
        step = 128 // CHUNKS
        self.outgoing[...] = low(compute(pl.ds(self.theirs, 128)))
        first = []
        for k in range(CHUNKS):
            here = pl.ds(k * step, step)
            first.append(
                self.go(self.outgoing.at[here], self.got.at[here], self.sems, k, self.sibling)
            )
        self.half[...] = low(compute(pl.ds(self.mine, 128)))
        self.second = []
        for k in range(CHUNKS):
            here = pl.ds(k * step, step)
            first[k].wait_recv()
            self.half[here] = low(wide(self.half[here]) + wide(self.got[here]))
            self.second.append(
                self.go(self.half.at[here], self.other.at[here], self.sems, CHUNKS + k, self.partner)
            )

    def end(self):
        step = 128 // CHUNKS
        third = []
        for k in range(CHUNKS):
            here = pl.ds(k * step, step)
            there = pl.ds(pl.multiple_of(self.mine + k * step, step), step)
            self.second[k].wait_recv()
            self.total[there] = low(wide(self.half[here]) + wide(self.other[here]))
            third.append(
                self.go(
                    self.total.at[there], self.total.at[there], self.sems, 2 * CHUNKS + k, self.sibling
                )
            )
        for copy in third:
            copy.wait_recv()


def sum_buffers():
    half = pltpu.VMEM((128, 1280), jnp.bfloat16)
    return [half, half, half, half, pltpu.VMEM((256, 1280), jnp.bfloat16)]


def head_mask(head):
    lane = lax.broadcasted_iota(jnp.int32, (1, 320), 1)
    inside = (lane >= head * HEAD_DIM) & (lane < (head + 1) * HEAD_DIM)
    return jnp.where(inside, 1.0, 0.0).astype(jnp.bfloat16)


def head_shares(queries, keys, mask, allowed):
    scores = last_with_last(queries * mask, keys) * (1.0 / math.sqrt(HEAD_DIM))
    scores = jnp.where(allowed, scores, -1e30)
    raised = jnp.exp(scores - jnp.max(scores, axis=-1, keepdims=True))
    return raised / jnp.sum(raised, axis=-1, keepdims=True)


def forward_kernel(*refs):
    block_input, across, downwards, gains, merge_gain, rows_across, cotangent = refs[:7]
    shards = refs[7:11]
    wholes = refs[11:15]
    attend, projected, heads_out, middle, feed, gate, upper, activated, block_out, merged = refs[15:25]
    backs, spill, spill_in = refs[25:28]
    sum_one, sum_two = refs[28:33], refs[33:38]
    own, *pairs = refs[38:]
    y_s, z_s, x_s, one_s, two_s, dp_s, back_s, fore_s = [
        (pairs[2 * i], pairs[2 * i + 1]) for i in range(8)
    ]
    me = Place()
    others = (1, 3, 2)
    y_at = {k: me.at(y=me.along_y(k)) for k in others}
    z_at = {k: me.at(z=me.along_z(k)) for k in others}
    side, sibling = me.at(low=1 - me.low), me.at(core=1 - me.core)
    after = me.at(z=(me.z + me.low) % 4, low=1 - me.low)
    far = me.at(z=(me.z + 3 + 2 * me.low) % 4, low=1 - me.low)

    def peer(j, k):
        return me.at(y=me.along_y(k), high=(me.high + j) % 2)

    greet([peer(j, k) for j, k in PAIRS] + [z_at[k] for k in others] + [side, far, sibling])
    pending = []

    def go(*arguments):
        copy = send(*arguments)
        pending.append(copy)
        return copy

    spans = (
        pl.ds(pl.multiple_of(me.z * QUARTER, 16), QUARTER),
        pl.ds(pl.multiple_of(4 * QUARTER + me.low * HALF, 16), HALF),
        pl.ds(320 - ALONE, ALONE),
    )
    local_copies, first, second = [], {}, {}

    def begin(u):
        t, p, n = UNITS[u]
        for k in others:
            for part in range(3):
                first[u, k, part] = go(
                    shards[t].at[pl.ds(p, n), spans[part]],
                    wholes[t].at[pl.ds(p, n), me.y, spans[part]],
                    y_s,
                    (u * 3 + k - 1) * 3 + part,
                    y_at[k],
                )

    def forward(u):
        t, p, n = UNITS[u]
        copies = []
        for k in others:
            source = me.along_y(4 - k)
            first[u, k, 0].wait_recv()
            block = wholes[t].at[pl.ds(p, n), source, spans[0]]
            for j in others:
                copies.append(go(block, block, z_s, (u * 3 + k - 1) * 3 + j - 1, z_at[j]))
            first[u, k, 1].wait_recv()
            block = wholes[t].at[pl.ds(p, n), source, spans[1]]
            copies.append(go(block, block, x_s, u * 3 + k - 1, side))
            copies.append(first[u, k, 2])
        second[u] = copies

    def complete(u):
        for copy in second[u]:
            copy.wait_recv()

    def whole(t, p):
        return wholes[t][p].reshape(1280, -1)

    begin(0)
    begin(1)
    for t in range(4):
        copy = pltpu.make_async_copy(shards[t], wholes[t].at[:, me.y], own.at[t])
        copy.start()
        local_copies.append(copy)
    slot = lax.broadcasted_iota(jnp.int32, (128, 256), 0)
    offset = (me.z * 2 + me.low) * 64
    taken = jnp.where(rows_across[...] - offset == slot, 1.0, 0.0).astype(jnp.bfloat16)
    column = me.high * 2 + me.core
    for i in range(4):
        span = pl.ds(i * STEP, STEP)
        arrived = low(product(taken, cotangent[:, span]))
        spill[:, span] = arrived[64:]
        backs[me.y, column, :, span] = arrived[:64]
    spill_copy = go(spill, spill_in, dp_s, 0, after)
    start = wide(block_input[...])
    attend[...] = low(start * root_scale(start) * gains[0:1])
    forward(0)
    begin(2)
    forward(1)
    begin(3)
    complete(0)
    for copy in local_copies:
        copy.wait()
    for p in range(3):
        projected[p] = low(product(attend[...], whole(0, p)))
    forward(2)
    begin(4)
    allowed = downwards[...] == across[...]
    mixed = jnp.zeros((256, 320), jnp.float32)
    for head in range(4):
        mask = head_mask(head)
        shares = head_shares(projected[0], projected[1], mask, allowed)
        mixed = mixed + product(low(shares), projected[2] * mask)
    heads_out[...] = low(mixed)
    complete(1)
    forward(3)
    total = SumOverMp(me, go, sum_one, one_s)
    total.begin(lambda rows: last_with_last(heads_out[rows], whole(1, 0)))
    spill_copy.wait_recv()
    for i in range(4):
        span = pl.ds(i * STEP, STEP)
        backs[me.y, column, :, span] = backs[me.y, column, :, span] + spill_in[:, span]
    forward(4)
    total.end()
    block = backs.at[me.y, column]
    back_copies = [go(block, block, back_s, j * 4 + k, peer(j, k)) for j, k in PAIRS]
    fore_copies = [go(block, block, fore_s, 0, sibling)]
    middle[...] = wide(block_input[...]) + wide(sum_one[4][...])
    feed[...] = low(middle[...] * root_scale(middle[...]) * gains[1:2])
    complete(2)
    gate[...] = product(feed[...], whole(2, 0))
    complete(3)
    upper[...] = product(feed[...], whole(2, 1))
    activated[...] = low(gate[...] * jax.nn.sigmoid(gate[...]) * upper[...])
    complete(4)
    total = SumOverMp(me, go, sum_two, two_s)
    total.begin(lambda rows: last_with_last(activated[rows], whole(3, 0)))
    for (j, k), copy in zip(PAIRS, back_copies):
        copy.wait_recv()
        region = backs.at[me.along_y((4 - k) % 4), ((me.high + j) % 2) * 2 + me.core]
        fore_copies.append(go(region, region, fore_s, j * 4 + k, sibling))
    total.end()
    block_out[...] = middle[...] + wide(sum_two[4][...])
    merged[...] = low(block_out[...] * root_scale(block_out[...]) * merge_gain[...])
    for copy in fore_copies:
        copy.wait_recv()
    for copy in pending:
        copy.wait_send()


def block_forward(block_input, patch_windows, gains, merge_gain, cell_rows, cotangent, shards):
    rows, width = block_input.shape
    units = shards[2].shape[2]

    def shape(kind, *dims):
        return jax.ShapeDtypeStruct(dims, kind)

    low_, wide_ = jnp.bfloat16, jnp.float32
    outs = [shape(low_, s.shape[0], 4, *s.shape[1:]) for s in shards] + [
        shape(low_, rows, width),
        shape(low_, 3, rows, 320),
        shape(low_, rows, 320),
        shape(wide_, rows, width),
        shape(low_, rows, width),
        shape(wide_, rows, units),
        shape(wide_, rows, units),
        shape(low_, rows, units),
        shape(wide_, rows, width),
        shape(low_, rows, width),
        shape(low_, 4, 4, 64, cotangent.shape[1]),
    ]
    spill = pltpu.VMEM((64, cotangent.shape[1]), jnp.bfloat16)
    scratch = [spill, spill] + sum_buffers() + sum_buffers() + [pltpu.SemaphoreType.DMA((4,))]
    for size in (45, 45, 15, 3 * CHUNKS, 3 * CHUNKS, 1, 8, 8):
        scratch += sem_pair(size)
    results = pl.pallas_call(
        forward_kernel,
        out_shape=outs,
        in_specs=[VMEM] * 11,
        out_specs=[VMEM] * len(outs),
        scratch_shapes=scratch,
        compiler_params=pltpu.CompilerParams(
            collective_id=1, has_side_effects=True, vmem_limit_bytes=VMEM_LIMIT
        ),
        name="block_forward",
    )(
        block_input,
        patch_windows[None],
        patch_windows[:, None],
        gains,
        merge_gain[None],
        cell_rows[None],
        cotangent,
        *shards,
    )
    return results[:4], results[4:14], results[14]


A_ROWS = 192
A_PART = A_ROWS // 4
B_PART = (320 - A_ROWS) // 4
E_ROWS = A_PART + B_PART
TILE = 16
ORDER = (1, 3, 2)


def over_rows(planes, rows, body):
    tiles = rows // TILE

    @pl.loop(0, planes * tiles)
    def _(i):
        body(i // tiles, pl.multiple_of((i % tiles) * TILE, TILE))


class Reduction:
    def __init__(self, me, go, term, out, buffers, sems, index, y_at, z_at, side):
        self.me, self.go, self.term, self.out = me, go, term, out
        self.ya, self.sa, self.za, self.zb, self.sb, self.yb, self.ee, self.ex = buffers
        self.sems, self.index, self.y_at, self.z_at, self.side = sems, index, y_at, z_at, side
        self.planes = term.shape[0]

    def stage_one(self):
        me = self.me
        self.first_a = [
            self.go(
                self.term.at[:, me.along_y(k), pl.ds(0, A_ROWS)],
                self.ya.at[k - 1],
                self.sems[0],
                self.index * 3 + k - 1,
                self.y_at[k],
            )
            for k in ORDER
        ]
        self.first_b = [
            self.go(
                self.term.at[
                    :, :, pl.ds(pl.multiple_of(A_ROWS + me.along_z(k) * B_PART, TILE), B_PART)
                ],
                self.zb.at[k - 1],
                self.sems[1],
                self.index * 3 + k - 1,
                self.z_at[k],
            )
            for k in ORDER
        ]

    def stage_two(self):
        me, term, ya, sa, zb, sb = self.me, self.term, self.ya, self.sa, self.zb, self.sb
        for copy in self.first_b:
            copy.wait_recv()

        def add_b(i, r):
            p, q = i // 4, i % 4
            here = pl.ds(r, TILE)
            there = pl.ds(pl.multiple_of(A_ROWS + me.z * B_PART + r, TILE), TILE)
            sb[p, q, here] = low(
                wide(term[p, q, there])
                + wide(zb[0, p, q, here])
                + wide(zb[1, p, q, here])
                + wide(zb[2, p, q, here])
            )

        over_rows(self.planes * 4, B_PART, add_b)
        self.second = [
            self.go(
                sb.at[:, me.along_y(k)],
                self.yb.at[k - 1],
                self.sems[2],
                self.index * 3 + k - 1,
                self.y_at[k],
            )
            for k in ORDER
        ]
        for copy in self.first_a:
            copy.wait_recv()

        def add_a(p, r):
            here = pl.ds(r, TILE)
            sa[p, here] = low(
                wide(term[p, me.y, here])
                + wide(ya[0, p, here])
                + wide(ya[1, p, here])
                + wide(ya[2, p, here])
            )

        over_rows(self.planes, A_ROWS, add_a)
        self.second += [
            self.go(
                sa.at[:, pl.ds(pl.multiple_of(me.along_z(k) * A_PART, TILE), A_PART)],
                self.za.at[k - 1],
                self.sems[3],
                self.index * 3 + k - 1,
                self.z_at[k],
            )
            for k in ORDER
        ]

    def stage_three(self):
        me, sa, za, sb, yb, ee = self.me, self.sa, self.za, self.sb, self.yb, self.ee
        for copy in self.second:
            copy.wait_recv()

        def add_a(p, r):
            here = pl.ds(r, TILE)
            there = pl.ds(pl.multiple_of(me.z * A_PART + r, TILE), TILE)
            ee[p, here] = low(
                wide(sa[p, there]) + wide(za[0, p, here]) + wide(za[1, p, here]) + wide(za[2, p, here])
            )

        def add_b(p, r):
            here = pl.ds(r, TILE)
            there = pl.ds(pl.multiple_of(A_PART + r, TILE), TILE)
            ee[p, there] = low(
                wide(sb[p, me.y, here])
                + wide(yb[0, p, here])
                + wide(yb[1, p, here])
                + wide(yb[2, p, here])
            )

        over_rows(self.planes, A_PART, add_a)
        over_rows(self.planes, B_PART, add_b)
        self.third = self.go(ee, self.ex, self.sems[4], self.index, self.side)

    def stage_four(self):
        me, out, ee, ex = self.me, self.out, self.ee, self.ex
        self.third.wait_recv()

        def add(p, r):
            here = pl.ds(r, TILE)
            out[me.z, p, here] = low(wide(ee[p, here]) + wide(ex[p, here]))

        over_rows(self.planes, E_ROWS, add)
        self.fourth = [
            self.go(
                out.at[me.z], out.at[me.z], self.sems[5], self.index * 3 + k - 1, self.z_at[k]
            )
            for k in ORDER
        ]

    def finish(self):
        for copy in self.fourth:
            copy.wait_recv()


def first_with_first(left, right):
    return lax.dot_general(
        left, right, (((0,), (0,)), ((), ())), preferred_element_type=jnp.float32
    )


def backward_kernel(*refs):
    (
        block_input,
        across,
        downwards,
        gains,
        merge_gain,
        cells_back,
        triple,
        output,
        gate_up,
        down,
        attend,
        projected,
        heads_out,
        middle,
        feed,
        gate,
        upper,
        activated,
        block_out,
    ) = refs[:19]
    input_gradient = refs[19]
    outs = refs[20:25]
    gain_out = refs[25]
    refs = refs[26:]
    sum_one, sum_two = refs[:5], refs[5:10]
    terms = refs[10:15]
    buffers = [refs[15 + 8 * t : 23 + 8 * t] for t in range(5)]
    middle_back, middle_low, out_low, gate_up_back, triple_back, gain, gain_in, gain_sum = refs[55:63]
    sems = refs[63:]
    pair = [(sems[2 * i], sems[2 * i + 1]) for i in range(9)]
    me = Place()
    y_at = {k: me.at(y=me.along_y(k)) for k in ORDER}
    z_at = {k: me.at(z=me.along_z(k)) for k in ORDER}
    side = me.at(low=1 - me.low)
    greet(
        [y_at[k] for k in ORDER]
        + [z_at[k] for k in ORDER]
        + [side, me.at(core=1 - me.core), me.at(high=1 - me.high)]
    )
    pending = []

    def go(*arguments):
        copy = send(*arguments)
        pending.append(copy)
        return copy

    reductions = [
        Reduction(me, go, terms[t], outs[t], buffers[t], pair[:6], t, y_at, z_at, side)
        for t in range(5)
    ]
    of_triple, of_output, of_gate, of_upper, of_down = reductions

    def form(t, p, left, right):
        for i in range(2):
            block = first_with_first(left[:, i * 640 : (i + 1) * 640], right)
            terms[t][p, 2 * i : 2 * i + 2] = low(block).reshape(2, 320, right.shape[1])

    def whole(weight, p):
        return weight[p].reshape(1280, -1)

    scale_three = root_scale(block_out[...])
    out_back = norm_backward(wide(cells_back[...]), block_out[...], scale_three, merge_gain[...])
    middle_back[...] = out_back
    out_low[...] = low(out_back)
    form(4, 0, out_low, activated[...])
    of_down.stage_one()
    activated_back = product(out_low[...], whole(down, 0))
    slope = jax.nn.sigmoid(gate[...])
    gate_up_back[1] = low(activated_back * gate[...] * slope)
    gate_up_back[0] = low(activated_back * upper[...] * slope * (1.0 + gate[...] * (1.0 - slope)))
    total = SumOverMp(me, go, sum_one, pair[6])
    total.begin(
        lambda rows: last_with_last(gate_up_back[0, rows], whole(gate_up, 0))
        + last_with_last(gate_up_back[1, rows], whole(gate_up, 1))
    )
    form(2, 0, feed, gate_up_back[0])
    of_gate.stage_one()
    total.end()
    feed_back = wide(sum_one[4][...])
    scale_two = root_scale(middle[...])
    middle_back[...] = middle_back[...] + norm_backward(
        feed_back, middle[...], scale_two, gains[1:2]
    )
    middle_low[...] = low(middle_back[...])
    gain[...] = jnp.zeros_like(gain)
    gain[1:2] = jnp.sum(feed_back * middle[...] * scale_two, axis=0, keepdims=True)
    form(3, 0, feed, gate_up_back[1])
    of_upper.stage_one()
    heads_back = low(product(middle_low[...], whole(output, 0)))
    of_down.stage_two()
    form(1, 0, middle_low, heads_out[...])
    of_output.stage_one()
    allowed = downwards[...] == across[...]
    query_back = jnp.zeros((256, 320), jnp.float32)
    key_back = jnp.zeros((256, 320), jnp.float32)
    value_back = jnp.zeros((256, 320), jnp.float32)
    for head in range(4):
        mask = head_mask(head)
        shares = head_shares(projected[0], projected[1], mask, allowed)
        share_back = last_with_last(heads_back * mask, projected[2])
        centre = jnp.sum(shares * share_back, axis=-1, keepdims=True)
        score_back = low(shares * (share_back - centre) * (1.0 / math.sqrt(HEAD_DIM)))
        query_back = query_back + product(score_back, projected[1] * mask)
        key_back = key_back + first_with_first(score_back, projected[0] * mask)
        value_back = value_back + first_with_first(low(shares), heads_back * mask)
    triple_back[0] = low(query_back)
    triple_back[1] = low(key_back)
    triple_back[2] = low(value_back)
    of_gate.stage_two()
    total = SumOverMp(me, go, sum_two, pair[7])
    total.begin(
        lambda rows: last_with_last(triple_back[0, rows], whole(triple, 0))
        + last_with_last(triple_back[1, rows], whole(triple, 1))
        + last_with_last(triple_back[2, rows], whole(triple, 2))
    )
    for p in range(3):
        form(0, p, attend, triple_back[p])
    of_triple.stage_one()
    of_down.stage_three()
    total.end()
    attend_back = wide(sum_two[4][...])
    start = wide(block_input[...])
    scale_one = root_scale(start)
    input_gradient[...] = middle_back[...] + norm_backward(attend_back, start, scale_one, gains[0:1])
    gain[0:1] = jnp.sum(attend_back * start * scale_one, axis=0, keepdims=True)
    gain_copies = [go(gain, gain_in.at[k - 1], pair[8], k - 1, y_at[k]) for k in ORDER]
    of_upper.stage_two()
    of_gate.stage_three()
    of_down.stage_four()
    of_output.stage_two()
    for copy in gain_copies:
        copy.wait_recv()
    gain_sum[0] = gain[...] + gain_in[0] + gain_in[1] + gain_in[2]
    gain_copies = [go(gain_sum.at[0], gain_in.at[2 + k], pair[8], 2 + k, z_at[k]) for k in ORDER]
    of_triple.stage_two()
    of_upper.stage_three()
    of_gate.stage_four()
    for copy in gain_copies:
        copy.wait_recv()
    gain_sum[1] = gain_sum[0] + gain_in[3] + gain_in[4] + gain_in[5]
    gain_copies = [go(gain_sum.at[1], gain_in.at[6], pair[8], 6, side)]
    of_output.stage_three()
    of_triple.stage_three()
    of_upper.stage_four()
    for copy in gain_copies:
        copy.wait_recv()
    gain_out[...] = gain_sum[1] + gain_in[6]
    of_output.stage_four()
    of_triple.stage_four()
    for reduction in reductions:
        reduction.finish()
    for copy in pending:
        copy.wait_send()


def block_backward(block_input, patch_windows, gains, merge_gain, cells_back, wholes, saved):
    rows, width = block_input.shape
    units = saved[5].shape[1]

    def low_buffer(*shape):
        return pltpu.VMEM(shape, jnp.bfloat16)

    def wide_buffer(*shape):
        return pltpu.VMEM(shape, jnp.float32)

    sizes = ((3, 320), (1, 320), (1, units), (1, units), (1, units))
    scratch = sum_buffers() + sum_buffers()
    scratch += [low_buffer(planes, 4, 320, columns) for planes, columns in sizes]
    for planes, columns in sizes:
        scratch += [
            low_buffer(3, planes, A_ROWS, columns),
            low_buffer(planes, A_ROWS, columns),
            low_buffer(3, planes, A_PART, columns),
            low_buffer(3, planes, 4, B_PART, columns),
            low_buffer(planes, 4, B_PART, columns),
            low_buffer(3, planes, B_PART, columns),
            low_buffer(planes, E_ROWS, columns),
            low_buffer(planes, E_ROWS, columns),
        ]
    scratch += [
        wide_buffer(rows, width),
        low_buffer(rows, width),
        low_buffer(rows, width),
        low_buffer(2, rows, units),
        low_buffer(3, rows, 320),
        wide_buffer(8, width),
        wide_buffer(7, 8, width),
        wide_buffer(2, 8, width),
    ]
    for size in (15, 15, 15, 15, 5, 15, 3 * CHUNKS, 3 * CHUNKS, 7):
        scratch += sem_pair(size)
    operands = [
        block_input,
        patch_windows[None],
        patch_windows[:, None],
        gains,
        merge_gain[None],
        cells_back,
        *wholes,
        *saved,
    ]
    outs = (
        [jax.ShapeDtypeStruct((rows, width), jnp.float32)]
        + [
            jax.ShapeDtypeStruct((4, planes, E_ROWS, columns), jnp.bfloat16)
            for planes, columns in sizes
        ]
        + [jax.ShapeDtypeStruct((8, width), jnp.float32)]
    )
    results = pl.pallas_call(
        backward_kernel,
        out_shape=outs,
        in_specs=[VMEM] * len(operands),
        out_specs=[VMEM] * len(outs),
        scratch_shapes=scratch,
        compiler_params=pltpu.CompilerParams(
            collective_id=3, has_side_effects=True, vmem_limit_bytes=VMEM_LIMIT
        ),
        name="block_backward",
    )(*operands)

    def assembled(owned):
        planes, columns = owned.shape[1], owned.shape[3]
        owned = jnp.transpose(owned, (1, 0, 2, 3))
        return wide(
            jnp.concatenate(
                [
                    owned[:, :, :A_PART].reshape(planes, -1, columns),
                    owned[:, :, A_PART:].reshape(planes, -1, columns),
                ],
                axis=1,
            )
        )

    gradients = [assembled(owned) for owned in results[1:6]]
    return results[0], gradients, results[6][:2]


def planes_of(weight):
    return jnp.transpose(weight, (1, 0, 2))


def local(
    block_input,
    windows,
    cell_rows,
    text_vectors,
    sequence_cotangent,
    norm_gains,
    merge_gain,
    triple_weight,
    output_weight,
    gate_up_weight,
    down_weight,
    merge_up,
    merge_down,
):
    patches = block_input[0]
    rows, width = patches.shape
    patch_windows = jnp.repeat(windows[0], 4)
    shards = (
        planes_of(triple_weight),
        output_weight[None],
        planes_of(gate_up_weight),
        down_weight[None],
    )
    wholes, saved, backs = block_forward(
        patches,
        patch_windows,
        norm_gains,
        merge_gain,
        cell_rows[0],
        sequence_cotangent[0],
        shards,
    )
    sequence, cells_back = merger(
        cell_rows[0],
        text_vectors[0],
        saved[-1].reshape(rows // 4, 4 * width),
        backs,
        merge_up.T,
        merge_down,
    )
    input_gradient, gradients, gain_gradient = block_backward(
        patches,
        patch_windows,
        norm_gains,
        merge_gain,
        cells_back.reshape(rows, width),
        wholes,
        saved[:-1],
    )
    return (
        sequence[None],
        input_gradient[None],
        planes_of(gradients[0]),
        gradients[1][0],
        jnp.stack([gradients[2][0], gradients[3][0]], axis=1),
        gradients[4][0],
        gain_gradient,
    )


def solution(mesh):
    placed = (
        P(("dp", "section"), None, None),
        P(("dp", "section"), None),
        P("section", "dp"),
        P("section", "dp", "mp"),
        P("section", "dp", "mp"),
        P(),
        P(),
        P("section", None, "mp"),
        P("section", "mp"),
        P("section", None, "mp"),
        P("section", "mp"),
        P(None, ("section", "mp")),
        P(("section", "mp"), None),
    )
    return jax.shard_map(
        local,
        mesh=mesh,
        in_specs=placed,
        out_specs=(
            P("section", "dp", "mp"),
            P(("dp", "section"), None, None),
            P("section", None, "mp"),
            P("section", "mp"),
            P("section", None, "mp"),
            P("section", "mp"),
            P(),
        ),
        check_vma=False,
    )
```

time: 929 us -> 355 us (0.38)
  waiting for transfers between devices: 551 us -> 0 us
  Pallas kernels: 0 us -> 317 us
  blocking collectives: 180 us -> 0 us
  matrix products: 74 us -> 0 us
  local copies, waits for them, and re-layouts: 61 us -> 22.6 us
  other arithmetic: 29.8 us -> 12 us
  between operations: 16.2 us -> 0.81 us
    pallas_call x0 -> x3, Pallas kernels: none -> 317 us  [the longest x1 124 us: block_backward(): pl.pallas_call(backward_kernel, out_shape=outs, in_specs=[VMEM] * len(ope...]
    reduce_scatter x6 -> x0, waiting for transfers between devices: 224 us -> none  [the longest x1 84.6 us: local(): lax.psum_scatter(terms.reshape(sections * columns, cells, -1).astype(jnp....]
    psum x6 -> x0, waiting for transfers between devices: 200 us -> none  [the longest x1 52.1 us: local(): lax.psum(contract_last(activated, whole_down).astype(jnp.bfloat16), 'mp')]
    psum x1 -> x0, blocking collectives: 160 us -> none  [local(): gain_gradient = lax.psum(gain_terms, ('dp', 'section'))]
    all_gather x5 -> x0, waiting for transfers between devices: 120 us -> none  [the longest x1 51.1 us: local(): lax.all_gather(gate_up_weight, 'section', axis=0, tiled=True)]
    dot_general x20 -> x0, matrix products: 71.5 us -> none  [the longest x5 22.9 us: contract_last(): lax.dot_general(left, right, (((1,), (1,)), ((), ())), preferred_element_...]
    all_gather x1 -> x0, blocking collectives: 19.7 us -> none  [local(): lax.all_gather(output_weight, 'section', axis=0, tiled=True)]
    all_gather x2 -> x0, local copies, waits for them, and re-layouts: 14.7 us -> none  [the longest x1 7.45 us: local(): lax.all_gather(triple_weight, 'section', axis=0, tiled=True)]
  transfers between devices with their start and end apart: 19 -> 0, of which waited for: 15 -> 0; matrix products, arithmetic and copies ran while one was open for 11% -> 0% of each run, Pallas kernels for 0% -> 0%
where the time goes in v3:
time: 355 us; the launch traced here: 353 us
  Pallas kernels  317 us (89%)
  local copies, waits for them, and re-layouts  22.6 us (6%)
  other arithmetic  12 us (3%)
    pallas_call x1, Pallas kernels, block_backward(): pl.pallas_call(backward_kernel, out_shape=outs, in_specs=[VMEM] * len(ope...  124 us
    pallas_call x1, Pallas kernels, block_forward(): pl.pallas_call(forward_kernel, out_shape=outs, in_specs=[VMEM] * 11, out_...  107 us
    pallas_call x1, Pallas kernels, merger(): pl.pallas_call(merger_kernel, out_shape=[jax.ShapeDtypeStruct(text.shape,...  86.8 us
    another operation x1, other arithmetic, local(): jnp.stack([gradients[2][0], gradients[3][0]], axis=1)  8.93 us

profile of v3, /device:TPU:0, one launch (start us, length us, event | category | flops | bytes accessed | tf_op | source)
XLA Modules:
  0.0 352.9 jit_solution(2256337308415570592)
XLA Ops:
  0.6 1.3 broadcast_in_dim.20.refs_4_
  1.9 0.7 broadcast_in_dim.19
  2.7 0.7 broadcast_in_dim_reshape.8.refs_1_
  3.3 0.7 broadcast_in_dim_reshape.10.refs_2_
  4.1 1.5 copy.27.rows_down
  5.5 2.4 copy.36
  7.9 106.9 %block_forward.1 = (bf16[3,4,320,320]{3,2,1,0:T(8,128)(2,1)}, bf16[1,4,320,320]{3,2,1,0:T(8,128)(2,1)}, bf16[2,4,320,855]{3,2,1,0:T(8,128)(2,1)}, bf16[1,4,320,8...) custom-call(bf16[256,1280]{1,0:T(8,128)(2,1)} %bitcast.33, ...), custom_call_target="tpu_custom_call" | custom-call | tf_op jit(solution)/shard_map/block_forward/pallas_call | solution.py:565
  114.8 2.2 reshape.140.merged
  117.0 86.8 %merger.1 = (bf16[256,2048]{1,0:T(8,128)(2,1)}, bf16[64,5120]{1,0:T(8,128)(2,1)}) custom-call(s32[256,1]{1,0:T(8,128)} %copy.27.rows_down, bf16[256,2048]{1,0:T(8,128)(2,1)} %bitcast.42, bf16[64,5120]{1,0:T(8,128)(2,1)} %reshape.140.merged, bf16[4,4,64,2048]{3,2,1,0:T(8,128)(2,1)} %get-tuple-element.32.backs, bf16[320,5120]{1,0:T(8,128)(2,1)} %bitcast.32, ...), custom_call_target="tpu_custom_call" | custom-call | tf_op jit(solution)/shard_map/merger/pallas_call | solution.py:315
  203.8 2.4 reshape.141.refs_5_
  206.2 123.8 %block_backward.1 = (f32[256,1280]{1,0:T(8,128)}, bf16[4,3,80,320]{3,2,1,0:T(8,128)(2,1)}, bf16[4,1,80,320]{3,2,1,0:T(8,128)(2,1)}, bf16[4,1,80,855]{3,2,1,0:T(8...) custom-call(bf16[256,1280]{1,0:T(8,128)(2,1)} %bitcast.34, ...), custom_call_target="tpu_custom_call" | custom-call | tf_op jit(solution)/shard_map/block_backward/pallas_call | solution.py:951
  330.1 0.0 copy-start.4
  330.1 1.4 slice.43
  331.5 0.9 slice.47
  332.4 0.9 slice.46
  333.4 1.0 slice.49
  334.3 0.0 copy-start.3
  334.3 1.1 slice.48
  335.4 0.4 copy.32
  335.8 0.0 copy-done.4
  335.8 0.0 copy-start.2
  335.9 0.4 copy.34
  336.3 0.8 maximum_convert_fusion.2
  337.3 0.5 copy.33
  337.8 0.5 copy.31
  338.4 8.9 %maximum_convert_fusion = f32[320,2,855]{2,1,0:T(2,128)} fusion(bf16[128,1,855]{2,1,0:T(2,128)(2,1)S(1)} %copy.34, bf16[192,1,855]{2,1,0:T(2,128)(2,1)S(1)} %copy.33, bf16[128,1,855]{2,1,0:T(2,128)(2,1)S(1)} %copy.32, bf16[192,1,855]{2,1,0:T(2,128)(2,1)S(1)} %copy.31), kind=kLoop, calls=%fused_computation.1 | loop fusion | flops 4377600 | bytes 3283200 | tf_op jit(solution)/shard_map/stack | solution.py:1039
  347.3 1.1 maximum_convert_fusion.1
  348.4 1.2 convert_bitcast_fusion
  349.6 0.5 copy-done.1
  350.1 1.0 copy.39
  351.1 0.7 copy-done
  351.8 1.1 copy.40
  (12 shorter events, 0.3 us)
Async XLA Ops:
  330.1 5.7 %copy-start.4 = (bf16[4,1,80,855]{3,2,1,0:T(8,128)(2,1)S(1)}, bf16[4,1,80,855]{3,2,1,0:T(8,128)(2,1)}, u32[]{:S(2)}) copy-start(bf16[4,1,80,855]{3,2,1,0:T(8,128)(2,1)} %get-tuple-element.52) | copy-start | bytes 1641604
  334.3 1.9 copy-start.3
  335.8 1.3 copy-start.2
  348.4 1.7 copy-start.1
  350.1 1.7 copy-start

commit v4 on v3

--- a/solution.py
+++ b/solution.py
@@ -16,9 +16,30 @@
 density_scale = 0.3989422804014327
 
 MESH = pl.DeviceIdType.MESH
-VMEM_LIMIT = 60 * 1024 * 1024
+VMEM_LIMIT = 62 * 1024 * 1024
 VMEM = pl.BlockSpec(memory_space=pltpu.VMEM)
 ANY = pl.BlockSpec(memory_space=pl.ANY)
+
+
+def upright(row):
+    count = row.shape[1]
+    across = lax.broadcasted_iota(jnp.int32, (count, count), 1)
+    down = lax.broadcasted_iota(jnp.int32, (count, count), 0)
+    return jnp.sum(jnp.where(across == down, row, 0), axis=1, keepdims=True)
+
+
+def same_image(windows):
+    across = lax.broadcasted_iota(jnp.int32, (64, 256), 1) // 4
+    down = lax.broadcasted_iota(jnp.int32, (64, 256), 0)
+    column = upright(windows)
+    of_patch = jnp.sum(jnp.where(across == down, column, 0), axis=0, keepdims=True)
+    return upright(of_patch) == of_patch
+
+
+def local_copy(source, target, sem):
+    copy = pltpu.make_async_copy(source, target, sem)
+    copy.start()
+    return copy
 
 
 class Place:
@@ -116,14 +137,19 @@
 
 
 def merger_kernel(
-    rows_down,
+    rows_across,
     text,
     merged,
+    backs_kept,
+    up_kept,
+    down_kept,
+    sequence,
+    gradient,
     backs,
     up,
     down,
-    sequence,
     cells_back,
+    apart,
     cells,
     pre,
     hidden,
@@ -141,8 +167,15 @@
     *sems,
 ):
     me = Place()
+    load, *sems = sems
     merged_s, share_s, dp_s, terms_s, visual_s, pieces_s, parts_s, mp_s = [
         (sems[2 * i], sems[2 * i + 1]) for i in range(8)
+    ]
+    loads = [
+        local_copy(source, target, load.at[i])
+        for i, (source, target) in enumerate(
+            ((down_kept, down), (backs_kept, backs), (up_kept, up))
+        )
     ]
     sibling, partner = me.at(core=1 - me.core), me.at(high=1 - me.high)
     turn = 1 - me.low
@@ -167,6 +200,8 @@
     cells[me.y] = merged[...]
     own = me.high * 2 + me.core
     hidden_back[...] = jnp.zeros_like(hidden_back)
+    for copy in loads:
+        copy.wait()
 
     @pl.loop(0, 16)
     def _(i):
@@ -275,17 +310,23 @@
         visual[here] = low(total)
 
     visual_copy = go(visual, following, dp_s, 0, before)
+    mp_copies[1].wait_recv()
+    mp_copies[2].wait_recv()
+    for i in range(10):
+        for j in range(4):
+            there = pl.ds(j * 1280 + i * 128, 128)
+            apart[i, pl.ds(j, 64, stride=4), :] = wide(cells_back[:, there])
+        gradient[:, i * 128 : (i + 1) * 128] = apart[i]
     slot = lax.broadcasted_iota(jnp.int32, (256, 64), 1)
+    rows_down = upright(rows_across[...])
     offset = (me.z * 2 + me.low) * 64
-    here_cells = jnp.where(rows_down[...] - offset == slot, 1.0, 0.0).astype(jnp.bfloat16)
-    next_cells = jnp.where(rows_down[...] - offset - 64 == slot, 1.0, 0.0).astype(jnp.bfloat16)
+    here_cells = jnp.where(rows_down - offset == slot, 1.0, 0.0).astype(jnp.bfloat16)
+    next_cells = jnp.where(rows_down - offset - 64 == slot, 1.0, 0.0).astype(jnp.bfloat16)
     visual_copy.wait_recv()
     for i in range(4):
         span = pl.ds(i * STEP, STEP)
         picked = product(here_cells, visual[:, span]) + product(next_cells, following[:, span])
-        sequence[:, span] = jnp.where(rows_down[...] >= 0, low(picked), text[:, span])
-    mp_copies[1].wait_recv()
-    mp_copies[2].wait_recv()
+        sequence[:, span] = jnp.where(rows_down >= 0, low(picked), text[:, span])
     for copy in pending:
         copy.wait_send()
 
@@ -295,6 +336,11 @@
         return pltpu.VMEM(shape, jnp.bfloat16)
 
     scratch = [
+        buffer(*backs.shape),
+        buffer(*up.shape),
+        buffer(*down.shape),
+        buffer(*merged.shape),
+        pltpu.VMEM((10, 256, 128), jnp.float32),
         buffer(4, 64, 5120),
         pltpu.VMEM((256, 320), jnp.float32),
         buffer(256, 320),
@@ -310,22 +356,23 @@
         buffer(4, 2, 16, 5120),
         buffer(8, 16, 5120),
     ]
+    scratch += [pltpu.SemaphoreType.DMA((3,))]
     for size in (4, 4, 1, 2, 8, 1, 8, 3):
         scratch += sem_pair(size)
     return pl.pallas_call(
         merger_kernel,
         out_shape=[
             jax.ShapeDtypeStruct(text.shape, jnp.bfloat16),
-            jax.ShapeDtypeStruct(merged.shape, jnp.bfloat16),
+            jax.ShapeDtypeStruct((256, 1280), jnp.float32),
         ],
-        in_specs=[VMEM] * 6,
+        in_specs=[VMEM] * 3 + [ANY] * 3,
         out_specs=[VMEM] * 2,
         scratch_shapes=scratch,
         compiler_params=pltpu.CompilerParams(
             collective_id=4, has_side_effects=True, vmem_limit_bytes=VMEM_LIMIT
         ),
         name="merger",
-    )(cell_rows[:, None], text, merged, backs, up, down)
+    )(cell_rows, text, merged, backs, up, down)
 
 
 CHUNKS = 4
@@ -395,13 +442,15 @@
 
 
 def forward_kernel(*refs):
-    block_input, across, downwards, gains, merge_gain, rows_across, cotangent = refs[:7]
-    shards = refs[7:11]
-    wholes = refs[11:15]
-    attend, projected, heads_out, middle, feed, gate, upper, activated, block_out, merged = refs[15:25]
-    backs, spill, spill_in = refs[25:28]
-    sum_one, sum_two = refs[28:33], refs[33:38]
-    own, *pairs = refs[38:]
+    block_input, windows, gains, merge_gain, rows_across, cotangent = refs[:6]
+    shards = refs[6:10]
+    kept = refs[10:14]
+    attend, projected, heads_out, middle, feed, gate, upper, activated, block_out, merged = refs[14:24]
+    backs = refs[24]
+    wholes = refs[25:29]
+    spill, spill_in, merged_wide = refs[29:32]
+    sum_one, sum_two = refs[32:37], refs[37:42]
+    own, keep, *pairs = refs[42:]
     y_s, z_s, x_s, one_s, two_s, dp_s, back_s, fore_s = [
         (pairs[2 * i], pairs[2 * i + 1]) for i in range(8)
     ]
@@ -458,9 +507,14 @@
             copies.append(first[u, k, 2])
         second[u] = copies
 
+    keeps = []
+
     def complete(u):
+        t, p, n = UNITS[u]
         for copy in second[u]:
             copy.wait_recv()
+        planes = pl.ds(p, n)
+        keeps.append(local_copy(wholes[t].at[planes], kept[t].at[planes], keep.at[u]))
 
     def whole(t, p):
         return wholes[t][p].reshape(1280, -1)
@@ -468,9 +522,7 @@
     begin(0)
     begin(1)
     for t in range(4):
-        copy = pltpu.make_async_copy(shards[t], wholes[t].at[:, me.y], own.at[t])
-        copy.start()
-        local_copies.append(copy)
+        local_copies.append(local_copy(shards[t], wholes[t].at[:, me.y], own.at[t]))
     slot = lax.broadcasted_iota(jnp.int32, (128, 256), 0)
     offset = (me.z * 2 + me.low) * 64
     taken = jnp.where(rows_across[...] - offset == slot, 1.0, 0.0).astype(jnp.bfloat16)
@@ -487,14 +539,14 @@
     begin(2)
     forward(1)
     begin(3)
-    complete(0)
     for copy in local_copies:
         copy.wait()
+    complete(0)
     for p in range(3):
         projected[p] = low(product(attend[...], whole(0, p)))
     forward(2)
     begin(4)
-    allowed = downwards[...] == across[...]
+    allowed = same_image(windows[...])
     mixed = jnp.zeros((256, 320), jnp.float32)
     for head in range(4):
         mask = head_mask(head)
@@ -530,14 +582,22 @@
         fore_copies.append(go(region, region, fore_s, j * 4 + k, sibling))
     total.end()
     block_out[...] = middle[...] + wide(sum_two[4][...])
-    merged[...] = low(block_out[...] * root_scale(block_out[...]) * merge_gain[...])
+    scale_three = root_scale(block_out[...])
+    for i in range(10):
+        span = slice(i * 128, (i + 1) * 128)
+        merged_wide[i] = block_out[:, span] * scale_three * merge_gain[:, span]
+        for j in range(4):
+            there = pl.ds(j * 1280 + i * 128, 128)
+            merged[:, there] = low(merged_wide[i, pl.ds(j, 64, stride=4), :])
     for copy in fore_copies:
         copy.wait_recv()
+    for copy in keeps:
+        copy.wait()
     for copy in pending:
         copy.wait_send()
 
 
-def block_forward(block_input, patch_windows, gains, merge_gain, cell_rows, cotangent, shards):
+def block_forward(block_input, windows, gains, merge_gain, cell_rows, cotangent, shards):
     rows, width = block_input.shape
     units = shards[2].shape[2]
 
@@ -555,18 +615,21 @@
         shape(wide_, rows, units),
         shape(low_, rows, units),
         shape(wide_, rows, width),
-        shape(low_, rows, width),
+        shape(low_, rows // 4, 4 * width),
         shape(low_, 4, 4, 64, cotangent.shape[1]),
     ]
     spill = pltpu.VMEM((64, cotangent.shape[1]), jnp.bfloat16)
-    scratch = [spill, spill] + sum_buffers() + sum_buffers() + [pltpu.SemaphoreType.DMA((4,))]
+    scratch = [pltpu.VMEM(out.shape, jnp.bfloat16) for out in outs[:4]]
+    scratch += [spill, spill, pltpu.VMEM((10, rows, 128), jnp.float32)]
+    scratch += sum_buffers() + sum_buffers()
+    scratch += [pltpu.SemaphoreType.DMA((4,)), pltpu.SemaphoreType.DMA((len(UNITS),))]
     for size in (45, 45, 15, 3 * CHUNKS, 3 * CHUNKS, 1, 8, 8):
         scratch += sem_pair(size)
     results = pl.pallas_call(
         forward_kernel,
         out_shape=outs,
-        in_specs=[VMEM] * 11,
-        out_specs=[VMEM] * len(outs),
+        in_specs=[VMEM] * 10,
+        out_specs=[ANY] * 4 + [VMEM] * (len(outs) - 4),
         scratch_shapes=scratch,
         compiler_params=pltpu.CompilerParams(
             collective_id=1, has_side_effects=True, vmem_limit_bytes=VMEM_LIMIT
@@ -574,11 +637,10 @@
         name="block_forward",
     )(
         block_input,
-        patch_windows[None],
-        patch_windows[:, None],
+        windows,
         gains,
         merge_gain[None],
-        cell_rows[None],
+        cell_rows,
         cotangent,
         *shards,
     )
@@ -589,6 +651,8 @@
 A_PART = A_ROWS // 4
 B_PART = (320 - A_ROWS) // 4
 E_ROWS = A_PART + B_PART
+A_HALF, B_HALF = A_ROWS // 2, B_PART // 2
+E_TOP = 48
 TILE = 16
 ORDER = (1, 3, 2)
 
@@ -602,35 +666,79 @@
 
 
 class Reduction:
-    def __init__(self, me, go, term, out, buffers, sems, index, y_at, z_at, side):
-        self.me, self.go, self.term, self.out = me, go, term, out
-        self.ya, self.sa, self.za, self.zb, self.sb, self.yb, self.ee, self.ex = buffers
+    def __init__(self, me, go, term, final, buffers, sems, index, y_at, z_at, side):
+        self.me, self.go, self.term, self.final = me, go, term, final
+        self.ya, self.fy, self.sa, self.za, self.zb, self.fz, self.sb, self.yb, self.ee, self.ex = buffers
         self.sems, self.index, self.y_at, self.z_at, self.side = sems, index, y_at, z_at, side
         self.planes = term.shape[0]
+        self.relayed = index >= 2
 
     def stage_one(self):
-        me = self.me
+        me, term, go, ya, zb = self.me, self.term, self.go, self.ya, self.zb
+        top, bottom = pl.ds(0, A_HALF), pl.ds(A_HALF, A_HALF)
+        at = self.index * 6
+
+        def a_rows(k, span):
+            return term.at[:, me.along_y(k), span]
+
+        def b_rows(k, half):
+            first = A_ROWS + me.along_z(k) * B_PART + half * B_HALF
+            return term.at[:, :, pl.ds(pl.multiple_of(first, TILE), B_HALF)]
+
+        up, down = self.y_at[1], self.y_at[3]
+        sems = self.sems[0]
+        self.far_a = [
+            go(a_rows(2, top), self.fy.at[0], sems, at, up),
+            go(a_rows(2, bottom), self.fy.at[1], sems, at + 1, down),
+        ]
+        up_z, down_z = self.z_at[1], self.z_at[3]
+        sems_z = self.sems[1]
+        self.far_b = [
+            go(b_rows(2, 0), self.fz.at[0], sems_z, at, up_z),
+            go(b_rows(2, 1), self.fz.at[1], sems_z, at + 1, down_z),
+        ]
         self.first_a = [
-            self.go(
-                self.term.at[:, me.along_y(k), pl.ds(0, A_ROWS)],
-                self.ya.at[k - 1],
-                self.sems[0],
-                self.index * 3 + k - 1,
-                self.y_at[k],
-            )
-            for k in ORDER
+            go(a_rows(1, bottom), ya.at[0, :, bottom], sems, at + 2, up),
+            go(a_rows(3, top), ya.at[1, :, top], sems, at + 3, down),
         ]
+        b_top, b_bottom = pl.ds(0, B_HALF), pl.ds(B_HALF, B_HALF)
         self.first_b = [
-            self.go(
-                self.term.at[
-                    :, :, pl.ds(pl.multiple_of(A_ROWS + me.along_z(k) * B_PART, TILE), B_PART)
-                ],
-                self.zb.at[k - 1],
-                self.sems[1],
-                self.index * 3 + k - 1,
-                self.z_at[k],
-            )
-            for k in ORDER
+            go(b_rows(1, 1), zb.at[0, :, :, b_bottom], sems_z, at + 2, up_z),
+            go(b_rows(3, 0), zb.at[1, :, :, b_top], sems_z, at + 3, down_z),
+        ]
+
+    def stage_half(self):
+        me, term, go, fy, fz = self.me, self.term, self.go, self.fy, self.fz
+        at = self.index * 6
+        for copy in self.far_b + self.far_a:
+            copy.wait_recv()
+
+        def add_b(i, r):
+            p, q = i // 4, i % 4
+            here = pl.ds(r, TILE)
+            first = pl.multiple_of(A_ROWS + me.along_z(1) * B_PART + r, TILE)
+            fz[0, p, q, here] = low(wide(fz[0, p, q, here]) + wide(term[p, q, pl.ds(first, TILE)]))
+            first = pl.multiple_of(A_ROWS + me.along_z(3) * B_PART + B_HALF + r, TILE)
+            fz[1, p, q, here] = low(wide(fz[1, p, q, here]) + wide(term[p, q, pl.ds(first, TILE)]))
+
+        def add_a(p, r):
+            here = pl.ds(r, TILE)
+            there = pl.ds(pl.multiple_of(A_HALF + r, TILE), TILE)
+            fy[0, p, here] = low(wide(fy[0, p, here]) + wide(term[p, me.along_y(1), here]))
+            fy[1, p, here] = low(wide(fy[1, p, here]) + wide(term[p, me.along_y(3), there]))
+
+        over_rows(self.planes * 4, B_HALF, add_b)
+        over_rows(self.planes, A_HALF, add_a)
+        top, bottom = pl.ds(0, A_HALF), pl.ds(A_HALF, A_HALF)
+        b_top, b_bottom = pl.ds(0, B_HALF), pl.ds(B_HALF, B_HALF)
+        ya, zb = self.ya, self.zb
+        self.first_b += [
+            go(fz.at[0], zb.at[0, :, :, b_top], self.sems[1], at + 4, self.z_at[1]),
+            go(fz.at[1], zb.at[1, :, :, b_bottom], self.sems[1], at + 5, self.z_at[3]),
+        ]
+        self.first_a += [
+            go(fy.at[0], ya.at[0, :, top], self.sems[0], at + 4, self.y_at[1]),
+            go(fy.at[1], ya.at[1, :, bottom], self.sems[0], at + 5, self.y_at[3]),
         ]
 
     def stage_two(self):
@@ -643,10 +751,7 @@
             here = pl.ds(r, TILE)
             there = pl.ds(pl.multiple_of(A_ROWS + me.z * B_PART + r, TILE), TILE)
             sb[p, q, here] = low(
-                wide(term[p, q, there])
-                + wide(zb[0, p, q, here])
-                + wide(zb[1, p, q, here])
-                + wide(zb[2, p, q, here])
+                wide(term[p, q, there]) + wide(zb[0, p, q, here]) + wide(zb[1, p, q, here])
             )
 
         over_rows(self.planes * 4, B_PART, add_b)
@@ -666,10 +771,7 @@
         def add_a(p, r):
             here = pl.ds(r, TILE)
             sa[p, here] = low(
-                wide(term[p, me.y, here])
-                + wide(ya[0, p, here])
-                + wide(ya[1, p, here])
-                + wide(ya[2, p, here])
+                wide(term[p, me.y, here]) + wide(ya[0, p, here]) + wide(ya[1, p, here])
             )
 
         over_rows(self.planes, A_ROWS, add_a)
@@ -710,25 +812,63 @@
         over_rows(self.planes, B_PART, add_b)
         self.third = self.go(ee, self.ex, self.sems[4], self.index, self.side)
 
+    def owned(self, source):
+        return source % 2, (source // 2) * (A_ROWS // 2)
+
     def stage_four(self):
-        me, out, ee, ex = self.me, self.out, self.ee, self.ex
+        me, ya, ee, ex = self.me, self.ya, self.ee, self.ex
         self.third.wait_recv()
+        slot, base = self.owned(me.z)
 
         def add(p, r):
+            there = pl.ds(pl.multiple_of(base + r, TILE), TILE)
             here = pl.ds(r, TILE)
-            out[me.z, p, here] = low(wide(ee[p, here]) + wide(ex[p, here]))
+            ya[slot, p, there] = low(wide(ee[p, here]) + wide(ex[p, here]))
 
         over_rows(self.planes, E_ROWS, add)
-        self.fourth = [
-            self.go(
-                out.at[me.z], out.at[me.z], self.sems[5], self.index * 3 + k - 1, self.z_at[k]
-            )
-            for k in ORDER
-        ]
+        mine = self.piece(0, 0, E_ROWS)
+        at = self.index * 4
+        near = (1, 3) if self.relayed else ORDER
+        self.fourth = {k: self.go(mine, mine, self.sems[5], at + k - 1, self.z_at[k]) for k in near}
+
+    def piece(self, k, start, rows):
+        slot, base = self.owned(self.me.along_z(k))
+        return self.ya.at[slot, :, pl.ds(pl.multiple_of(base + start, TILE), rows)]
+
+    def relay(self):
+        if not self.relayed:
+            return
+        at = self.index * 4
+        self.fourth[1].wait_recv()
+        piece = self.piece(3, 0, E_TOP)
+        self.fourth[2] = self.go(piece, piece, self.sems[5], at + 1, self.z_at[1])
+        self.fourth[3].wait_recv()
+        piece = self.piece(1, E_TOP, E_ROWS - E_TOP)
+        self.fourth[4] = self.go(piece, piece, self.sems[5], at + 3, self.z_at[3])
 
     def finish(self):
-        for copy in self.fourth:
-            copy.wait_recv()
+        me, ya, final = self.me, self.ya, self.final
+        for k in (0,) + ORDER:
+            if k == 2 and self.relayed:
+                self.fourth[2].wait_recv()
+                self.fourth[4].wait_recv()
+            elif k and not self.relayed:
+                self.fourth[k].wait_recv()
+            source = me.along_z((4 - k) % 4)
+            slot, base = self.owned(source)
+
+            def put_a(p, r):
+                there = pl.ds(pl.multiple_of(source * A_PART + r, TILE), TILE)
+                here = pl.ds(pl.multiple_of(base + r, TILE), TILE)
+                final[p, there] = wide(ya[slot, p, here])
+
+            def put_b(p, r):
+                there = pl.ds(pl.multiple_of(A_ROWS + source * B_PART + r, TILE), TILE)
+                here = pl.ds(pl.multiple_of(base + A_PART + r, TILE), TILE)
+                final[p, there] = wide(ya[slot, p, here])
+
+            over_rows(self.planes, A_PART, put_a)
+            over_rows(self.planes, B_PART, put_b)
 
 
 def first_with_first(left, right):
@@ -740,15 +880,14 @@
 def backward_kernel(*refs):
     (
         block_input,
-        across,
-        downwards,
+        windows,
         gains,
         merge_gain,
         cells_back,
-        triple,
-        output,
-        gate_up,
-        down,
+        triple_kept,
+        output_kept,
+        gate_up_kept,
+        down_kept,
         attend,
         projected,
         heads_out,
@@ -758,17 +897,25 @@
         upper,
         activated,
         block_out,
-    ) = refs[:19]
-    input_gradient = refs[19]
-    outs = refs[20:25]
-    gain_out = refs[25]
-    refs = refs[26:]
+    ) = refs[:18]
+    input_gradient = refs[18]
+    outs = refs[19:24]
+    gain_out = refs[24]
+    refs = refs[25:]
+    triple, output, gate_up, down, load = refs[:5]
+    refs = refs[5:]
     sum_one, sum_two = refs[:5], refs[5:10]
     terms = refs[10:15]
-    buffers = [refs[15 + 8 * t : 23 + 8 * t] for t in range(5)]
-    middle_back, middle_low, out_low, gate_up_back, triple_back, gain, gain_in, gain_sum = refs[55:63]
-    sems = refs[63:]
+    buffers = [refs[15 + 10 * t : 25 + 10 * t] for t in range(5)]
+    middle_back, middle_low, out_low, gate_up_back, triple_back, gain, gain_in, gain_sum = refs[65:73]
+    sems = refs[73:]
     pair = [(sems[2 * i], sems[2 * i + 1]) for i in range(9)]
+    loads = [
+        local_copy(source, target, load.at[i])
+        for i, (source, target) in enumerate(
+            ((down_kept, down), (gate_up_kept, gate_up), (output_kept, output), (triple_kept, triple))
+        )
+    ]
     me = Place()
     y_at = {k: me.at(y=me.along_y(k)) for k in ORDER}
     z_at = {k: me.at(z=me.along_z(k)) for k in ORDER}
@@ -800,11 +947,13 @@
         return weight[p].reshape(1280, -1)
 
     scale_three = root_scale(block_out[...])
-    out_back = norm_backward(wide(cells_back[...]), block_out[...], scale_three, merge_gain[...])
+    out_back = norm_backward(cells_back[...], block_out[...], scale_three, merge_gain[...])
     middle_back[...] = out_back
     out_low[...] = low(out_back)
     form(4, 0, out_low, activated[...])
     of_down.stage_one()
+    for copy in loads:
+        copy.wait()
     activated_back = product(out_low[...], whole(down, 0))
     slope = jax.nn.sigmoid(gate[...])
     gate_up_back[1] = low(activated_back * gate[...] * slope)
@@ -816,6 +965,7 @@
     )
     form(2, 0, feed, gate_up_back[0])
     of_gate.stage_one()
+    of_down.stage_half()
     total.end()
     feed_back = wide(sum_one[4][...])
     scale_two = root_scale(middle[...])
@@ -827,11 +977,9 @@
     gain[1:2] = jnp.sum(feed_back * middle[...] * scale_two, axis=0, keepdims=True)
     form(3, 0, feed, gate_up_back[1])
     of_upper.stage_one()
+    of_gate.stage_half()
     heads_back = low(product(middle_low[...], whole(output, 0)))
-    of_down.stage_two()
-    form(1, 0, middle_low, heads_out[...])
-    of_output.stage_one()
-    allowed = downwards[...] == across[...]
+    allowed = same_image(windows[...])
     query_back = jnp.zeros((256, 320), jnp.float32)
     key_back = jnp.zeros((256, 320), jnp.float32)
     value_back = jnp.zeros((256, 320), jnp.float32)
@@ -847,17 +995,21 @@
     triple_back[0] = low(query_back)
     triple_back[1] = low(key_back)
     triple_back[2] = low(value_back)
-    of_gate.stage_two()
+    for p in range(3):
+        form(0, p, attend, triple_back[p])
+    of_triple.stage_one()
+    form(1, 0, middle_low, heads_out[...])
+    of_output.stage_one()
+    of_upper.stage_half()
+    of_down.stage_two()
     total = SumOverMp(me, go, sum_two, pair[7])
     total.begin(
         lambda rows: last_with_last(triple_back[0, rows], whole(triple, 0))
         + last_with_last(triple_back[1, rows], whole(triple, 1))
         + last_with_last(triple_back[2, rows], whole(triple, 2))
     )
-    for p in range(3):
-        form(0, p, attend, triple_back[p])
-    of_triple.stage_one()
-    of_down.stage_three()
+    of_triple.stage_half()
+    of_gate.stage_two()
     total.end()
     attend_back = wide(sum_two[4][...])
     start = wide(block_input[...])
@@ -865,10 +1017,11 @@
     input_gradient[...] = middle_back[...] + norm_backward(attend_back, start, scale_one, gains[0:1])
     gain[0:1] = jnp.sum(attend_back * start * scale_one, axis=0, keepdims=True)
     gain_copies = [go(gain, gain_in.at[k - 1], pair[8], k - 1, y_at[k]) for k in ORDER]
+    of_down.stage_three()
+    of_output.stage_half()
     of_upper.stage_two()
     of_gate.stage_three()
     of_down.stage_four()
-    of_output.stage_two()
     for copy in gain_copies:
         copy.wait_recv()
     gain_sum[0] = gain[...] + gain_in[0] + gain_in[1] + gain_in[2]
@@ -876,25 +1029,29 @@
     of_triple.stage_two()
     of_upper.stage_three()
     of_gate.stage_four()
+    of_down.relay()
+    of_output.stage_two()
     for copy in gain_copies:
         copy.wait_recv()
     gain_sum[1] = gain_sum[0] + gain_in[3] + gain_in[4] + gain_in[5]
     gain_copies = [go(gain_sum.at[1], gain_in.at[6], pair[8], 6, side)]
-    of_output.stage_three()
     of_triple.stage_three()
     of_upper.stage_four()
+    of_gate.relay()
+    of_output.stage_three()
     for copy in gain_copies:
         copy.wait_recv()
     gain_out[...] = gain_sum[1] + gain_in[6]
+    of_triple.stage_four()
+    of_upper.relay()
     of_output.stage_four()
-    of_triple.stage_four()
-    for reduction in reductions:
+    for reduction in (of_down, of_gate, of_upper, of_triple, of_output):
         reduction.finish()
     for copy in pending:
         copy.wait_send()
 
 
-def block_backward(block_input, patch_windows, gains, merge_gain, cells_back, wholes, saved):
+def block_backward(block_input, windows, gains, merge_gain, cells_back, wholes, saved):
     rows, width = block_input.shape
     units = saved[5].shape[1]
 
@@ -905,14 +1062,18 @@
         return pltpu.VMEM(shape, jnp.float32)
 
     sizes = ((3, 320), (1, 320), (1, units), (1, units), (1, units))
-    scratch = sum_buffers() + sum_buffers()
+    scratch = [low_buffer(*whole.shape) for whole in wholes]
+    scratch += [pltpu.SemaphoreType.DMA((4,))]
+    scratch += sum_buffers() + sum_buffers()
     scratch += [low_buffer(planes, 4, 320, columns) for planes, columns in sizes]
     for planes, columns in sizes:
         scratch += [
-            low_buffer(3, planes, A_ROWS, columns),
+            low_buffer(2, planes, A_ROWS, columns),
+            low_buffer(2, planes, A_HALF, columns),
             low_buffer(planes, A_ROWS, columns),
             low_buffer(3, planes, A_PART, columns),
-            low_buffer(3, planes, 4, B_PART, columns),
+            low_buffer(2, planes, 4, B_PART, columns),
+            low_buffer(2, planes, 4, B_HALF, columns),
             low_buffer(planes, 4, B_PART, columns),
             low_buffer(3, planes, B_PART, columns),
             low_buffer(planes, E_ROWS, columns),
@@ -928,12 +1089,11 @@
         wide_buffer(7, 8, width),
         wide_buffer(2, 8, width),
     ]
-    for size in (15, 15, 15, 15, 5, 15, 3 * CHUNKS, 3 * CHUNKS, 7):
+    for size in (30, 30, 15, 15, 5, 20, 3 * CHUNKS, 3 * CHUNKS, 7):
         scratch += sem_pair(size)
     operands = [
         block_input,
-        patch_windows[None],
-        patch_windows[:, None],
+        windows,
         gains,
         merge_gain[None],
         cells_back,
@@ -943,15 +1103,14 @@
     outs = (
         [jax.ShapeDtypeStruct((rows, width), jnp.float32)]
         + [
-            jax.ShapeDtypeStruct((4, planes, E_ROWS, columns), jnp.bfloat16)
-            for planes, columns in sizes
+            jax.ShapeDtypeStruct((planes, 320, columns), jnp.float32) for planes, columns in sizes
         ]
         + [jax.ShapeDtypeStruct((8, width), jnp.float32)]
     )
     results = pl.pallas_call(
         backward_kernel,
         out_shape=outs,
-        in_specs=[VMEM] * len(operands),
+        in_specs=[VMEM] * 5 + [ANY] * 4 + [VMEM] * (len(operands) - 9),
         out_specs=[VMEM] * len(outs),
         scratch_shapes=scratch,
         compiler_params=pltpu.CompilerParams(
@@ -960,20 +1119,7 @@
         name="block_backward",
     )(*operands)
 
-    def assembled(owned):
-        planes, columns = owned.shape[1], owned.shape[3]
-        owned = jnp.transpose(owned, (1, 0, 2, 3))
-        return wide(
-            jnp.concatenate(
-                [
-                    owned[:, :, :A_PART].reshape(planes, -1, columns),
-                    owned[:, :, A_PART:].reshape(planes, -1, columns),
-                ],
-                axis=1,
-            )
-        )
-
-    gradients = [assembled(owned) for owned in results[1:6]]
+    gradients = results[1:6]
     return results[0], gradients, results[6][:2]
 
 
@@ -997,8 +1143,6 @@
     merge_down,
 ):
     patches = block_input[0]
-    rows, width = patches.shape
-    patch_windows = jnp.repeat(windows[0], 4)
     shards = (
         planes_of(triple_weight),
         output_weight[None],
@@ -1007,27 +1151,27 @@
     )
     wholes, saved, backs = block_forward(
         patches,
-        patch_windows,
+        windows,
         norm_gains,
         merge_gain,
-        cell_rows[0],
+        cell_rows,
         sequence_cotangent[0],
         shards,
     )
     sequence, cells_back = merger(
-        cell_rows[0],
+        cell_rows,
         text_vectors[0],
-        saved[-1].reshape(rows // 4, 4 * width),
+        saved[-1],
         backs,
         merge_up.T,
         merge_down,
     )
     input_gradient, gradients, gain_gradient = block_backward(
         patches,
-        patch_windows,
+        windows,
         norm_gains,
         merge_gain,
-        cells_back.reshape(rows, width),
+        cells_back,
         wholes,
         saved[:-1],
     )

time: 355 us -> 313 us (0.88)
  Pallas kernels: 317 us -> 295 us
  other arithmetic: 12 us -> 1.75 us
  local copies, waits for them, and re-layouts: 22.6 us -> 14.3 us
    pallas_call x2, Pallas kernels: 231 us -> 211 us  [the longest x1 108 us: block_backward(): pl.pallas_call(backward_kernel, out_shape=outs, in_specs=[VMEM] * 5 + [AN...]
    another operation x1, other arithmetic: 8.93 us -> 1.75 us  [local(): jnp.stack([gradients[2][0], gradients[3][0]], axis=1)]
    unnamed x13 -> x17, local copies, waits for them, and re-layouts: 5.66 us -> 11.5 us
    reshape x2 -> x0, local copies, waits for them, and re-layouts: 4.68 us -> none  [the longest x1 2.43 us: local(): cells_back.reshape(rows, width)]
    slice x12 -> x0, local copies, waits for them, and re-layouts: 4.12 us -> none  [the longest x6 2.15 us: assembled(): owned[:, :, :A_PART].reshape(planes, -1, columns)]
where the time goes in v4:
time: 313 us; the launch traced here: 312 us
  Pallas kernels  295 us (94%)
  local copies, waits for them, and re-layouts  14.3 us (5%)
    pallas_call x1, Pallas kernels, block_backward(): pl.pallas_call(backward_kernel, out_shape=outs, in_specs=[VMEM] * 5 + [AN...  108 us
    pallas_call x1, Pallas kernels, block_forward(): pl.pallas_call(forward_kernel, out_shape=outs, in_specs=[VMEM] * 10, out_...  104 us
    pallas_call x1, Pallas kernels, merger(): pl.pallas_call(merger_kernel, out_shape=[jax.ShapeDtypeStruct(text.shape,...  83.5 us
    unnamed x17, local copies, waits for them, and re-layouts  11.5 us

profile of v4, /device:TPU:0, one launch (start us, length us, event | category | flops | bytes accessed | tf_op | source)
XLA Modules:
  0.0 311.5 jit_solution(13042394099879058947)
XLA Ops:
  0.6 1.3 broadcast_in_dim.16.refs_3_
  1.9 2.4 copy.23
  4.3 103.6 %block_forward.1 = (bf16[3,4,320,320]{3,2,1,0:T(8,128)(2,1)}, bf16[1,4,320,320]{3,2,1,0:T(8,128)(2,1)}, bf16[2,4,320,855]{3,2,1,0:T(8,128)(2,1)}, bf16[1,4,320,8...) custom-call(bf16[256,1280]{1,0:T(8,128)(2,1)} %bitcast.19, ...), custom_call_target="tpu_custom_call" | custom-call | tf_op jit(solution)/shard_map/block_forward/pallas_call | solution.py:628
  107.9 83.5 %merger.1 = (bf16[256,2048]{1,0:T(8,128)(2,1)}, f32[256,1280]{1,0:T(8,128)}) custom-call(s32[1,256]{1,0:T(1,128)} %rows_across.1, bf16[256,2048]{1,0:T(8,128)(2,1)} %bitcast.26, bf16[64,5120]{1,0:T(8,128)(2,1)} %get-tuple-element.31.merged, bf16[4,4,64,2048]{3,2,1,0:T(8,128)(2,1)} %get-tuple-element.32.backs_kept, bf16[320,5120]{1,0:T(8,128)(2,1)} %bitcast.18, ...), custom_call_target="tpu_custom_call" | custom-call | tf_op jit(solution)/shard_map/merger/pallas_call | solution.py:362
  191.4 107.8 %block_backward.1 = (f32[256,1280]{1,0:T(8,128)}, f32[3,320,320]{2,1,0:T(8,128)}, f32[1,320,320]{2,1,0:T(8,128)}, f32[1,320,855]{2,1,0:T(8,128)}, f32[1,320,855]...) custom-call(bf16[256,1280]{1,0:T(8,128)(2,1)} %bitcast.20, s32[1,64]{1,0:T(1,128)} %refs_1_.3, ...), custom_call_target="tpu_custom_call" | custom-call | tf_op jit(solution)/shard_map/block_backward/pallas_call | solution.py:1110
  299.2 1.8 pad_maximum_fusion
  300.9 0.0 copy-start.3
  300.9 3.2 %copy.21 = f32[320,2,855]{2,1,0:T(2,128)} copy(f32[320,2,855]{2,0,1:T(8,128)S(1)} %pad_maximum_fusion) | data formatting | bytes 4377600
  304.1 0.0 copy-start.1
  304.1 1.5 slice.3
  305.6 0.0 copy-done.3
  305.6 1.0 copy.29
  306.6 0.0 copy-done.1
  306.6 0.0 copy-start
  306.6 1.1 copy.30
  307.6 0.8 copy-done
  308.4 0.0 copy-start.4
  308.4 0.0 copy-start.2
  308.4 1.1 copy.31
  309.5 0.2 copy-done.4
  309.7 0.8 copy.32
  310.5 0.0 copy-done.2
  310.5 1.0 copy.33
Async XLA Ops:
  300.9 4.7 %copy-start.3 = (bf16[256,2048]{1,0:T(8,128)(2,1)S(1)}, bf16[256,2048]{1,0:T(8,128)(2,1)}, u32[]{:S(2)}) copy-start(bf16[256,2048]{1,0:T(8,128)(2,1)} %get-tuple-element.33) | copy-start | bytes 3145732
  304.1 2.5 copy-start.1
  306.6 1.8 copy-start
  308.4 1.3 copy-start.4
  308.4 2.1 copy-start.2

commit v5 on v4

--- a/solution.py
+++ b/solution.py
@@ -124,6 +124,8 @@
 QUARTER, HALF = 48, 48
 ALONE = 320 - 4 * QUARTER - 2 * HALF
 UNITS = ((0, 0, 3), (1, 0, 1), (2, 0, 1), (2, 1, 1), (3, 0, 1))
+SHARE_Z = ({1: (0, 16), 3: (16, 32)}, {1: (0, 32), 3: (32, 16)})
+SHARE = ({1: (0, 32), 3: (32, 16)}, {1: (0, 16), 3: (16, 32)}, {1: (0, 16), 3: (16, 16)})
 PAIRS = [(j, k) for k in (1, 3, 2) for j in (0, 1)] + [(1, 0)]
 
 
@@ -462,10 +464,9 @@
     after = me.at(z=(me.z + me.low) % 4, low=1 - me.low)
     far = me.at(z=(me.z + 3 + 2 * me.low) % 4, low=1 - me.low)
 
-    def peer(j, k):
-        return me.at(y=me.along_y(k), high=(me.high + j) % 2)
-
-    greet([peer(j, k) for j, k in PAIRS] + [z_at[k] for k in others] + [side, far, sibling])
+    greet(
+        [y_at[1], y_at[3], z_at[1], z_at[3], side, far, sibling, me.at(high=1 - me.high)]
+    )
     pending = []
 
     def go(*arguments):
@@ -473,46 +474,71 @@
         pending.append(copy)
         return copy
 
-    spans = (
-        pl.ds(pl.multiple_of(me.z * QUARTER, 16), QUARTER),
-        pl.ds(pl.multiple_of(4 * QUARTER + me.low * HALF, 16), HALF),
-        pl.ds(320 - ALONE, ALONE),
-    )
-    local_copies, first, second = [], {}, {}
+    starts = (me.z * QUARTER, 4 * QUARTER + me.low * HALF, 320 - ALONE)
+    sizes = (QUARTER, HALF, ALONE)
+    local_copies, near, far_copies, along, onwards, relays = [], {}, {}, {}, {}, {}
+
+    def rows_of(u, source, start, size):
+        t, p, n = UNITS[u]
+        return wholes[t].at[pl.ds(p, n), source, pl.ds(pl.multiple_of(start, 16), size)]
 
     def begin(u):
         t, p, n = UNITS[u]
-        for k in others:
+        for d in (1, 3):
             for part in range(3):
-                first[u, k, part] = go(
-                    shards[t].at[pl.ds(p, n), spans[part]],
-                    wholes[t].at[pl.ds(p, n), me.y, spans[part]],
+                span = pl.ds(pl.multiple_of(starts[part], 16), sizes[part])
+                near[u, d, part] = go(
+                    shards[t].at[pl.ds(p, n), span],
+                    wholes[t].at[pl.ds(p, n), me.y, span],
                     y_s,
-                    (u * 3 + k - 1) * 3 + part,
-                    y_at[k],
+                    u * 12 + (d // 2) * 3 + part,
+                    y_at[d],
                 )
 
-    def forward(u):
-        t, p, n = UNITS[u]
-        copies = []
-        for k in others:
-            source = me.along_y(4 - k)
-            first[u, k, 0].wait_recv()
-            block = wholes[t].at[pl.ds(p, n), source, spans[0]]
-            for j in others:
-                copies.append(go(block, block, z_s, (u * 3 + k - 1) * 3 + j - 1, z_at[j]))
-            first[u, k, 1].wait_recv()
-            block = wholes[t].at[pl.ds(p, n), source, spans[1]]
-            copies.append(go(block, block, x_s, u * 3 + k - 1, side))
-            copies.append(first[u, k, 2])
-        second[u] = copies
+    def onward(u, k):
+        source = me.along_y(k)
+        block = rows_of(u, source, starts[0], sizes[0])
+        for e in (1, 3):
+            along[u, k, e] = go(block, block, z_s, u * 12 + (k - 1) * 2 + e // 2, z_at[e])
+        block = rows_of(u, source, starts[1], sizes[1])
+        onwards[u, k] = go(block, block, x_s, u * 3 + k - 1, side)
+
+    def relay_y(u):
+        for d in (1, 3):
+            for part in range(3):
+                near[u, d, part].wait_recv()
+                first, size = SHARE[part][d]
+                block = rows_of(u, me.along_y(4 - d), starts[part] + first, size)
+                far_copies[u, d, part] = go(
+                    block, block, y_s, u * 12 + 6 + (d // 2) * 3 + part, y_at[d]
+                )
+        onward(u, 3)
+        onward(u, 1)
+
+    def distant(u):
+        for d in (1, 3):
+            for part in range(3):
+                far_copies[u, d, part].wait_recv()
+        onward(u, 2)
+
+    def relay_z(u):
+        for k in (3, 1, 2):
+            for e in (1, 3):
+                along[u, k, e].wait_recv()
+                first, size = SHARE_Z[k % 2][e]
+                block = rows_of(u, me.along_y(k), me.along_z(4 - e) * QUARTER + first, size)
+                relays[u, k, e] = go(
+                    block, block, z_s, u * 12 + 6 + (k - 1) * 2 + e // 2, z_at[e]
+                )
 
     keeps = []
 
     def complete(u):
         t, p, n = UNITS[u]
-        for copy in second[u]:
-            copy.wait_recv()
+        for k in (3, 1, 2):
+            onwards[u, k].wait_recv()
+            relays[u, k, 1].wait_recv()
+            relays[u, k, 3].wait_recv()
         planes = pl.ds(p, n)
         keeps.append(local_copy(wholes[t].at[planes], kept[t].at[planes], keep.at[u]))
 
@@ -535,17 +561,28 @@
     spill_copy = go(spill, spill_in, dp_s, 0, after)
     start = wide(block_input[...])
     attend[...] = low(start * root_scale(start) * gains[0:1])
-    forward(0)
+    relay_y(0)
     begin(2)
-    forward(1)
+    distant(0)
+    relay_y(1)
+    distant(1)
     begin(3)
+    relay_z(0)
+    spill_copy.wait_recv()
+    for i in range(4):
+        span = pl.ds(i * STEP, STEP)
+        backs[me.y, column, :, span] = backs[me.y, column, :, span] + spill_in[:, span]
+    block = backs.at[me.y, column]
+    across = go(block, block, back_s, 0, me.at(high=1 - me.high))
+    relay_z(1)
     for copy in local_copies:
         copy.wait()
     complete(0)
     for p in range(3):
         projected[p] = low(product(attend[...], whole(0, p)))
-    forward(2)
+    relay_y(2)
     begin(4)
+    distant(2)
     allowed = same_image(windows[...])
     mixed = jnp.zeros((256, 320), jnp.float32)
     for head in range(4):
@@ -554,38 +591,52 @@
         mixed = mixed + product(low(shares), projected[2] * mask)
     heads_out[...] = low(mixed)
     complete(1)
-    forward(3)
+    relay_y(3)
+    distant(3)
+    relay_z(2)
     total = SumOverMp(me, go, sum_one, one_s)
     total.begin(lambda rows: last_with_last(heads_out[rows], whole(1, 0)))
-    spill_copy.wait_recv()
-    for i in range(4):
-        span = pl.ds(i * STEP, STEP)
-        backs[me.y, column, :, span] = backs[me.y, column, :, span] + spill_in[:, span]
-    forward(4)
+    relay_y(4)
+    across.wait_recv()
+    columns = (column, (1 - me.high) * 2 + me.core)
+    back_copies, back_relays, fore_copies = {}, [], []
+    for j in (0, 1):
+        block = backs.at[me.y, columns[j]]
+        for d in (1, 3):
+            back_copies[j, d] = go(block, block, back_s, 1 + j * 2 + d // 2, y_at[d])
+        fore_copies.append(go(block, block, fore_s, j * 4, sibling))
+    distant(4)
     total.end()
-    block = backs.at[me.y, column]
-    back_copies = [go(block, block, back_s, j * 4 + k, peer(j, k)) for j, k in PAIRS]
-    fore_copies = [go(block, block, fore_s, 0, sibling)]
     middle[...] = wide(block_input[...]) + wide(sum_one[4][...])
     feed[...] = low(middle[...] * root_scale(middle[...]) * gains[1:2])
+    relay_z(3)
     complete(2)
     gate[...] = product(feed[...], whole(2, 0))
+    relay_z(4)
+    for (j, d), copy in back_copies.items():
+        copy.wait_recv()
+        source = me.along_y(4 - d)
+        block = backs.at[source, columns[j], pl.ds(16 * (d - 1), 32)]
+        back_relays.append(go(block, block, back_s, 5 + j * 2 + d // 2, y_at[d]))
+        block = backs.at[source, columns[j]]
+        fore_copies.append(go(block, block, fore_s, j * 4 + d, sibling))
     complete(3)
     upper[...] = product(feed[...], whole(2, 1))
     activated[...] = low(gate[...] * jax.nn.sigmoid(gate[...]) * upper[...])
     complete(4)
     total = SumOverMp(me, go, sum_two, two_s)
     total.begin(lambda rows: last_with_last(activated[rows], whole(3, 0)))
-    for (j, k), copy in zip(PAIRS, back_copies):
+    for copy in back_relays:
         copy.wait_recv()
-        region = backs.at[me.along_y((4 - k) % 4), ((me.high + j) % 2) * 2 + me.core]
-        fore_copies.append(go(region, region, fore_s, j * 4 + k, sibling))
+    for j in (0, 1):
+        block = backs.at[me.along_y(2), columns[j]]
+        fore_copies.append(go(block, block, fore_s, j * 4 + 2, sibling))
     total.end()
     block_out[...] = middle[...] + wide(sum_two[4][...])
     scale_three = root_scale(block_out[...])
     for i in range(10):
         span = slice(i * 128, (i + 1) * 128)
-        merged_wide[i] = block_out[:, span] * scale_three * merge_gain[:, span]
+        merged_wide[i] = block_out[:, span] * scale_three * merge_gain[span][None]
         for j in range(4):
             there = pl.ds(j * 1280 + i * 128, 128)
             merged[:, there] = low(merged_wide[i, pl.ds(j, 64, stride=4), :])
@@ -623,7 +674,7 @@
     scratch += [spill, spill, pltpu.VMEM((10, rows, 128), jnp.float32)]
     scratch += sum_buffers() + sum_buffers()
     scratch += [pltpu.SemaphoreType.DMA((4,)), pltpu.SemaphoreType.DMA((len(UNITS),))]
-    for size in (45, 45, 15, 3 * CHUNKS, 3 * CHUNKS, 1, 8, 8):
+    for size in (60, 60, 15, 3 * CHUNKS, 3 * CHUNKS, 1, 9, 8):
         scratch += sem_pair(size)
     results = pl.pallas_call(
         forward_kernel,
@@ -639,7 +690,7 @@
         block_input,
         windows,
         gains,
-        merge_gain[None],
+        merge_gain,
         cell_rows,
         cotangent,
         *shards,
@@ -846,8 +897,14 @@
         piece = self.piece(1, E_TOP, E_ROWS - E_TOP)
         self.fourth[4] = self.go(piece, piece, self.sems[5], at + 3, self.z_at[3])
 
+    def put(self, p, rows, value):
+        if self.index in (2, 3):
+            self.final[rows, self.index - 2] = value
+        else:
+            self.final[p, rows] = value
+
     def finish(self):
-        me, ya, final = self.me, self.ya, self.final
+        me, ya = self.me, self.ya
         for k in (0,) + ORDER:
             if k == 2 and self.relayed:
                 self.fourth[2].wait_recv()
@@ -860,12 +917,12 @@
             def put_a(p, r):
                 there = pl.ds(pl.multiple_of(source * A_PART + r, TILE), TILE)
                 here = pl.ds(pl.multiple_of(base + r, TILE), TILE)
-                final[p, there] = wide(ya[slot, p, here])
+                self.put(p, there, wide(ya[slot, p, here]))
 
             def put_b(p, r):
                 there = pl.ds(pl.multiple_of(A_ROWS + source * B_PART + r, TILE), TILE)
                 here = pl.ds(pl.multiple_of(base + A_PART + r, TILE), TILE)
-                final[p, there] = wide(ya[slot, p, here])
+                self.put(p, there, wide(ya[slot, p, here]))
 
             over_rows(self.planes, A_PART, put_a)
             over_rows(self.planes, B_PART, put_b)
@@ -899,9 +956,9 @@
         block_out,
     ) = refs[:18]
     input_gradient = refs[18]
-    outs = refs[19:24]
-    gain_out = refs[24]
-    refs = refs[25:]
+    outs = (refs[19], refs[20], refs[21], refs[21], refs[22])
+    gain_out = refs[23]
+    refs = refs[24:]
     triple, output, gate_up, down, load = refs[:5]
     refs = refs[5:]
     sum_one, sum_two = refs[:5], refs[5:10]
@@ -947,7 +1004,7 @@
         return weight[p].reshape(1280, -1)
 
     scale_three = root_scale(block_out[...])
-    out_back = norm_backward(cells_back[...], block_out[...], scale_three, merge_gain[...])
+    out_back = norm_backward(cells_back[...], block_out[...], scale_three, merge_gain[...][None])
     middle_back[...] = out_back
     out_low[...] = low(out_back)
     form(4, 0, out_low, activated[...])
@@ -1041,7 +1098,7 @@
     of_output.stage_three()
     for copy in gain_copies:
         copy.wait_recv()
-    gain_out[...] = gain_sum[1] + gain_in[6]
+    gain_out[...] = gain_sum[1, :2] + gain_in[6, :2]
     of_triple.stage_four()
     of_upper.relay()
     of_output.stage_four()
@@ -1095,7 +1152,7 @@
         block_input,
         windows,
         gains,
-        merge_gain[None],
+        merge_gain,
         cells_back,
         *wholes,
         *saved,
@@ -1103,9 +1160,10 @@
     outs = (
         [jax.ShapeDtypeStruct((rows, width), jnp.float32)]
         + [
-            jax.ShapeDtypeStruct((planes, 320, columns), jnp.float32) for planes, columns in sizes
+            jax.ShapeDtypeStruct(dims, jnp.float32)
+            for dims in ((3, 320, 320), (1, 320, 320), (320, 2, units), (1, 320, units))
         ]
-        + [jax.ShapeDtypeStruct((8, width), jnp.float32)]
+        + [jax.ShapeDtypeStruct((2, width), jnp.float32)]
     )
     results = pl.pallas_call(
         backward_kernel,
@@ -1119,8 +1177,7 @@
         name="block_backward",
     )(*operands)
 
-    gradients = results[1:6]
-    return results[0], gradients, results[6][:2]
+    return results[0], results[1:5], results[5]
 
 
 def planes_of(weight):
@@ -1180,8 +1237,8 @@
         input_gradient[None],
         planes_of(gradients[0]),
         gradients[1][0],
-        jnp.stack([gradients[2][0], gradients[3][0]], axis=1),
-        gradients[4][0],
+        gradients[2],
+        gradients[3][0],
         gain_gradient,
     )
 

time: 313 us -> 295 us (0.942)
  Pallas kernels: 295 us -> 282 us
    pallas_call x1, Pallas kernels: 104 us -> 89.2 us  [block_forward(): pl.pallas_call(forward_kernel, out_shape=outs, in_specs=[VMEM] * 10, out_...]
    unnamed x17 -> x22, local copies, waits for them, and re-layouts: 11.5 us -> 12 us
where the time goes in v5:
time: 295 us; the launch traced here: 294 us
  Pallas kernels  282 us (96%)
  local copies, waits for them, and re-layouts  12 us (4%)
    pallas_call x1, Pallas kernels, block_backward(): pl.pallas_call(backward_kernel, out_shape=outs, in_specs=[VMEM] * 5 + [AN...  108 us
    pallas_call x1, Pallas kernels, block_forward(): pl.pallas_call(forward_kernel, out_shape=outs, in_specs=[VMEM] * 10, out_...  89.2 us
    pallas_call x1, Pallas kernels, merger(): pl.pallas_call(merger_kernel, out_shape=[jax.ShapeDtypeStruct(text.shape,...  84.9 us
    unnamed x22, local copies, waits for them, and re-layouts  12 us

profile of v5, /device:TPU:0, one launch (start us, length us, event | category | flops | bytes accessed | tf_op | source)
XLA Modules:
  0.0 294.5 jit_solution(15092640777081356637)
XLA Ops:
  0.6 2.4 copy.22
  3.0 89.2 %block_forward.1 = (bf16[3,4,320,320]{3,2,1,0:T(8,128)(2,1)}, bf16[1,4,320,320]{3,2,1,0:T(8,128)(2,1)}, bf16[2,4,320,855]{3,2,1,0:T(8,128)(2,1)}, bf16[1,4,320,8...) custom-call(bf16[256,1280]{1,0:T(8,128)(2,1)} %bitcast.17, ...), custom_call_target="tpu_custom_call" | custom-call | tf_op jit(solution)/shard_map/block_forward/pallas_call | solution.py:679
  92.2 84.9 %merger.1 = (bf16[256,2048]{1,0:T(8,128)(2,1)}, f32[256,1280]{1,0:T(8,128)}) custom-call(s32[1,256]{1,0:T(1,128)} %rows_across.1, bf16[256,2048]{1,0:T(8,128)(2,1)} %bitcast.22, bf16[64,5120]{1,0:T(8,128)(2,1)} %get-tuple-element.30.merged, bf16[4,4,64,2048]{3,2,1,0:T(8,128)(2,1)} %get-tuple-element.31.backs_kept, bf16[320,5120]{1,0:T(8,128)(2,1)} %bitcast.16, ...), custom_call_target="tpu_custom_call" | custom-call | tf_op jit(solution)/shard_map/merger/pallas_call | solution.py:364
  177.1 0.0 copy-start.4
  177.2 107.7 %block_backward.1 = (f32[256,1280]{1,0:T(8,128)}, f32[3,320,320]{2,1,0:T(8,128)}, f32[1,320,320]{2,1,0:T(8,128)}, f32[320,2,855]{2,1,0:T(2,128)}, f32[1,320,855]{2,1,0:T(8,128)}, /*index=5*/f32[2,1280]{1,0:T(2,128)}) custom-call(bf16[256,1280]{1,0:T(8,128)(2,1)} %bitcast.18, s32[1,64]{1,0:T(1,128)} %refs_1_.3, f32[2,1280]{1,0:T(2,128)} %refs_2_.3, ...), custom_call_target="tpu_custom_call" | custom-call | tf_op jit(solution)/shard_map/block_backward/pallas_call | solution.py:1168
  284.9 0.0 copy-start.2
  284.9 0.0 copy-done.4
  284.9 1.0 copy.30
  285.9 0.7 copy-done.2
  286.6 0.0 copy-start.1
  286.6 1.1 copy.31
  287.6 0.8 copy-done.1
  288.4 0.0 copy-start.5
  288.4 0.0 copy-start
  288.4 1.1 copy.32
  289.5 0.2 copy-done.5
  289.7 0.8 copy.33
  290.5 0.3 copy-done
  290.8 0.0 copy-start.3
  290.8 1.4 copy.34
  292.2 0.7 copy-done.3
  292.9 0.0 copy-start.6
  292.9 1.0 copy.35
  293.9 0.0 copy-done.6
  293.9 0.6 copy.36
Async XLA Ops:
  177.1 107.7 %copy-start.4 = (bf16[256,2048]{1,0:T(8,128)(2,1)S(1)}, bf16[256,2048]{1,0:T(8,128)(2,1)}, u32[]{:S(2)}) copy-start(bf16[256,2048]{1,0:T(8,128)(2,1)} %get-tuple-element.32) | copy-start | bytes 3145732
  284.9 1.7 copy-start.2
  286.6 1.8 copy-start.1
  288.4 1.3 copy-start.5
  288.4 2.4 copy-start
  290.8 2.1 copy-start.3
  292.9 1.0 copy-start.6

commit v6 on v5

--- a/solution.py
+++ b/solution.py
@@ -139,13 +139,11 @@
 
 
 def merger_kernel(
-    rows_across,
-    text,
     merged,
     backs_kept,
     up_kept,
     down_kept,
-    sequence,
+    visual_terms,
     gradient,
     backs,
     up,
@@ -159,9 +157,6 @@
     hidden_back,
     terms,
     terms_in,
-    visual_in,
-    visual,
-    following,
     pieces,
     pieces_in,
     parts,
@@ -170,8 +165,8 @@
 ):
     me = Place()
     load, *sems = sems
-    merged_s, share_s, dp_s, terms_s, visual_s, pieces_s, parts_s, mp_s = [
-        (sems[2 * i], sems[2 * i + 1]) for i in range(8)
+    merged_s, share_s, terms_s, pieces_s, parts_s, mp_s = [
+        (sems[2 * i], sems[2 * i + 1]) for i in range(6)
     ]
     loads = [
         local_copy(source, target, load.at[i])
@@ -180,14 +175,11 @@
         )
     ]
     sibling, partner = me.at(core=1 - me.core), me.at(high=1 - me.high)
-    turn = 1 - me.low
-    after = me.at(z=(me.z + me.low) % 4, low=turn)
-    before = me.at(z=(me.z + 3 + me.low) % 4, low=turn)
 
     def peer(j, k):
         return me.at(y=me.along_y(k), high=(me.high + j) % 2)
 
-    greet([peer(j, k) for j, k in PAIRS] + [sibling, after, before])
+    greet([peer(j, k) for j, k in PAIRS] + [sibling])
     pending = []
 
     def go(*arguments):
@@ -272,16 +264,8 @@
         @pl.loop(0, 16)
         def _(i):
             here = pl.ds(pl.multiple_of(i * 16, 16), 16)
-            terms[column, here] = low(wide(terms[column, here]) + wide(terms_in[j, here]))
-
-    def visual_region(j, k):
-        rows = pl.ds(pl.multiple_of(me.along_y(k) * 64, 64), 64)
-        return terms.at[((me.high + j) % 2) * 2 + me.core, rows]
-
-    visual_copies = [
-        go(visual_region(j, k), visual_in.at[j * 4 + k], visual_s, j * 4 + k, peer(j, k))
-        for j, k in PAIRS
-    ]
+            visual_terms[j, here] = low(wide(terms[column, here]) + wide(terms_in[j, here]))
+
     for copy in part_copies:
         copy.wait_recv()
     mine = pl.ds(pl.multiple_of(own * 16, 16), 16)
@@ -299,19 +283,6 @@
     theirs = pl.ds(pl.multiple_of(((1 - me.high) * 2 + me.core) * 16, 16), 16)
     mp_copies.append(go(cells_back.at[theirs], cells_back.at[theirs], mp_s, 2, sibling))
 
-    for copy in visual_copies:
-        copy.wait_recv()
-    mine_rows = pl.multiple_of(me.y * 64, 64)
-
-    @pl.loop(0, 4)
-    def _(i):
-        here = pl.ds(pl.multiple_of(i * 16, 16), 16)
-        total = wide(terms[own, pl.ds(pl.multiple_of(mine_rows + i * 16, 16), 16)])
-        for j, k in PAIRS:
-            total = total + wide(visual_in[j * 4 + k, here])
-        visual[here] = low(total)
-
-    visual_copy = go(visual, following, dp_s, 0, before)
     mp_copies[1].wait_recv()
     mp_copies[2].wait_recv()
     for i in range(10):
@@ -319,21 +290,11 @@
             there = pl.ds(j * 1280 + i * 128, 128)
             apart[i, pl.ds(j, 64, stride=4), :] = wide(cells_back[:, there])
         gradient[:, i * 128 : (i + 1) * 128] = apart[i]
-    slot = lax.broadcasted_iota(jnp.int32, (256, 64), 1)
-    rows_down = upright(rows_across[...])
-    offset = (me.z * 2 + me.low) * 64
-    here_cells = jnp.where(rows_down - offset == slot, 1.0, 0.0).astype(jnp.bfloat16)
-    next_cells = jnp.where(rows_down - offset - 64 == slot, 1.0, 0.0).astype(jnp.bfloat16)
-    visual_copy.wait_recv()
-    for i in range(4):
-        span = pl.ds(i * STEP, STEP)
-        picked = product(here_cells, visual[:, span]) + product(next_cells, following[:, span])
-        sequence[:, span] = jnp.where(rows_down >= 0, low(picked), text[:, span])
     for copy in pending:
         copy.wait_send()
 
 
-def merger(cell_rows, text, merged, backs, up, down):
+def merger(merged, backs, up, down):
     def buffer(*shape):
         return pltpu.VMEM(shape, jnp.bfloat16)
 
@@ -350,31 +311,28 @@
         pltpu.VMEM((256, 320), jnp.float32),
         buffer(4, 256, 2048),
         buffer(2, 256, 2048),
-        buffer(8, 64, 2048),
-        buffer(64, 2048),
-        buffer(64, 2048),
         buffer(4, 2, 2, 16, 5120),
         buffer(4, 2, 16, 5120),
         buffer(4, 2, 16, 5120),
         buffer(8, 16, 5120),
     ]
     scratch += [pltpu.SemaphoreType.DMA((3,))]
-    for size in (4, 4, 1, 2, 8, 1, 8, 3):
+    for size in (4, 4, 2, 1, 8, 3):
         scratch += sem_pair(size)
     return pl.pallas_call(
         merger_kernel,
         out_shape=[
-            jax.ShapeDtypeStruct(text.shape, jnp.bfloat16),
+            jax.ShapeDtypeStruct((2, 256, 2048), jnp.bfloat16),
             jax.ShapeDtypeStruct((256, 1280), jnp.float32),
         ],
-        in_specs=[VMEM] * 3 + [ANY] * 3,
+        in_specs=[VMEM] + [ANY] * 3,
         out_specs=[VMEM] * 2,
         scratch_shapes=scratch,
         compiler_params=pltpu.CompilerParams(
             collective_id=4, has_side_effects=True, vmem_limit_bytes=VMEM_LIMIT
         ),
         name="merger",
-    )(cell_rows, text, merged, backs, up, down)
+    )(merged, backs, up, down)
 
 
 CHUNKS = 4
@@ -954,19 +912,28 @@
         upper,
         activated,
         block_out,
-    ) = refs[:18]
+        rows_across,
+        text,
+        visual_terms,
+    ) = refs[:21]
+    sequence = refs[21]
+    refs = refs[4:]
     input_gradient = refs[18]
     outs = (refs[19], refs[20], refs[21], refs[21], refs[22])
     gain_out = refs[23]
     refs = refs[24:]
     triple, output, gate_up, down, load = refs[:5]
-    refs = refs[5:]
+    visual_in, following, text_part, part_sems = refs[5:9]
+    visual = visual_in.at[0]
+    refs = refs[9:]
     sum_one, sum_two = refs[:5], refs[5:10]
     terms = refs[10:15]
     buffers = [refs[15 + 10 * t : 25 + 10 * t] for t in range(5)]
-    middle_back, middle_low, out_low, gate_up_back, triple_back, gain, gain_in, gain_sum = refs[65:73]
-    sems = refs[73:]
-    pair = [(sems[2 * i], sems[2 * i + 1]) for i in range(9)]
+    middle_back = input_gradient
+    out_low, gate_up_back, triple_back, gain, gain_in, gain_sum = refs[65:71]
+    middle_low = out_low
+    sems = refs[71:]
+    pair = [(sems[2 * i], sems[2 * i + 1]) for i in range(11)]
     loads = [
         local_copy(source, target, load.at[i])
         for i, (source, target) in enumerate(
@@ -977,10 +944,16 @@
     y_at = {k: me.at(y=me.along_y(k)) for k in ORDER}
     z_at = {k: me.at(z=me.along_z(k)) for k in ORDER}
     side = me.at(low=1 - me.low)
+    far = me.at(z=(me.z + 3 + 2 * me.low) % 4, low=1 - me.low)
+    before = me.at(z=(me.z + 3 + me.low) % 4, low=1 - me.low)
+
+    def peer(j, k):
+        return me.at(y=me.along_y(k), high=(me.high + j) % 2)
+
     greet(
-        [y_at[k] for k in ORDER]
+        [peer(j, k) for j, k in PAIRS]
         + [z_at[k] for k in ORDER]
-        + [side, me.at(core=1 - me.core), me.at(high=1 - me.high)]
+        + [side, far, me.at(core=1 - me.core)]
     )
     pending = []
 
@@ -1077,6 +1050,16 @@
     of_down.stage_three()
     of_output.stage_half()
     of_upper.stage_two()
+    own_visual = local_copy(
+        visual_terms.at[me.high, pl.ds(pl.multiple_of(me.y * 64, 64), 64)],
+        visual_in.at[0],
+        part_sems.at[0],
+    )
+    visual_copies = []
+    for j, k in PAIRS:
+        rows = pl.ds(pl.multiple_of(me.along_y(k) * 64, 64), 64)
+        region = visual_terms.at[(me.high + j) % 2, rows]
+        visual_copies.append(go(region, visual_in.at[j * 4 + k], pair[9], j * 4 + k, peer(j, k)))
     of_gate.stage_three()
     of_down.stage_four()
     for copy in gain_copies:
@@ -1096,19 +1079,46 @@
     of_upper.stage_four()
     of_gate.relay()
     of_output.stage_three()
+    own_visual.wait()
+    for copy in visual_copies:
+        copy.wait_recv()
+
+    @pl.loop(0, 4)
+    def _(i):
+        here = pl.ds(pl.multiple_of(i * 16, 16), 16)
+        total = wide(visual_in[0, here])
+        for j, k in PAIRS:
+            total = total + wide(visual_in[j * 4 + k, here])
+        visual[here] = low(total)
+
+    visual_copy = go(visual, following, pair[10], 0, before)
     for copy in gain_copies:
         copy.wait_recv()
     gain_out[...] = gain_sum[1, :2] + gain_in[6, :2]
     of_triple.stage_four()
     of_upper.relay()
     of_output.stage_four()
+    slot = lax.broadcasted_iota(jnp.int32, (256, 64), 1)
+    rows_down = upright(rows_across[...])
+    offset = (me.z * 2 + me.low) * 64
+    here_cells = jnp.where(rows_down - offset == slot, 1.0, 0.0).astype(jnp.bfloat16)
+    next_cells = jnp.where(rows_down - offset - 64 == slot, 1.0, 0.0).astype(jnp.bfloat16)
+    visual_copy.wait_recv()
+    for i in range(4):
+        span = pl.ds(i * STEP, STEP)
+        local_copy(text.at[:, span], text_part, part_sems.at[1]).wait()
+        picked = product(here_cells, visual[:, span]) + product(next_cells, following[:, span])
+        text_part[...] = jnp.where(rows_down >= 0, low(picked), text_part[...])
+        local_copy(text_part, sequence.at[:, span], part_sems.at[2]).wait()
     for reduction in (of_down, of_gate, of_upper, of_triple, of_output):
         reduction.finish()
     for copy in pending:
         copy.wait_send()
 
 
-def block_backward(block_input, windows, gains, merge_gain, cells_back, wholes, saved):
+def block_backward(
+    block_input, windows, gains, merge_gain, cells_back, wholes, saved, cell_rows, text, visual_terms
+):
     rows, width = block_input.shape
     units = saved[5].shape[1]
 
@@ -1120,7 +1130,8 @@
 
     sizes = ((3, 320), (1, 320), (1, units), (1, units), (1, units))
     scratch = [low_buffer(*whole.shape) for whole in wholes]
-    scratch += [pltpu.SemaphoreType.DMA((4,))]
+    scratch += [pltpu.SemaphoreType.DMA((4,)), low_buffer(8, 64, 2048)]
+    scratch += [low_buffer(64, 2048), low_buffer(rows, STEP), pltpu.SemaphoreType.DMA((3,))]
     scratch += sum_buffers() + sum_buffers()
     scratch += [low_buffer(planes, 4, 320, columns) for planes, columns in sizes]
     for planes, columns in sizes:
@@ -1137,8 +1148,6 @@
             low_buffer(planes, E_ROWS, columns),
         ]
     scratch += [
-        wide_buffer(rows, width),
-        low_buffer(rows, width),
         low_buffer(rows, width),
         low_buffer(2, rows, units),
         low_buffer(3, rows, 320),
@@ -1146,7 +1155,7 @@
         wide_buffer(7, 8, width),
         wide_buffer(2, 8, width),
     ]
-    for size in (30, 30, 15, 15, 5, 20, 3 * CHUNKS, 3 * CHUNKS, 7):
+    for size in (30, 30, 15, 15, 5, 20, 3 * CHUNKS, 3 * CHUNKS, 7, 8, 1):
         scratch += sem_pair(size)
     operands = [
         block_input,
@@ -1156,9 +1165,13 @@
         cells_back,
         *wholes,
         *saved,
+        cell_rows,
+        text,
+        visual_terms,
     ]
     outs = (
-        [jax.ShapeDtypeStruct((rows, width), jnp.float32)]
+        [jax.ShapeDtypeStruct(text.shape, jnp.bfloat16)]
+        + [jax.ShapeDtypeStruct((rows, width), jnp.float32)]
         + [
             jax.ShapeDtypeStruct(dims, jnp.float32)
             for dims in ((3, 320, 320), (1, 320, 320), (320, 2, units), (1, 320, units))
@@ -1168,8 +1181,8 @@
     results = pl.pallas_call(
         backward_kernel,
         out_shape=outs,
-        in_specs=[VMEM] * 5 + [ANY] * 4 + [VMEM] * (len(operands) - 9),
-        out_specs=[VMEM] * len(outs),
+        in_specs=[VMEM] * 5 + [ANY] * 4 + [VMEM] * (len(operands) - 11) + [ANY] * 2,
+        out_specs=[ANY] + [VMEM] * (len(outs) - 1),
         scratch_shapes=scratch,
         compiler_params=pltpu.CompilerParams(
             collective_id=3, has_side_effects=True, vmem_limit_bytes=VMEM_LIMIT
@@ -1177,7 +1190,7 @@
         name="block_backward",
     )(*operands)
 
-    return results[0], results[1:5], results[5]
+    return results[0], results[1], results[2:6], results[6]
 
 
 def planes_of(weight):
@@ -1215,15 +1228,13 @@
         sequence_cotangent[0],
         shards,
     )
-    sequence, cells_back = merger(
-        cell_rows,
-        text_vectors[0],
+    visual_terms, cells_back = merger(
         saved[-1],
         backs,
         merge_up.T,
         merge_down,
     )
-    input_gradient, gradients, gain_gradient = block_backward(
+    sequence, input_gradient, gradients, gain_gradient = block_backward(
         patches,
         windows,
         norm_gains,
@@ -1231,6 +1242,9 @@
         cells_back,
         wholes,
         saved[:-1],
+        cell_rows,
+        text_vectors[0],
+        visual_terms,
     )
     return (
         sequence[None],

time: 295 us -> 289 us (0.980)
  Pallas kernels: 282 us -> 274 us
    pallas_call x1, Pallas kernels: 84.9 us -> 58.5 us  [merger(): pl.pallas_call(merger_kernel, out_shape=[jax.ShapeDtypeStruct((2, 256, 20...]
    pallas_call x1, Pallas kernels: 108 us -> 127 us  [block_backward(): pl.pallas_call(backward_kernel, out_shape=outs, in_specs=[VMEM] * 5 + [AN...]
    unnamed x22 -> x20, local copies, waits for them, and re-layouts: 12 us -> 12.7 us
where the time goes in v6:
time: 289 us; the launch traced here: 288 us
  Pallas kernels  274 us (95%)
  local copies, waits for them, and re-layouts  12.7 us (4%)
    pallas_call x1, Pallas kernels, block_backward(): pl.pallas_call(backward_kernel, out_shape=outs, in_specs=[VMEM] * 5 + [AN...  127 us
    pallas_call x1, Pallas kernels, block_forward(): pl.pallas_call(forward_kernel, out_shape=outs, in_specs=[VMEM] * 10, out_...  89.2 us
    pallas_call x1, Pallas kernels, merger(): pl.pallas_call(merger_kernel, out_shape=[jax.ShapeDtypeStruct((2, 256, 20...  58.5 us
    unnamed x20, local copies, waits for them, and re-layouts  12.7 us

profile of v6, /device:TPU:0, one launch (start us, length us, event | category | flops | bytes accessed | tf_op | source)
XLA Modules:
  0.0 287.6 jit_solution(3441624943441183877)
XLA Ops:
  0.6 2.4 copy.22
  3.0 89.2 %block_forward.1 = (bf16[3,4,320,320]{3,2,1,0:T(8,128)(2,1)}, bf16[1,4,320,320]{3,2,1,0:T(8,128)(2,1)}, bf16[2,4,320,855]{3,2,1,0:T(8,128)(2,1)}, bf16[1,4,320,8...) custom-call(bf16[256,1280]{1,0:T(8,128)(2,1)} %bitcast.17, ...), custom_call_target="tpu_custom_call" | custom-call | tf_op jit(solution)/shard_map/block_forward/pallas_call | solution.py:637
  92.2 58.5 %merger.1 = (bf16[2,256,2048]{2,1,0:T(8,128)(2,1)}, f32[256,1280]{1,0:T(8,128)}) custom-call(bf16[64,5120]{1,0:T(8,128)(2,1)} %get-tuple-element.31.merged, bf16[4,4,64,2048]{3,2,1,0:T(8,128)(2,1)} %get-tuple-element.32.backs_kept, bf16[320,5120]{1,0:T(8,128)(2,1)} %bitcast.16, bf16[320,8192]{1,0:T(8,128)(2,1)} %down_kept.1), custom_call_target="tpu_custom_call" | custom-call | tf_op jit(solution)/shard_map/merger/pallas_call | solution.py:322
  150.7 126.6 %block_backward.1 = (bf16[256,2048]{1,0:T(8,128)(2,1)}, f32[256,1280]{1,0:T(8,128)}, f32[3,320,320]{2,1,0:T(8,128)}, f32[1,320,320]{2,1,0:T(8,128)}, f32[320,2,8...) custom-call(bf16[256,1280]{1,0:T(8,128)(2,1)} %bitcast.18, s32[1,64]{1,0:T(1,128)} %refs_1_.3, ...), custom_call_target="tpu_custom_call" | custom-call | tf_op jit(solution)/shard_map/block_backward/pallas_call | solution.py:1181
  277.3 0.0 copy-start.2
  277.3 2.4 copy.30
  279.7 0.0 copy-done.2
  279.7 0.0 copy-start.1
  279.7 1.1 copy.31
  280.8 0.8 copy-done.1
  281.6 0.0 copy-start.4
  281.6 0.0 copy-start
  281.6 1.1 copy.32
  282.7 0.2 copy-done.4
  282.9 0.8 copy.33
  283.7 0.3 copy-done
  284.0 0.0 copy-start.3
  284.0 1.4 copy.34
  285.4 0.7 copy-done.3
  286.0 0.0 copy-start.5
  286.0 1.0 copy.35
  287.0 0.0 copy-done.5
  287.0 0.6 copy.36
Async XLA Ops:
  277.3 2.4 copy-start.2
  279.7 1.8 copy-start.1
  281.6 1.3 copy-start.4
  281.6 2.4 copy-start
  284.0 2.1 copy-start.3
  286.0 1.0 copy-start.5

commit v7 on v6

--- a/solution.py
+++ b/solution.py
@@ -335,7 +335,7 @@
     )(merged, backs, up, down)
 
 
-CHUNKS = 4
+CHUNKS = 2
 
 
 class SumOverMp:
@@ -406,11 +406,11 @@
     shards = refs[6:10]
     kept = refs[10:14]
     attend, projected, heads_out, middle, feed, gate, upper, activated, block_out, merged = refs[14:24]
-    backs = refs[24]
-    wholes = refs[25:29]
-    spill, spill_in, merged_wide = refs[29:32]
-    sum_one, sum_two = refs[32:37], refs[37:42]
-    own, keep, *pairs = refs[42:]
+    backs_kept = refs[24]
+    wholes, backs = refs[25:29], refs[29]
+    spill, spill_in, merged_wide = refs[30:33]
+    sum_one, sum_two = refs[33:38], refs[38:43]
+    own, keep, *pairs = refs[43:]
     y_s, z_s, x_s, one_s, two_s, dp_s, back_s, fore_s = [
         (pairs[2 * i], pairs[2 * i + 1]) for i in range(8)
     ]
@@ -589,6 +589,9 @@
     for j in (0, 1):
         block = backs.at[me.along_y(2), columns[j]]
         fore_copies.append(go(block, block, fore_s, j * 4 + 2, sibling))
+    for copy in fore_copies:
+        copy.wait_recv()
+    keeps.append(local_copy(backs, backs_kept, keep.at[len(UNITS)]))
     total.end()
     block_out[...] = middle[...] + wide(sum_two[4][...])
     scale_three = root_scale(block_out[...])
@@ -598,8 +601,6 @@
         for j in range(4):
             there = pl.ds(j * 1280 + i * 128, 128)
             merged[:, there] = low(merged_wide[i, pl.ds(j, 64, stride=4), :])
-    for copy in fore_copies:
-        copy.wait_recv()
     for copy in keeps:
         copy.wait()
     for copy in pending:
@@ -628,17 +629,17 @@
         shape(low_, 4, 4, 64, cotangent.shape[1]),
     ]
     spill = pltpu.VMEM((64, cotangent.shape[1]), jnp.bfloat16)
-    scratch = [pltpu.VMEM(out.shape, jnp.bfloat16) for out in outs[:4]]
+    scratch = [pltpu.VMEM(out.shape, jnp.bfloat16) for out in outs[:4] + outs[-1:]]
     scratch += [spill, spill, pltpu.VMEM((10, rows, 128), jnp.float32)]
     scratch += sum_buffers() + sum_buffers()
-    scratch += [pltpu.SemaphoreType.DMA((4,)), pltpu.SemaphoreType.DMA((len(UNITS),))]
+    scratch += [pltpu.SemaphoreType.DMA((4,)), pltpu.SemaphoreType.DMA((len(UNITS) + 1,))]
     for size in (60, 60, 15, 3 * CHUNKS, 3 * CHUNKS, 1, 9, 8):
         scratch += sem_pair(size)
     results = pl.pallas_call(
         forward_kernel,
         out_shape=outs,
         in_specs=[VMEM] * 10,
-        out_specs=[ANY] * 4 + [VMEM] * (len(outs) - 4),
+        out_specs=[ANY] * 4 + [VMEM] * (len(outs) - 5) + [ANY],
         scratch_shapes=scratch,
         compiler_params=pltpu.CompilerParams(
             collective_id=1, has_side_effects=True, vmem_limit_bytes=VMEM_LIMIT
@@ -1008,6 +1009,7 @@
     form(3, 0, feed, gate_up_back[1])
     of_upper.stage_one()
     of_gate.stage_half()
+    of_down.stage_two()
     heads_back = low(product(middle_low[...], whole(output, 0)))
     allowed = same_image(windows[...])
     query_back = jnp.zeros((256, 320), jnp.float32)
@@ -1031,7 +1033,6 @@
     form(1, 0, middle_low, heads_out[...])
     of_output.stage_one()
     of_upper.stage_half()
-    of_down.stage_two()
     total = SumOverMp(me, go, sum_two, pair[7])
     total.begin(
         lambda rows: last_with_last(triple_back[0, rows], whole(triple, 0))
@@ -1050,16 +1051,6 @@
     of_down.stage_three()
     of_output.stage_half()
     of_upper.stage_two()
-    own_visual = local_copy(
-        visual_terms.at[me.high, pl.ds(pl.multiple_of(me.y * 64, 64), 64)],
-        visual_in.at[0],
-        part_sems.at[0],
-    )
-    visual_copies = []
-    for j, k in PAIRS:
-        rows = pl.ds(pl.multiple_of(me.along_y(k) * 64, 64), 64)
-        region = visual_terms.at[(me.high + j) % 2, rows]
-        visual_copies.append(go(region, visual_in.at[j * 4 + k], pair[9], j * 4 + k, peer(j, k)))
     of_gate.stage_three()
     of_down.stage_four()
     for copy in gain_copies:
@@ -1067,6 +1058,16 @@
     gain_sum[0] = gain[...] + gain_in[0] + gain_in[1] + gain_in[2]
     gain_copies = [go(gain_sum.at[0], gain_in.at[2 + k], pair[8], 2 + k, z_at[k]) for k in ORDER]
     of_triple.stage_two()
+    own_visual = local_copy(
+        visual_terms.at[me.high, pl.ds(pl.multiple_of(me.y * 64, 64), 64)],
+        visual_in.at[0],
+        part_sems.at[0],
+    )
+    visual_copies = []
+    for j, k in PAIRS:
+        rows = pl.ds(pl.multiple_of(me.along_y(k) * 64, 64), 64)
+        region = visual_terms.at[(me.high + j) % 2, rows]
+        visual_copies.append(go(region, visual_in.at[j * 4 + k], pair[9], j * 4 + k, peer(j, k)))
     of_upper.stage_three()
     of_gate.stage_four()
     of_down.relay()
@@ -1079,6 +1080,10 @@
     of_upper.stage_four()
     of_gate.relay()
     of_output.stage_three()
+    for copy in gain_copies:
+        copy.wait_recv()
+    gain_out[...] = gain_sum[1, :2] + gain_in[6, :2]
+    of_triple.stage_four()
     own_visual.wait()
     for copy in visual_copies:
         copy.wait_recv()
@@ -1092,10 +1097,6 @@
         visual[here] = low(total)
 
     visual_copy = go(visual, following, pair[10], 0, before)
-    for copy in gain_copies:
-        copy.wait_recv()
-    gain_out[...] = gain_sum[1, :2] + gain_in[6, :2]
-    of_triple.stage_four()
     of_upper.relay()
     of_output.stage_four()
     slot = lax.broadcasted_iota(jnp.int32, (256, 64), 1)

time: 289 us -> 286 us (0.990)
  no operation moved by 1% of the time
where the time goes in v7:
time: 286 us
  Pallas kernels  273 us (95%)
  local copies, waits for them, and re-layouts  12.7 us (4%)
    pallas_call x1, Pallas kernels, block_backward(): pl.pallas_call(backward_kernel, out_shape=outs, in_specs=[VMEM] * 5 + [AN...  126 us
    pallas_call x1, Pallas kernels, block_forward(): pl.pallas_call(forward_kernel, out_shape=outs, in_specs=[VMEM] * 10, out_...  88.1 us
    pallas_call x1, Pallas kernels, merger(): pl.pallas_call(merger_kernel, out_shape=[jax.ShapeDtypeStruct((2, 256, 20...  58.5 us
    unnamed x20, local copies, waits for them, and re-layouts  12.7 us

profile of v7, /device:TPU:0, one launch (start us, length us, event | category | flops | bytes accessed | tf_op | source)
XLA Modules:
  0.0 285.9 jit_solution(4275802904194706092)
XLA Ops:
  0.6 2.4 copy.22
  3.0 88.1 %block_forward.1 = (bf16[3,4,320,320]{3,2,1,0:T(8,128)(2,1)}, bf16[1,4,320,320]{3,2,1,0:T(8,128)(2,1)}, bf16[2,4,320,855]{3,2,1,0:T(8,128)(2,1)}, bf16[1,4,320,8...) custom-call(bf16[256,1280]{1,0:T(8,128)(2,1)} %bitcast.17, ...), custom_call_target="tpu_custom_call" | custom-call | tf_op jit(solution)/shard_map/block_forward/pallas_call | solution.py:638
  91.1 58.5 %merger.1 = (bf16[2,256,2048]{2,1,0:T(8,128)(2,1)}, f32[256,1280]{1,0:T(8,128)}) custom-call(bf16[64,5120]{1,0:T(8,128)(2,1)} %get-tuple-element.31.merged, bf16[4,4,64,2048]{3,2,1,0:T(8,128)(2,1)} %get-tuple-element.32.backs_kept, bf16[320,5120]{1,0:T(8,128)(2,1)} %bitcast.16, bf16[320,8192]{1,0:T(8,128)(2,1)} %down_kept.1), custom_call_target="tpu_custom_call" | custom-call | tf_op jit(solution)/shard_map/merger/pallas_call | solution.py:322
  149.5 126.0 %block_backward.1 = (bf16[256,2048]{1,0:T(8,128)(2,1)}, f32[256,1280]{1,0:T(8,128)}, f32[3,320,320]{2,1,0:T(8,128)}, f32[1,320,320]{2,1,0:T(8,128)}, f32[320,2,8...) custom-call(bf16[256,1280]{1,0:T(8,128)(2,1)} %bitcast.18, s32[1,64]{1,0:T(1,128)} %refs_1_.3, ...), custom_call_target="tpu_custom_call" | custom-call | tf_op jit(solution)/shard_map/block_backward/pallas_call | solution.py:1182
  275.6 0.0 copy-start.2
  275.6 2.4 copy.30
  278.0 0.0 copy-done.2
  278.0 0.0 copy-start.1
  278.0 1.1 copy.31
  279.0 0.8 copy-done.1
  279.8 0.0 copy-start.4
  279.8 0.0 copy-start
  279.8 1.1 copy.32
  280.9 0.2 copy-done.4
  281.2 0.8 copy.33
  281.9 0.3 copy-done
  282.2 0.0 copy-start.3
  282.2 1.4 copy.34
  283.6 0.7 copy-done.3
  284.3 0.0 copy-start.5
  284.3 1.0 copy.35
  285.3 0.0 copy-done.5
  285.3 0.6 copy.36
Async XLA Ops:
  275.6 2.4 copy-start.2
  278.0 1.8 copy-start.1
  279.8 1.3 copy-start.4
  279.8 2.4 copy-start
  282.2 2.1 copy-start.3
  284.3 1.0 copy-start.5
